TPU v7x, 32 devices: a whole 2x2x4 slice. The times are simulated.
32 devices in a mesh: dp: 8 (over z, y), mp: 4 (over x, core).
Axes of the slice: x: 2, y: 2, z: 4, core: 2. Of those that a mesh axis runs over, the one named last changes fastest.
Arguments:
- inputs: bfloat16 [4096, 1024], P('dp'), may hold values from -6 to 6
- lengths: int32 [8, 4], P('dp'), may hold values from 0 to 512, as said below
- out_grad: bfloat16 [4096, 1024], P('dp'), may hold values from -6 to 6
- first_norm: float32 [1024], P('dp'), may hold values from 0.5 to 1.5
- first_up: float32 [1024, 4096], P('dp', 'mp'), may hold values from -0.1875 to 0.1875
- first_down: float32 [1024, 4096], P('dp', 'mp'), may hold values from -0.1875 to 0.1875
- attention_norm: float32 [1024], P('dp'), may hold values from 0.5 to 1.5
- query_weight: float32 [1024, 1024], P('dp', 'mp'), may hold values from -0.1875 to 0.1875
- key_weight: float32 [1024, 1024], P('dp', 'mp'), may hold values from -0.1875 to 0.1875
- value_weight: float32 [1024, 1024], P('dp', 'mp'), may hold values from -0.1875 to 0.1875
- position_weight: float32 [1024, 1024], P('dp', 'mp'), may hold values from -0.1875 to 0.1875
- output_weight: float32 [1024, 1024], P('dp', 'mp'), may hold values from -0.75 to 0.75
- content_bias: float32 [128, 8], P('dp', 'mp'), may hold values from -3 to 3
- position_bias: float32 [128, 8], P('dp', 'mp'), may hold values from -3 to 3
- convolution_norm: float32 [1024], P('dp'), may hold values from 0.5 to 1.5
- pointwise_in: float32 [1024, 2, 1024], P('dp', None, 'mp'), may hold values from -0.1875 to 0.1875
- depthwise_kernel: float32 [1024, 5], P(('mp', 'dp')), may hold values from -2.5 to 2.5
- batch_gain: float32 [1024], P(('mp', 'dp')), may hold values from 0.5 to 1.5
- batch_shift: float32 [1024], P(('mp', 'dp')), may hold values from -3 to 3
- pointwise_out: float32 [1024, 1024], P('dp', 'mp'), may hold values from -0.375 to 0.375
- second_norm: float32 [1024], P('dp'), may hold values from 0.5 to 1.5
- second_up: float32 [1024, 4096], P('dp', 'mp'), may hold values from -0.1875 to 0.1875
- second_down: float32 [1024, 4096], P('dp', 'mp'), may hold values from -0.1875 to 0.1875
- final_norm: float32 [1024], P('dp'), may hold values from 0.5 to 1.5
Outputs:
- result: bfloat16 [4096, 1024], P('dp')
- inputs_grad: float32 [4096, 1024], P('dp')
- first_norm_grad: float32 [1024], P('dp')
- first_up_grad: float32 [1024, 4096], P('dp', 'mp')
- first_down_grad: float32 [1024, 4096], P('dp', 'mp')
- attention_norm_grad: float32 [1024], P('dp')
- query_weight_grad: float32 [1024, 1024], P('dp', 'mp')
- key_weight_grad: float32 [1024, 1024], P('dp', 'mp')
- value_weight_grad: float32 [1024, 1024], P('dp', 'mp')
- position_weight_grad: float32 [1024, 1024], P('dp', 'mp')
- output_weight_grad: float32 [1024, 1024], P('dp', 'mp')
- content_bias_grad: float32 [128, 8], P('dp', 'mp')
- position_bias_grad: float32 [128, 8], P('dp', 'mp')
- convolution_norm_grad: float32 [1024], P('dp')
- pointwise_in_grad: float32 [1024, 2, 1024], P('dp', None, 'mp')
- depthwise_kernel_grad: float32 [1024, 5], P(('mp', 'dp'))
- batch_gain_gradient: float32 [1024], P(('mp', 'dp'))
- batch_shift_grad: float32 [1024], P(('mp', 'dp'))
- pointwise_out_grad: float32 [1024, 1024], P('dp', 'mp')
- second_norm_grad: float32 [1024], P('dp')
- second_up_grad: float32 [1024, 4096], P('dp', 'mp')
- second_down_grad: float32 [1024, 4096], P('dp', 'mp')
- final_norm_grad: float32 [1024], P('dp')
Inputs may be any that keep to these rules, and one draw needn't show every extreme that they name: Lengths are whole numbers; the lengths of one group add up to at most 512; one group holds a single utterance of 512 frames and zero lengths in its other slots; a group's rows past its total are padding.
All inputs are finite; a program needn't handle non-finite values.
Results may differ from a plain program's by a relative error of at most 0.04.
Values may be sent and summed in bfloat16 or wider, within the bound.
No kernel may reach another device: no remote copies, remote signals or barrier semaphores. Data moves between devices by JAX's collectives and lax.ppermute only.
A program may use at most 128 MiB of HBM per device.

v0:
```python
import math

import jax
import jax.numpy as jnp
from jax import lax
from jax.sharding import PartitionSpec as P

EPSILON = 1e-05


def matmul(left_side, right_side):
    return jnp.dot(left_side, right_side, preferred_element_type=jnp.float32)


def times_transposed(left_side, right_side):
    return lax.dot_general(
        left_side, right_side, (((1,), (1,)), ((), ())), preferred_element_type=jnp.float32
    )


def outer_sum(left_side, right_side):
    return lax.dot_general(
        left_side, right_side, (((0,), (0,)), ((), ())), preferred_element_type=jnp.float32
    )


def layer_norm(values, norm_gain):
    average = jnp.mean(values, axis=-1, keepdims=True)
    centred = values - average
    spread = jnp.mean(centred * centred, axis=-1, keepdims=True)
    return centred * lax.rsqrt(spread + EPSILON) * norm_gain


def norm_back(residual, norm_gain, normed_grad):
    outcome, pullback = jax.vjp(layer_norm, residual, norm_gain)
    return pullback(normed_grad)


def segment_ids(utterances, row_count):
    bounds = jnp.cumsum(utterances)
    places = jnp.arange(row_count, dtype=jnp.int32)
    return jnp.sum((places[:, None] >= bounds[None, :]).astype(jnp.int32), axis=1)


def position_table(row_count, feature_count):
    offsets = (row_count - 1 - jnp.arange(2 * row_count - 1)).astype(jnp.float32)
    rates = jnp.exp(
        jnp.arange(0, feature_count, 2).astype(jnp.float32) * (-math.log(10000.0) / feature_count)
    )
    angles = offsets[:, None] * rates[None, :]
    return jnp.concatenate([jnp.sin(angles), jnp.cos(angles)], axis=1)


def shear_rows(broad_score_rows):
    head_count, row_count, span_count = broad_score_rows.shape
    flattened = broad_score_rows.reshape(head_count, row_count * span_count)
    flattened = flattened[:, row_count - 1 : row_count - 1 + row_count * (span_count - 1)]
    return flattened.reshape(head_count, row_count, span_count - 1)[:, :, :row_count]


def unshear_rows(narrow):
    head_count, row_count = (narrow.shape[0], narrow.shape[1])
    padded = jnp.pad(narrow, ((0, 0), (0, 0), (0, row_count - 2)))
    flattened = jnp.pad(
        padded.reshape(head_count, row_count * (2 * row_count - 2)), ((0, 0), (row_count - 1, 1))
    )
    return flattened.reshape(head_count, row_count, 2 * row_count - 1)


def shift_rows(values, offset):
    row_count = values.shape[0]
    if offset > 0:
        return jnp.concatenate(
            [values[offset:], jnp.zeros((offset,) + values.shape[1:], values.dtype)], axis=0
        )
    if offset < 0:
        return jnp.concatenate(
            [jnp.zeros((-offset,) + values.shape[1:], values.dtype), values[: row_count + offset]],
            axis=0,
        )
    return values


def depthwise(gated_rows, kernel, segment):
    tap_count = kernel.shape[1]
    marker = segment + 1
    output = jnp.zeros_like(gated_rows)
    for tap_index in range(tap_count):
        offset = tap_index - tap_count // 2
        matching = (shift_rows(marker, offset) == marker).astype(gated_rows.dtype)
        output = output + kernel[:, tap_index][None, :] * matching[:, None] * shift_rows(
            gated_rows, offset
        )
    return output


def gated_conv(lifted, kernel, segment, valid_rows):
    gated_rows = lifted[:, 0] * jax.nn.sigmoid(lifted[:, 1]) * valid_rows[:, None]
    return depthwise(gated_rows, kernel, segment)


def branch_total(piece_terms):
    return lax.psum(piece_terms.astype(jnp.bfloat16), "mp").astype(jnp.float32)


def fetch_first(norm_gain, up_weight, down_weight):
    return (
        lax.all_gather(norm_gain.astype(jnp.bfloat16), "dp", axis=0, tiled=True),
        lax.all_gather(up_weight.astype(jnp.bfloat16), "dp", axis=0, tiled=True),
        lax.all_gather(down_weight.astype(jnp.bfloat16), "dp", axis=0, tiled=True),
    )


def fetch_second(norm_gain, up_weight, down_weight, final_gain):
    return (
        lax.all_gather(norm_gain.astype(jnp.bfloat16), "dp", axis=0, tiled=True),
        lax.all_gather(up_weight.astype(jnp.bfloat16), "dp", axis=0, tiled=True),
        lax.all_gather(down_weight.astype(jnp.bfloat16), "dp", axis=0, tiled=True),
        lax.all_gather(final_gain.astype(jnp.bfloat16), "dp", axis=0, tiled=True),
    )


def fetch_attention(
    norm_gain,
    query_weight,
    key_weight,
    value_weight,
    position_weight,
    output_weight,
    content_bias,
    position_bias,
):
    return (
        lax.all_gather(norm_gain.astype(jnp.bfloat16), "dp", axis=0, tiled=True),
        lax.all_gather(query_weight.astype(jnp.bfloat16), "dp", axis=0, tiled=True),
        lax.all_gather(key_weight.astype(jnp.bfloat16), "dp", axis=0, tiled=True),
        lax.all_gather(value_weight.astype(jnp.bfloat16), "dp", axis=0, tiled=True),
        lax.all_gather(position_weight.astype(jnp.bfloat16), "dp", axis=0, tiled=True),
        lax.all_gather(output_weight.astype(jnp.bfloat16), "dp", axis=0, tiled=True),
        lax.all_gather(content_bias.astype(jnp.bfloat16), "dp", axis=0, tiled=True),
        lax.all_gather(position_bias.astype(jnp.bfloat16), "dp", axis=0, tiled=True),
    )


def fetch_convolution(
    norm_gain, pointwise_in, depthwise_kernel, batch_gain, batch_shift, pointwise_out
):
    return (
        lax.all_gather(norm_gain.astype(jnp.bfloat16), "dp", axis=0, tiled=True),
        lax.all_gather(pointwise_in.astype(jnp.bfloat16), "dp", axis=0, tiled=True),
        lax.all_gather(depthwise_kernel.astype(jnp.bfloat16), "dp", axis=0, tiled=True),
        lax.all_gather(batch_gain.astype(jnp.bfloat16), "dp", axis=0, tiled=True),
        lax.all_gather(batch_shift.astype(jnp.bfloat16), "dp", axis=0, tiled=True),
        lax.all_gather(pointwise_out.astype(jnp.bfloat16), "dp", axis=0, tiled=True),
    )


def ffn_forward(residual, weights):
    norm_gain, up_weight, down_weight = (weights[0], weights[1], weights[2])
    normed = layer_norm(residual, norm_gain.astype(jnp.float32)).astype(jnp.bfloat16)
    before = matmul(normed, up_weight)
    active = (before * jax.nn.sigmoid(before)).astype(jnp.bfloat16)
    residual_next = residual + 0.5 * branch_total(times_transposed(active, down_weight))
    return (residual_next, (normed, before, active))


def ffn_backward(residual_grad, residual, weights, stored):
    norm_gain, up_weight, down_weight = (weights[0], weights[1], weights[2])
    normed, before, active = stored
    branch_grad = (0.5 * residual_grad).astype(jnp.bfloat16)
    down_grad = outer_sum(branch_grad, active)
    squashed = jax.nn.sigmoid(before)
    before_grad = (
        matmul(branch_grad, down_weight) * squashed * (1.0 + before * (1.0 - squashed))
    ).astype(jnp.bfloat16)
    up_grad = outer_sum(normed, before_grad)
    normed_grad = branch_total(times_transposed(before_grad, up_weight))
    input_grad, gain_grad = norm_back(residual, norm_gain.astype(jnp.float32), normed_grad)
    return (residual_grad + input_grad, (gain_grad, up_grad, down_grad))


def attention_scores(with_content, plus_position_term, key_rows, relative_offset, segment):
    head_size = key_rows.shape[2]
    direct = jnp.einsum("ihd,jhd->hij", with_content, key_rows, preferred_element_type=jnp.float32)
    broad_score_rows = jnp.einsum(
        "tkn,ukn->ktu", plus_position_term, relative_offset, preferred_element_type=jnp.float32
    )
    scores = (direct + shear_rows(broad_score_rows)) * head_size ** (-0.5)
    matching = segment[:, None] == segment[None, :]
    return jnp.where(matching[None], scores, -1e30)


def attention_forward(residual, weights, segment):
    (
        norm_gain,
        query_weight,
        key_weight,
        value_weight,
        position_weight,
        output_weight,
        content_bias,
        position_bias,
    ) = weights
    head_size, head_count = content_bias.shape
    normed = layer_norm(residual, norm_gain.astype(jnp.float32)).astype(jnp.bfloat16)
    row_count, feature_count = normed.shape
    query_rows = matmul(normed, query_weight).reshape(row_count, head_count, head_size)
    with_content = (query_rows + content_bias.astype(jnp.float32).T[None]).astype(jnp.bfloat16)
    plus_position_term = (query_rows + position_bias.astype(jnp.float32).T[None]).astype(
        jnp.bfloat16
    )
    key_rows = (
        matmul(normed, key_weight).astype(jnp.bfloat16).reshape(row_count, head_count, head_size)
    )
    value_rows = (
        matmul(normed, value_weight).astype(jnp.bfloat16).reshape(row_count, head_count, head_size)
    )
    sin_table = position_table(row_count, feature_count).astype(jnp.bfloat16)
    relative_offset = (
        matmul(sin_table, position_weight)
        .astype(jnp.bfloat16)
        .reshape(2 * row_count - 1, head_count, head_size)
    )
    masked = attention_scores(with_content, plus_position_term, key_rows, relative_offset, segment)
    row_peak = jnp.max(masked, axis=-1, keepdims=True)
    exponent = jnp.exp(masked - row_peak)
    totals = jnp.sum(exponent, axis=-1, keepdims=True)
    prob_low = (exponent / totals).astype(jnp.bfloat16)
    log_total = row_peak + jnp.log(totals)
    mixed_rows = jnp.einsum(
        "hij,jhd->ihd", prob_low, value_rows, preferred_element_type=jnp.float32
    )
    mixed_rows = mixed_rows.astype(jnp.bfloat16).reshape(row_count, head_count * head_size)
    residual_next = residual + branch_total(times_transposed(mixed_rows, output_weight))
    return (
        residual_next,
        (
            normed,
            with_content,
            plus_position_term,
            key_rows,
            value_rows,
            sin_table,
            relative_offset,
            log_total,
            mixed_rows,
        ),
    )


def attention_backward(residual_grad, residual, weights, stored, segment):
    (
        norm_gain,
        query_weight,
        key_weight,
        value_weight,
        position_weight,
        output_weight,
        content_bias,
        position_bias,
    ) = weights
    (
        normed,
        with_content,
        plus_position_term,
        key_rows,
        value_rows,
        sin_table,
        relative_offset,
        log_total,
        mixed_rows,
    ) = stored
    row_count, head_count, head_size = with_content.shape
    score_scale = head_size ** (-0.5)
    branch_grad = residual_grad.astype(jnp.bfloat16)
    output_grad = outer_sum(branch_grad, mixed_rows)
    mixed_grad = (
        matmul(branch_grad, output_weight)
        .astype(jnp.bfloat16)
        .reshape(row_count, head_count, head_size)
    )
    masked = attention_scores(with_content, plus_position_term, key_rows, relative_offset, segment)
    prob_rows = jnp.exp(masked - log_total)
    prob_low = prob_rows.astype(jnp.bfloat16)
    value_grad = jnp.einsum(
        "hij,ihd->jhd", prob_low, mixed_grad, preferred_element_type=jnp.float32
    )
    value_grad = value_grad.astype(jnp.bfloat16).reshape(row_count, head_count * head_size)
    prob_grad = jnp.einsum(
        "ihd,jhd->hij", mixed_grad, value_rows, preferred_element_type=jnp.float32
    )
    inner_term = jnp.sum(prob_grad * prob_rows, axis=-1, keepdims=True)
    score_grad = (prob_rows * (prob_grad - inner_term)).astype(jnp.bfloat16)
    content_part = (
        jnp.einsum("hij,jhd->ihd", score_grad, key_rows, preferred_element_type=jnp.float32)
        * score_scale
    )
    key_grad = (
        jnp.einsum("hij,ihd->jhd", score_grad, with_content, preferred_element_type=jnp.float32)
        * score_scale
    )
    key_grad = key_grad.astype(jnp.bfloat16).reshape(row_count, head_count * head_size)
    broad_score_gradient = unshear_rows(score_grad)
    position_part = (
        jnp.einsum(
            "yfa,ayt->fyt",
            broad_score_gradient,
            relative_offset,
            preferred_element_type=jnp.float32,
        )
        * score_scale
    )
    position_grad = (
        jnp.einsum(
            "nsq,snr->qnr",
            broad_score_gradient,
            plus_position_term,
            preferred_element_type=jnp.float32,
        )
        * score_scale
    )
    position_grad = position_grad.astype(jnp.bfloat16).reshape(
        2 * row_count - 1, head_count * head_size
    )
    query_grad = (
        (content_part + position_part)
        .astype(jnp.bfloat16)
        .reshape(row_count, head_count * head_size)
    )
    content_grad = jnp.sum(content_part, axis=0).T
    bias_grad = jnp.sum(position_part, axis=0).T
    query_weight_grad = outer_sum(normed, query_grad)
    key_weight_grad = outer_sum(normed, key_grad)
    value_weight_grad = outer_sum(normed, value_grad)
    position_weight_grad = outer_sum(sin_table, position_grad)
    normed_grad = branch_total(
        times_transposed(query_grad, query_weight)
        + times_transposed(key_grad, key_weight)
        + times_transposed(value_grad, value_weight)
    )
    input_grad, gain_grad = norm_back(residual, norm_gain.astype(jnp.float32), normed_grad)
    return (
        residual_grad + input_grad,
        (
            gain_grad,
            query_weight_grad,
            key_weight_grad,
            value_weight_grad,
            position_weight_grad,
            output_grad,
            content_grad,
            bias_grad,
        ),
    )


def convolution_forward(residual, weights, segment, valid_rows):
    norm_gain, pointwise_in, depthwise_kernel, batch_gain, batch_shift, pointwise_out = weights
    normed = layer_norm(residual, norm_gain.astype(jnp.float32)).astype(jnp.bfloat16)
    lifted = jnp.einsum("rd,dgc->rgc", normed, pointwise_in, preferred_element_type=jnp.float32)
    convolved = gated_conv(lifted, depthwise_kernel.astype(jnp.float32), segment, valid_rows)
    masked_conv = convolved * valid_rows[:, None]
    first_sum, second_sum, frame_count = lax.psum(
        (
            jnp.sum(masked_conv, axis=0),
            jnp.sum(masked_conv * convolved, axis=0),
            jnp.sum(valid_rows),
        ),
        "dp",
    )
    average = first_sum / frame_count
    inverse = lax.rsqrt(second_sum / frame_count - average * average + EPSILON)
    hatted = (convolved - average) * inverse
    normalized = hatted * batch_gain.astype(jnp.float32) + batch_shift.astype(jnp.float32)
    swished = (normalized * jax.nn.sigmoid(normalized) * valid_rows[:, None]).astype(jnp.bfloat16)
    residual_next = residual + branch_total(times_transposed(swished, pointwise_out))
    return (residual_next, (normed, lifted, hatted, normalized, swished, inverse, frame_count))


def convolution_backward(residual_grad, residual, weights, stored, segment, valid_rows):
    norm_gain, pointwise_in, depthwise_kernel, batch_gain, batch_shift, pointwise_out = weights
    normed, lifted, hatted, normalized, swished, inverse, frame_count = stored
    branch_grad = residual_grad.astype(jnp.bfloat16)
    pointwise_out_grad = outer_sum(branch_grad, swished)
    squashed = jax.nn.sigmoid(normalized)
    normal_grad = (
        matmul(branch_grad, pointwise_out)
        * valid_rows[:, None]
        * squashed
        * (1.0 + normalized * (1.0 - squashed))
    )
    shift_total, gain_total = lax.psum(
        (jnp.sum(normal_grad, axis=0), jnp.sum(normal_grad * hatted, axis=0)), "dp"
    )
    gain_float = batch_gain.astype(jnp.float32)
    conv_grad = inverse * (
        normal_grad * gain_float
        - valid_rows[:, None] * gain_float * (shift_total + hatted * gain_total) / frame_count
    )
    outcome, pullback = jax.vjp(
        lambda lifted_in, kernel_in: gated_conv(lifted_in, kernel_in, segment, valid_rows),
        lifted,
        depthwise_kernel.astype(jnp.float32),
    )
    lifted_grad, kernel_grad = pullback(conv_grad)
    lifted_low = lifted_grad.astype(jnp.bfloat16)
    pointwise_in_grad = jnp.einsum(
        "rd,rgc->dgc", normed, lifted_low, preferred_element_type=jnp.float32
    )
    normed_grad = branch_total(
        jnp.einsum("rgc,dgc->rd", lifted_low, pointwise_in, preferred_element_type=jnp.float32)
    )
    input_grad, gain_grad = norm_back(residual, norm_gain.astype(jnp.float32), normed_grad)
    piece_size = gain_total.shape[0] // lax.axis_size("dp")
    first_row = lax.axis_index("dp") * piece_size
    gain_piece = lax.dynamic_slice_in_dim(gain_total, first_row, piece_size)
    shift_piece = lax.dynamic_slice_in_dim(shift_total, first_row, piece_size)
    return (
        residual_grad + input_grad,
        (gain_grad, pointwise_in_grad, kernel_grad, pointwise_out_grad),
        gain_piece,
        shift_piece,
    )


def per_device(
    inputs,
    lengths,
    out_grad,
    first_norm,
    first_up,
    first_down,
    attention_norm,
    query_weight,
    key_weight,
    value_weight,
    position_weight,
    output_weight,
    content_bias,
    position_bias,
    convolution_norm,
    pointwise_in,
    depthwise_kernel,
    batch_gain,
    batch_shift,
    pointwise_out,
    second_norm,
    second_up,
    second_down,
    final_norm,
):
    row_count = inputs.shape[0]
    segment = segment_ids(lengths[0], row_count)
    valid_rows = (segment < lengths.shape[1]).astype(jnp.float32)
    first_set = fetch_first(first_norm, first_up, first_down)
    residual_zero = inputs.astype(jnp.float32)
    residual_one, first_stored = ffn_forward(residual_zero, first_set)
    attention_set = fetch_attention(
        attention_norm,
        query_weight,
        key_weight,
        value_weight,
        position_weight,
        output_weight,
        content_bias,
        position_bias,
    )
    residual_two, attention_stored = attention_forward(residual_one, attention_set, segment)
    convolution_set = fetch_convolution(
        convolution_norm, pointwise_in, depthwise_kernel, batch_gain, batch_shift, pointwise_out
    )
    residual_three, convolution_saved_state = convolution_forward(
        residual_two, convolution_set, segment, valid_rows
    )
    second_set = fetch_second(second_norm, second_up, second_down, final_norm)
    residual_four, second_stored = ffn_forward(residual_three, second_set)
    final_gain = second_set[3].astype(jnp.float32)
    result = layer_norm(residual_four, final_gain).astype(jnp.bfloat16)
    residual_grad, final_grad = norm_back(residual_four, final_gain, out_grad.astype(jnp.float32))
    second_set = fetch_second(second_norm, second_up, second_down, final_norm)
    residual_grad, second_feed_gradients = ffn_backward(
        residual_grad, residual_three, second_set, second_stored
    )
    convolution_set = fetch_convolution(
        convolution_norm, pointwise_in, depthwise_kernel, batch_gain, batch_shift, pointwise_out
    )
    residual_grad, convolution_grads, gain_piece, shift_piece = convolution_backward(
        residual_grad, residual_two, convolution_set, convolution_saved_state, segment, valid_rows
    )
    attention_set = fetch_attention(
        attention_norm,
        query_weight,
        key_weight,
        value_weight,
        position_weight,
        output_weight,
        content_bias,
        position_bias,
    )
    residual_grad, attention_grads = attention_backward(
        residual_grad, residual_one, attention_set, attention_stored, segment
    )
    first_set = fetch_first(first_norm, first_up, first_down)
    residual_grad, first_grads = ffn_backward(residual_grad, residual_zero, first_set, first_stored)
    gain_first, gain_attention, gain_convolution = (
        first_grads[0],
        attention_grads[0],
        convolution_grads[0],
    )
    gain_second, gain_final = (second_feed_gradients[0], final_grad)
    every_grad = (
        lax.psum_scatter(gain_first, "dp", scatter_dimension=0, tiled=True),
        lax.psum_scatter(first_grads[1], "dp", scatter_dimension=0, tiled=True),
        lax.psum_scatter(first_grads[2], "dp", scatter_dimension=0, tiled=True),
        lax.psum_scatter(gain_attention, "dp", scatter_dimension=0, tiled=True),
        lax.psum_scatter(attention_grads[1], "dp", scatter_dimension=0, tiled=True),
        lax.psum_scatter(attention_grads[2], "dp", scatter_dimension=0, tiled=True),
        lax.psum_scatter(attention_grads[3], "dp", scatter_dimension=0, tiled=True),
        lax.psum_scatter(attention_grads[4], "dp", scatter_dimension=0, tiled=True),
        lax.psum_scatter(attention_grads[5], "dp", scatter_dimension=0, tiled=True),
        lax.psum_scatter(attention_grads[6], "dp", scatter_dimension=0, tiled=True),
        lax.psum_scatter(attention_grads[7], "dp", scatter_dimension=0, tiled=True),
        lax.psum_scatter(gain_convolution, "dp", scatter_dimension=0, tiled=True),
        lax.psum_scatter(convolution_grads[1], "dp", scatter_dimension=0, tiled=True),
        lax.psum_scatter(convolution_grads[2], "dp", scatter_dimension=0, tiled=True),
        lax.psum_scatter(convolution_grads[3], "dp", scatter_dimension=0, tiled=True),
        lax.psum_scatter(gain_second, "dp", scatter_dimension=0, tiled=True),
        lax.psum_scatter(second_feed_gradients[1], "dp", scatter_dimension=0, tiled=True),
        lax.psum_scatter(second_feed_gradients[2], "dp", scatter_dimension=0, tiled=True),
        lax.psum_scatter(gain_final, "dp", scatter_dimension=0, tiled=True),
    )
    return (
        result,
        residual_grad,
        every_grad[0],
        every_grad[1],
        every_grad[2],
        every_grad[3],
        every_grad[4],
        every_grad[5],
        every_grad[6],
        every_grad[7],
        every_grad[8],
        every_grad[9],
        every_grad[10],
        every_grad[11],
        every_grad[12],
        every_grad[13],
        gain_piece,
        shift_piece,
        every_grad[14],
        every_grad[15],
        every_grad[16],
        every_grad[17],
        every_grad[18],
    )


def solution(mesh):
    return jax.shard_map(
        per_device,
        mesh=mesh,
        in_specs=(
            P("dp", None),
            P("dp", None),
            P("dp", None),
            P("dp"),
            P("dp", "mp"),
            P("dp", "mp"),
            P("dp"),
            P("dp", "mp"),
            P("dp", "mp"),
            P("dp", "mp"),
            P("dp", "mp"),
            P("dp", "mp"),
            P("dp", "mp"),
            P("dp", "mp"),
            P("dp"),
            P("dp", None, "mp"),
            P(("mp", "dp"), None),
            P(("mp", "dp")),
            P(("mp", "dp")),
            P("dp", "mp"),
            P("dp"),
            P("dp", "mp"),
            P("dp", "mp"),
            P("dp"),
        ),
        out_specs=(
            P("dp", None),
            P("dp", None),
            P("dp"),
            P("dp", "mp"),
            P("dp", "mp"),
            P("dp"),
            P("dp", "mp"),
            P("dp", "mp"),
            P("dp", "mp"),
            P("dp", "mp"),
            P("dp", "mp"),
            P("dp", "mp"),
            P("dp", "mp"),
            P("dp"),
            P("dp", None, "mp"),
            P(("mp", "dp"), None),
            P(("mp", "dp")),
            P(("mp", "dp")),
            P("dp", "mp"),
            P("dp"),
            P("dp", "mp"),
            P("dp", "mp"),
            P("dp"),
        ),
        check_vma=False,
    )
```

profile of v0, /device:TPU:0, one launch (start us, length us, event | category | flops | bytes accessed | tf_op | source)
XLA Modules:
  0.0 1925.7 jit_solution(13970487286113267523)
XLA Ops:
  85.5 32.8 %all_gather.83 = bf16[1024,256]{1,0:T(8,128)(2,1)S(1)} all-gather(bf16[128,256]{1,0:T(8,128)(2,1)S(1)} %convert_element_type.333), channel_id=1, replica_groups=mesh['dp'=8,'mp'=4] {'dp'}, dimensions={0}, use_global_device_ids=true | all-gather | bytes 589824 | tf_op jit(solution)/shard_map/all_gather | solution.py:137
  118.2 31.5 %all_gather.88 = bf16[1024,256]{1,0:T(8,128)(2,1)S(1)} all-gather(bf16[128,256]{1,0:T(8,128)(2,1)S(1)} %convert_element_type.345), channel_id=1, replica_groups=mesh['dp'=8,'mp'=4] {'dp'}, dimensions={0}, use_global_device_ids=true | all-gather | bytes 589824 | tf_op jit(solution)/shard_map/all_gather | solution.py:138
  149.8 33.4 %all_gather.84 = bf16[1024,256]{1,0:T(8,128)(2,1)} all-gather(bf16[128,256]{1,0:T(8,128)(2,1)S(1)} %convert_element_type.336), channel_id=1, replica_groups=mesh['dp'=8,'mp'=4] {'dp'}, dimensions={0}, use_global_device_ids=true | all-gather | bytes 589824 | tf_op jit(solution)/shard_map/all_gather | solution.py:135
  214.4 33.2 %all_gather.89 = bf16[1024,256]{1,0:T(8,128)(2,1)} all-gather(bf16[128,256]{1,0:T(8,128)(2,1)S(1)} %convert_element_type.350), channel_id=1, replica_groups=mesh['dp'=8,'mp'=4] {'dp'}, dimensions={0}, use_global_device_ids=true | all-gather | bytes 589824 | tf_op jit(solution)/shard_map/all_gather | solution.py:139
  404.9 34.0 %all_gather.95 = bf16[1024,256]{1,0:T(8,128)(2,1)} all-gather(bf16[128,256]{1,0:T(8,128)(2,1)S(1)} %convert_element_type.369), channel_id=1, replica_groups=mesh['dp'=8,'mp'=4] {'dp'}, dimensions={0}, use_global_device_ids=true | all-gather | bytes 589824 | tf_op jit(solution)/shard_map/all_gather | solution.py:154
  504.4 49.5 %all-gather.20.cloned.1.call-done = bf16[1024,1024]{1,0:T(8,128)(2,1)} async-done(((bf16[128,1024]{1,0:T(8,128)(2,1)}), bf16[1024,1024]{1,0:T(8,128)(2,1)}) %all-gather.20.cloned.1.call-update) | async-done | bytes 2097168 | tf_op jit(solution)/shard_map/all_gather | solution.py:117
  558.2 45.9 %all-gather.22.cloned.1.call-done = bf16[1024,1024]{1,0:T(8,128)(2,1)} async-done(((bf16[128,1024]{1,0:T(8,128)(2,1)}), bf16[1024,1024]{1,0:T(8,128)(2,1)}) %all-gather.22.cloned.1.call-update) | async-done | bytes 2097168 | tf_op jit(solution)/shard_map/all_gather | solution.py:118
  654.7 36.6 %all-reduce.47.cloned.1.call-done = bf16[512,1024]{1,0:T(8,128)(2,1)} async-done(((bf16[512,1024]{1,0:T(8,128)(2,1)}), bf16[512,1024]{1,0:T(8,128)(2,1)}) %all-reduce.47.cloned.1.call-update) | async-done | bytes 1048592 | tf_op jit(solution)/shard_map/psum | solution.py:103
  728.3 32.9 %all-reduce.49.cloned.1.call-done = bf16[512,1024]{1,0:T(8,128)(2,1)} async-done(((bf16[512,1024]{1,0:T(8,128)(2,1)}), bf16[512,1024]{1,0:T(8,128)(2,1)}) %all-reduce.49.cloned.1.call-update) | async-done | bytes 1048592 | tf_op jit(solution)/shard_map/psum | solution.py:103
  814.6 33.6 %all-reduce.51.cloned.1.call-done = bf16[512,1024]{1,0:T(8,128)(2,1)} async-done(((bf16[512,1024]{1,0:T(8,128)(2,1)}), bf16[512,1024]{1,0:T(8,128)(2,1)}) %all-reduce.51.cloned.1.call-update) | async-done | bytes 1048592 | tf_op jit(solution)/shard_map/psum | solution.py:103
  914.5 62.6 %reduce-scatter.43.cloned.1.call-done = f32[16,2]{1,0:T(8,128)} async-done(((f32[128,2]{1,0:T(8,128)}), f32[16,2]{1,0:T(8,128)}) %reduce-scatter.43.cloned.1.call-update) | async-done | bytes 144
  978.4 62.6 %reduce-scatter.45.cloned.1.call-done = f32[16,2]{1,0:T(8,128)} async-done(((f32[128,2]{1,0:T(8,128)}), f32[16,2]{1,0:T(8,128)}) %reduce-scatter.45.cloned.1.call-update) | async-done | bytes 144
  1042.4 36.2 %all-reduce.53.cloned.1.call-done = bf16[512,1024]{1,0:T(8,128)(2,1)} async-done(((bf16[512,1024]{1,0:T(8,128)(2,1)}), bf16[512,1024]{1,0:T(8,128)(2,1)}) %all-reduce.53.cloned.1.call-update) | async-done | bytes 1048592 | tf_op jit(solution)/shard_map/psum | solution.py:103
  1081.7 37.3 %all-reduce.26 = (f32[1024]{0:T(1024)S(1)}, f32[1024]{0:T(1024)S(1)}, f32[1024]{0:T(1024)S(1)}, f32[1024]{0:T(1024)S(1)}, f32[1024]{0:T(1024)S(1)}) all-reduce(f32[1024]{0:T(1024)S(1)} %get-tuple-element.146, f32[1024]{0:T(1024)S(1)} %get-tuple-element.142, ...), channel_id=2, replica_groups=mesh['dp'=8,'mp'=4] {'dp'}, use_global_device_ids=true, to_apply=%region_44.45.clone | all-reduce | flops 5120 | bytes 40960
  1152.8 64.5 %reduce-scatter.37.cloned.1.call-done = f32[128,256]{1,0:T(8,128)} async-done(((f32[1024,256]{1,0:T(8,128)}), f32[128,256]{1,0:T(8,128)}) %reduce-scatter.37.cloned.1.call-update) | async-done | bytes 131088 | tf_op jit(solution)/shard_map/reduce_scatter | solution.py:526
  1217.3 66.9 %reduce-scatter.25.cloned.1.call-done = f32[128,256]{1,0:T(8,128)} async-done(((f32[1024,256]{1,0:T(8,128)}), f32[128,256]{1,0:T(8,128)}) %reduce-scatter.25.cloned.1.call-update) | async-done | bytes 131088 | tf_op jit(solution)/shard_map/reduce_scatter | solution.py:516
  1284.2 66.3 %reduce-scatter.27.cloned.1.call-done = f32[128,256]{1,0:T(8,128)} async-done(((f32[1024,256]{1,0:T(8,128)}), f32[128,256]{1,0:T(8,128)}) %reduce-scatter.27.cloned.1.call-update) | async-done | bytes 131088 | tf_op jit(solution)/shard_map/reduce_scatter | solution.py:517
  1350.5 66.9 %reduce-scatter.29.cloned.1.call-done = f32[128,256]{1,0:T(8,128)} async-done(((f32[1024,256]{1,0:T(8,128)}), f32[128,256]{1,0:T(8,128)}) %reduce-scatter.29.cloned.1.call-update) | async-done | bytes 131088 | tf_op jit(solution)/shard_map/reduce_scatter | solution.py:518
  1417.4 66.5 %reduce-scatter.31.cloned.1.call-done = f32[128,256]{1,0:T(8,128)} async-done(((f32[1024,256]{1,0:T(8,128)}), f32[128,256]{1,0:T(8,128)}) %reduce-scatter.31.cloned.1.call-update) | async-done | bytes 131088 | tf_op jit(solution)/shard_map/reduce_scatter | solution.py:519
  1483.9 67.0 %reduce-scatter.33.cloned.1.call-done = f32[128,256]{1,0:T(8,128)} async-done(((f32[1024,256]{1,0:T(8,128)}), f32[128,256]{1,0:T(8,128)}) %reduce-scatter.33.cloned.1.call-update) | async-done | bytes 131088 | tf_op jit(solution)/shard_map/reduce_scatter | solution.py:520
  1550.9 91.1 %reduce-scatter.39.cloned.1.call-done = f32[128,1024]{1,0:T(8,128)} async-done(((f32[1024,1024]{1,0:T(8,128)}), f32[128,1024]{1,0:T(8,128)}) %reduce-scatter.39.cloned.1.call-update) | async-done | bytes 524304 | tf_op jit(solution)/shard_map/reduce_scatter | solution.py:528
  1642.0 92.5 %reduce-scatter.41.cloned.1.call-done = f32[128,1024]{1,0:T(8,128)} async-done(((f32[1024,1024]{1,0:T(8,128)}), f32[128,1024]{1,0:T(8,128)}) %reduce-scatter.41.cloned.1.call-update) | async-done | bytes 524304 | tf_op jit(solution)/shard_map/reduce_scatter | solution.py:529
  1734.6 91.7 %reduce-scatter.21.cloned.1.call-done = f32[128,1024]{1,0:T(8,128)} async-done(((f32[1024,1024]{1,0:T(8,128)}), f32[128,1024]{1,0:T(8,128)}) %reduce-scatter.21.cloned.1.call-update) | async-done | bytes 524304 | tf_op jit(solution)/shard_map/reduce_scatter | solution.py:513
  1826.3 92.3 %reduce-scatter.23.cloned.1.call-done = f32[128,1024]{1,0:T(8,128)} async-done(((f32[1024,1024]{1,0:T(8,128)}), f32[128,1024]{1,0:T(8,128)}) %reduce-scatter.23.cloned.1.call-update) | async-done | bytes 524304 | tf_op jit(solution)/shard_map/reduce_scatter | solution.py:514
  (450 shorter events, 580.4 us)
Async XLA Ops:
  7.3 241.2 %all-gather.14.cloned.1.call-start = ((), (), s32[]{:S(2)}) async-start(), calls=%async_computation.14 | async-start | bytes 2359296 | tf_op jit(solution)/shard_map/all_gather | solution.py:109
  9.3 243.4 %all-gather.16.cloned.1.call-start = ((), (), s32[]{:S(2)}) async-start(), calls=%async_computation.15 | async-start | bytes 2359296 | tf_op jit(solution)/shard_map/all_gather | solution.py:110
  11.2 280.6 %all-reduce.39.cloned.1.call-start = ((), (), s32[]{:S(2)}) async-start(), calls=%async_computation.16 | async-start | bytes 2097152 | tf_op jit(solution)/shard_map/psum | solution.py:103
  257.2 181.7 %all-reduce.41.cloned.1.call-start = ((), (), s32[]{:S(2)}) async-start(), calls=%async_computation.17 | async-start | bytes 2097152 | tf_op jit(solution)/shard_map/psum | solution.py:103
  339.2 102.3 %all-gather.18.cloned.1.call-start = ((), (), s32[]{:S(2)}) async-start(), calls=%async_computation.18 | async-start | bytes 1179648 | tf_op jit(solution)/shard_map/all_gather | solution.py:150
  339.9 162.0 %all-reduce.43.cloned.1.call-start = ((), (), s32[]{:S(2)}) async-start(), calls=%async_computation.19 | async-start | bytes 2097152 | tf_op jit(solution)/shard_map/psum | solution.py:103
  469.6 134.4 %all-gather.22.cloned.1.call-start = ((), (), s32[]{:S(2)}) async-start(), calls=%async_computation.21 | async-start | bytes 2359296 | tf_op jit(solution)/shard_map/all_gather | solution.py:118
  470.5 172.8 %all-reduce.45.cloned.1.call-start = ((), (), s32[]{:S(2)}) async-start(), calls=%async_computation.22 | async-start | bytes 2097152 | tf_op jit(solution)/shard_map/psum | solution.py:103
  654.7 106.5 %all-reduce.49.cloned.1.call-start = ((), (), s32[]{:S(2)}) async-start(), calls=%async_computation.24 | async-start | bytes 2097152 | tf_op jit(solution)/shard_map/psum | solution.py:103
  728.3 120.0 %all-reduce.51.cloned.1.call-start = ((), (), s32[]{:S(2)}) async-start(), calls=%async_computation.25 | async-start | bytes 2097152 | tf_op jit(solution)/shard_map/psum | solution.py:103
  812.5 164.6 %reduce-scatter.43.cloned.1.call-start = ((), (), s32[]{:S(2)}) async-start(), calls=%async_computation.38 | async-start | bytes 73728
  813.3 227.7 %reduce-scatter.45.cloned.1.call-start = ((), (), s32[]{:S(2)}) async-start(), calls=%async_computation.39 | async-start | bytes 73728
  814.1 264.4 %all-reduce.53.cloned.1.call-start = ((), (), s32[]{:S(2)}) async-start(), calls=%async_computation.26 | async-start | bytes 2097152 | tf_op jit(solution)/shard_map/psum | solution.py:103
  859.4 291.6 %reduce-scatter.35.cloned.1.call-start = ((), (), s32[]{:S(2)}) async-start(), calls=%async_computation.34 | async-start | bytes 2359296 | tf_op jit(solution)/shard_map/reduce_scatter | solution.py:524
  863.5 353.8 %reduce-scatter.37.cloned.1.call-start = ((), (), s32[]{:S(2)}) async-start(), calls=%async_computation.35 | async-start | bytes 1179648 | tf_op jit(solution)/shard_map/reduce_scatter | solution.py:526
  867.4 416.7 %reduce-scatter.25.cloned.1.call-start = ((), (), s32[]{:S(2)}) async-start(), calls=%async_computation.29 | async-start | bytes 1179648 | tf_op jit(solution)/shard_map/reduce_scatter | solution.py:516
  870.3 480.2 %reduce-scatter.27.cloned.1.call-start = ((), (), s32[]{:S(2)}) async-start(), calls=%async_computation.30 | async-start | bytes 1179648 | tf_op jit(solution)/shard_map/reduce_scatter | solution.py:517
  873.2 544.3 %reduce-scatter.29.cloned.1.call-start = ((), (), s32[]{:S(2)}) async-start(), calls=%async_computation.31 | async-start | bytes 1179648 | tf_op jit(solution)/shard_map/reduce_scatter | solution.py:518
  875.9 608.0 %reduce-scatter.31.cloned.1.call-start = ((), (), s32[]{:S(2)}) async-start(), calls=%async_computation.32 | async-start | bytes 1179648 | tf_op jit(solution)/shard_map/reduce_scatter | solution.py:519
  880.2 670.7 %reduce-scatter.33.cloned.1.call-start = ((), (), s32[]{:S(2)}) async-start(), calls=%async_computation.33 | async-start | bytes 1179648 | tf_op jit(solution)/shard_map/reduce_scatter | solution.py:520
  883.4 758.6 %reduce-scatter.39.cloned.1.call-start = ((), (), s32[]{:S(2)}) async-start(), calls=%async_computation.36 | async-start | bytes 4718592 | tf_op jit(solution)/shard_map/reduce_scatter | solution.py:528
  888.1 846.5 %reduce-scatter.41.cloned.1.call-start = ((), (), s32[]{:S(2)}) async-start(), calls=%async_computation.37 | async-start | bytes 4718592 | tf_op jit(solution)/shard_map/reduce_scatter | solution.py:529
  894.7 931.6 %reduce-scatter.21.cloned.1.call-start = ((), (), s32[]{:S(2)}) async-start(), calls=%async_computation.27 | async-start | bytes 4718592 | tf_op jit(solution)/shard_map/reduce_scatter | solution.py:513
  899.3 1019.3 %reduce-scatter.23.cloned.1.call-start = ((), (), s32[]{:S(2)}) async-start(), calls=%async_computation.28 | async-start | bytes 4718592 | tf_op jit(solution)/shard_map/reduce_scatter | solution.py:514
  (102 other events, 2148.3 us)
Sparse Core Ops, SparseCore 0:
  10.8 52.0 all-gather.13
  65.6 55.4 all-gather.15
  339.3 36.4 all-reduce.40
  378.4 43.0 all-gather.17
  504.2 49.6 all-gather.19
  556.3 47.7 all-gather.21
  608.7 34.5 all-reduce.44
  654.8 36.4 all-reduce.46
  811.7 36.4 all-reduce.50
  851.9 61.2 reduce-scatter.46
  916.8 60.2 reduce-scatter.42
  980.7 60.2 reduce-scatter.44
  1043.4 35.1 all-reduce.52
  1082.0 68.9 reduce-scatter.34
  1154.8 62.4 reduce-scatter.36
  1221.7 62.4 reduce-scatter.24
  1288.0 62.4 reduce-scatter.26
  1354.9 62.5 reduce-scatter.28
  1421.4 62.4 reduce-scatter.30
  1488.3 62.5 reduce-scatter.32
  1555.0 87.0 reduce-scatter.38
  1646.7 87.8 reduce-scatter.40
  1738.6 87.6 reduce-scatter.20
  1830.8 87.8 reduce-scatter.22
  (3 shorter events, 100.0 us)
where the time goes:
time: 1930 us
  waiting for transfers between devices  1210 us (63%)
  blocking collectives  445 us (23%)
  local copies, waits for them, and re-layouts  97.2 us (5%)
  matrix products  96.2 us (5%)
  other arithmetic  56.3 us (3%)
    psum x8, waiting for transfers between devices, branch_total(): return lax.psum(piece_terms.astype(jnp.bfloat16), 'mp').astype(jnp.float32)  194 us
    unnamed x30, waiting for transfers between devices  131 us
    reduce_scatter x1, waiting for transfers between devices, per_device(): lax.psum_scatter(second_feed_gradients[2], 'dp', scatter_dimension=0, til...  92.5 us
    reduce_scatter x1, waiting for transfers between devices, per_device(): lax.psum_scatter(first_grads[2], 'dp', scatter_dimension=0, tiled=True)  92.3 us
    reduce_scatter x1, waiting for transfers between devices, per_device(): lax.psum_scatter(first_grads[1], 'dp', scatter_dimension=0, tiled=True)  91.7 us
    reduce_scatter x1, waiting for transfers between devices, per_device(): lax.psum_scatter(second_feed_gradients[1], 'dp', scatter_dimension=0, til...  91.1 us
    reduce_scatter x1, waiting for transfers between devices, per_device(): lax.psum_scatter(attention_grads[5], 'dp', scatter_dimension=0, tiled=True)  67 us
    reduce_scatter x1, waiting for transfers between devices, per_device(): lax.psum_scatter(attention_grads[3], 'dp', scatter_dimension=0, tiled=True)  66.9 us
  transfers between devices with their start and end apart: 27, of which 23 were waited for; matrix products, arithmetic and copies ran while one was open for 5% of the time, Pallas kernels for 0%

commit v1 on v0

v1 whole, which is shorter than its diff:
```python
import math

import jax
import jax.numpy as jnp
from jax import lax
from jax.sharding import PartitionSpec as P

EPSILON = 1e-05
LOW = jnp.bfloat16
FLOAT = jnp.float32


def matmul(left_side, right_side):
    return jnp.dot(left_side, right_side, preferred_element_type=FLOAT)


def times_transposed(left_side, right_side):
    return lax.dot_general(
        left_side, right_side, (((1,), (1,)), ((), ())), preferred_element_type=FLOAT
    )


def outer_sum(left_side, right_side):
    return lax.dot_general(
        left_side, right_side, (((0,), (0,)), ((), ())), preferred_element_type=FLOAT
    )


def reversed_bits(places, size):
    outcome = places * 0
    mask, back = size // 2, 1
    while mask:
        outcome = outcome + ((places // back) % 2) * mask
        mask, back = mask // 2, back * 2
    return outcome


def swap(values, axis, mask):
    size = lax.axis_size(axis)
    return lax.ppermute(values, axis, [(i, i ^ mask) for i in range(size)])


def spread(values, axis):
    mask = lax.axis_size(axis) // 2
    while mask:
        values = jnp.concatenate([values, swap(values, axis, mask)], axis=0)
        mask //= 2
    return values


def collect(values, axis, wire, mask=1):
    while mask < lax.axis_size(axis):
        half = values.shape[0] // 2
        values = values[:half] + swap(values[half:].astype(wire), axis, mask).astype(FLOAT)
        mask *= 2
    return values


def total_over(values, axis):
    mask = 1
    while mask < lax.axis_size(axis):
        values = values + swap(values, axis, mask)
        mask *= 2
    return values


def reduce_rows(left_side, right_side):
    half = left_side.shape[0] // 2
    sent = swap(times_transposed(left_side[half:], right_side).astype(LOW), "mp", 1)
    kept = times_transposed(left_side[:half], right_side) + sent.astype(FLOAT)
    return collect(kept, "mp", LOW, 2)


def reduce_weight(left_side, right_side):
    half = left_side.shape[1] // 2
    sent = swap(outer_sum(left_side[:, half:], right_side).astype(LOW), "dp", 1)
    kept = outer_sum(left_side[:, :half], right_side) + sent.astype(FLOAT)
    return collect(kept, "dp", LOW, 2)


def standardize(values):
    average = jnp.mean(values, axis=-1, keepdims=True)
    centred = values - average
    spread_of = jnp.mean(centred * centred, axis=-1, keepdims=True)
    scale = lax.rsqrt(spread_of + EPSILON)
    return centred * scale, scale


def layer_norm(values, norm_gain):
    return standardize(values)[0] * norm_gain


def norm_back(values, norm_gain, normed_grad):
    hat, scale = standardize(values)
    gained = normed_grad * norm_gain
    first = jnp.mean(gained, axis=-1, keepdims=True)
    second = jnp.mean(gained * hat, axis=-1, keepdims=True)
    return (gained - first - hat * second) * scale, jnp.sum(normed_grad * hat, axis=0)


def segment_ids(utterances, row_count):
    bounds = jnp.cumsum(utterances)
    places = jnp.arange(row_count, dtype=jnp.int32)
    return jnp.sum((places[:, None] >= bounds[None, :]).astype(jnp.int32), axis=1)


def position_table(row_count, feature_count):
    offsets = (row_count - 1 - jnp.arange(2 * row_count - 1)).astype(FLOAT)
    rates = jnp.exp(
        jnp.arange(0, feature_count, 2).astype(FLOAT) * (-math.log(10000.0) / feature_count)
    )
    angles = offsets[:, None] * rates[None, :]
    return jnp.concatenate([jnp.sin(angles), jnp.cos(angles)], axis=1)


def shear_rows(broad_score_rows):
    head_count, row_count, span_count = broad_score_rows.shape
    flattened = broad_score_rows.reshape(head_count, row_count * span_count)
    flattened = flattened[:, row_count - 1 : row_count - 1 + row_count * (span_count - 1)]
    return flattened.reshape(head_count, row_count, span_count - 1)[:, :, :row_count]


def unshear_rows(narrow):
    head_count, row_count = (narrow.shape[0], narrow.shape[1])
    padded = jnp.pad(narrow, ((0, 0), (0, 0), (0, row_count - 2)))
    flattened = jnp.pad(
        padded.reshape(head_count, row_count * (2 * row_count - 2)), ((0, 0), (row_count - 1, 1))
    )
    return flattened.reshape(head_count, row_count, 2 * row_count - 1)


def shift_rows(values, offset):
    row_count = values.shape[0]
    if offset > 0:
        return jnp.concatenate(
            [values[offset:], jnp.zeros((offset,) + values.shape[1:], values.dtype)], axis=0
        )
    if offset < 0:
        return jnp.concatenate(
            [jnp.zeros((-offset,) + values.shape[1:], values.dtype), values[: row_count + offset]],
            axis=0,
        )
    return values


def depthwise(gated_rows, kernel, segment):
    tap_count = kernel.shape[1]
    marker = segment + 1
    output = jnp.zeros_like(gated_rows)
    for tap_index in range(tap_count):
        offset = tap_index - tap_count // 2
        matching = (shift_rows(marker, offset) == marker).astype(gated_rows.dtype)
        output = output + kernel[:, tap_index][None, :] * matching[:, None] * shift_rows(
            gated_rows, offset
        )
    return output


def gated_conv(lifted, kernel, segment, valid_rows):
    half = lifted.shape[1] // 2
    gated_rows = lifted[:, :half] * jax.nn.sigmoid(lifted[:, half:]) * valid_rows[:, None]
    return depthwise(gated_rows, kernel, segment)


def attention_scores(with_content, with_position, key_rows, relative_offset, segment):
    head_size = key_rows.shape[2]
    direct = jnp.einsum("ihd,jhd->hij", with_content, key_rows, preferred_element_type=FLOAT)
    broad_score_rows = jnp.einsum(
        "tkn,ukn->ktu", with_position, relative_offset, preferred_element_type=FLOAT
    )
    scores = (direct + shear_rows(broad_score_rows)) * head_size ** (-0.5)
    matching = segment[:, None] == segment[None, :]
    return jnp.where(matching[None], scores, -1e30)


def ffn_forward(residual, normed, up_weight, down_weight):
    before = matmul(normed, up_weight)
    active = (before * jax.nn.sigmoid(before)).astype(LOW)
    return residual + 0.5 * reduce_rows(active, down_weight), (before, active)


def ffn_backward(residual_grad, residual, norm_gain, normed, up_weight, down_weight, stored):
    before, active = stored
    branch_grad = spread((0.5 * residual_grad).astype(LOW), "mp")
    squashed = jax.nn.sigmoid(before)
    before_grad = (
        matmul(branch_grad, down_weight) * squashed * (1.0 + before * (1.0 - squashed))
    ).astype(LOW)
    normed_grad = reduce_rows(before_grad, up_weight)
    down_grad = reduce_weight(branch_grad, active)
    up_grad = reduce_weight(normed, before_grad)
    input_grad, gain_grad = norm_back(residual, norm_gain, normed_grad)
    return residual_grad + input_grad, gain_grad, up_grad, down_grad


def per_device(
    inputs,
    lengths,
    out_grad,
    first_norm,
    first_up,
    first_down,
    attention_norm,
    query_weight,
    key_weight,
    value_weight,
    position_weight,
    output_weight,
    content_bias,
    position_bias,
    convolution_norm,
    pointwise_in,
    depthwise_kernel,
    batch_gain,
    batch_shift,
    pointwise_out,
    second_norm,
    second_up,
    second_down,
    final_norm,
):
    row_count, feature_count = inputs.shape
    dp_size, mp_size = lax.axis_size("dp"), lax.axis_size("mp")
    dp_at, mp_at = lax.axis_index("dp"), lax.axis_index("mp")
    block = first_up.shape[0]
    row_block = row_count // mp_size
    bias_rows, head_count = content_bias.shape
    head_size = bias_rows * dp_size
    local_channels, tap_count = depthwise_kernel.shape
    channels = local_channels * dp_size
    score_scale = head_size ** (-0.5)

    places = jnp.arange(feature_count, dtype=jnp.int32)
    owners = dp_at ^ reversed_bits(places // block, dp_size)
    source = owners * block + places % block
    selection = (places[:, None] == source[None, :]).astype(LOW)
    block_places = jnp.arange(dp_size, dtype=jnp.int32)
    block_owners = dp_at ^ reversed_bits(block_places, dp_size)
    block_selection = (block_places[:, None] == block_owners[None, :]).astype(FLOAT)
    mp_back = reversed_bits(mp_at, mp_size)

    def own_rows(values):
        pieces = [
            lax.dynamic_slice_in_dim(
                values, (mp_at ^ reversed_bits(p, mp_size)) * row_block, row_block, axis=0
            )
            for p in range(mp_size)
        ]
        return jnp.concatenate(pieces, axis=0)

    def plain_rows(values):
        pieces = [
            lax.dynamic_slice_in_dim(
                values, (mp_back ^ reversed_bits(p, mp_size)) * row_block, row_block, axis=0
            )
            for p in range(mp_size)
        ]
        return jnp.concatenate(pieces, axis=0)

    first_up_all = spread(first_up.astype(LOW), "dp")
    small_parts = [
        first_norm, attention_norm, convolution_norm, second_norm, final_norm,
        content_bias.reshape(-1), position_bias.reshape(-1), depthwise_kernel.reshape(-1),
        batch_gain, batch_shift,
    ]
    small_own = jnp.concatenate([part.astype(LOW).astype(FLOAT) for part in small_parts])
    small_all = spread(small_own[None], "dp")
    first_down_all = spread(first_down.astype(LOW), "dp")
    attention_own = jnp.concatenate(
        [query_weight, key_weight, value_weight, position_weight, output_weight], axis=1
    ).astype(LOW)
    attention_all = spread(attention_own, "dp")
    convolution_own = jnp.concatenate(
        [pointwise_in.reshape(block, 2 * channels), pointwise_out], axis=1
    ).astype(LOW)
    convolution_all = spread(convolution_own, "dp")
    second_up_all = spread(second_up.astype(LOW), "dp")
    second_down_all = spread(second_down.astype(LOW), "dp")

    norms = small_all[:, : 5 * block].reshape(dp_size, 5, block)
    norms = norms.transpose(1, 0, 2).reshape(5, feature_count)
    first_gain, attention_gain, convolution_gain, second_gain, final_gain = norms
    plain_small = jnp.dot(
        block_selection, small_all[:, 5 * block :], preferred_element_type=FLOAT
    )
    cut = bias_rows * head_count
    content_all = plain_small[:, :cut].reshape(head_size, head_count)
    position_all = plain_small[:, cut : 2 * cut].reshape(head_size, head_count)
    at = 2 * cut + local_channels * tap_count
    taps = plain_small[:, 2 * cut : at].reshape(channels, tap_count)
    gain_all = plain_small[:, at : at + local_channels].reshape(channels)
    shift_all = plain_small[:, at + local_channels :].reshape(channels)

    segment = segment_ids(lengths[0], row_count)
    valid_rows = (segment < lengths.shape[1]).astype(FLOAT)
    arranged = matmul(own_rows(inputs), selection)
    own_out_grad = matmul(
        lax.dynamic_slice_in_dim(out_grad, mp_at * row_block, row_block, axis=0), selection
    )
    sin_table = position_table(row_count, feature_count).astype(LOW)
    sin_table = matmul(sin_table, selection).astype(LOW)
    frame_count = jnp.sum(valid_rows)

    residual_zero = arranged[:row_block]
    normed_a = layer_norm(arranged, first_gain).astype(LOW)
    residual_one, first_stored = ffn_forward(residual_zero, normed_a, first_up_all, first_down_all)

    heads = head_count * head_size
    normed_b = spread(layer_norm(residual_one, attention_gain).astype(LOW), "mp")
    qkv_weight = attention_all[:, : 3 * heads]
    position_weight_all = attention_all[:, 3 * heads : 4 * heads]
    output_weight_all = attention_all[:, 4 * heads :]
    qkv = plain_rows(matmul(normed_b, qkv_weight))
    query_rows = qkv[:, :heads].reshape(row_count, head_count, head_size)
    with_content = (query_rows + content_all.T[None]).astype(LOW)
    with_position = (query_rows + position_all.T[None]).astype(LOW)
    key_rows = qkv[:, heads : 2 * heads].astype(LOW).reshape(row_count, head_count, head_size)
    value_rows = qkv[:, 2 * heads :].astype(LOW).reshape(row_count, head_count, head_size)
    relative_offset = (
        matmul(sin_table, position_weight_all)
        .astype(LOW)
        .reshape(2 * row_count - 1, head_count, head_size)
    )
    masked = attention_scores(with_content, with_position, key_rows, relative_offset, segment)
    row_peak = jnp.max(masked, axis=-1, keepdims=True)
    exponent = jnp.exp(masked - row_peak)
    prob_low = (exponent / jnp.sum(exponent, axis=-1, keepdims=True)).astype(LOW)
    mixed_rows = jnp.einsum("hij,jhd->ihd", prob_low, value_rows, preferred_element_type=FLOAT)
    mixed_rows = own_rows(mixed_rows.astype(LOW).reshape(row_count, heads))
    residual_two = residual_one + reduce_rows(mixed_rows, output_weight_all)

    normed_c = spread(layer_norm(residual_two, convolution_gain).astype(LOW), "mp")
    pointwise_in_all = convolution_all[:, : 2 * channels]
    pointwise_out_all = convolution_all[:, 2 * channels :]
    lifted = plain_rows(matmul(normed_c, pointwise_in_all))
    convolved = gated_conv(lifted, taps, segment, valid_rows)
    masked_conv = convolved * valid_rows[:, None]
    sums = jnp.stack(
        [
            jnp.sum(masked_conv, axis=0),
            jnp.sum(masked_conv * convolved, axis=0),
            jnp.broadcast_to(frame_count, (channels,)),
        ]
    )
    sums = total_over(sums, "dp")
    frame_total = sums[2]
    average = sums[0] / frame_total
    inverse = lax.rsqrt(sums[1] / frame_total - average * average + EPSILON)
    hatted = (convolved - average) * inverse
    normalized = hatted * gain_all + shift_all
    swished = own_rows(
        (normalized * jax.nn.sigmoid(normalized) * valid_rows[:, None]).astype(LOW)
    )
    residual_three = residual_two + reduce_rows(swished, pointwise_out_all)

    normed_d = spread(layer_norm(residual_three, second_gain).astype(LOW), "mp")
    residual_four, second_stored = ffn_forward(
        residual_three, normed_d, second_up_all, second_down_all
    )
    own_result = layer_norm(residual_four, final_gain).astype(LOW)
    result = plain_rows(spread(times_transposed(own_result, selection).astype(LOW), "mp"))

    residual_grad, final_gain_grad = norm_back(residual_four, final_gain, own_out_grad)
    residual_grad, second_gain_grad, second_up_grad, second_down_grad = ffn_backward(
        residual_grad, residual_three, second_gain, normed_d, second_up_all, second_down_all,
        second_stored,
    )

    branch_grad = spread(residual_grad.astype(LOW), "mp")
    squashed = jax.nn.sigmoid(normalized)
    normal_grad = (
        plain_rows(matmul(branch_grad, pointwise_out_all))
        * valid_rows[:, None]
        * squashed
        * (1.0 + normalized * (1.0 - squashed))
    )
    back_sums = total_over(
        jnp.stack([jnp.sum(normal_grad, axis=0), jnp.sum(normal_grad * hatted, axis=0)]), "dp"
    )
    shift_total, gain_total = back_sums[0], back_sums[1]
    conv_grad = inverse * (
        normal_grad * gain_all
        - valid_rows[:, None] * gain_all * (shift_total + hatted * gain_total) / frame_total
    )
    _, pullback = jax.vjp(
        lambda lifted_in, kernel_in: gated_conv(lifted_in, kernel_in, segment, valid_rows),
        lifted,
        taps,
    )
    lifted_grad, taps_grad = pullback(conv_grad)
    lifted_low = own_rows(lifted_grad.astype(LOW))
    normed_grad = reduce_rows(lifted_low, pointwise_in_all)
    pointwise_out_grad = reduce_weight(branch_grad, swished)
    pointwise_in_grad = reduce_weight(normed_c, lifted_low)
    input_grad, convolution_gain_grad = norm_back(residual_two, convolution_gain, normed_grad)
    residual_grad = residual_grad + input_grad
    first_row = dp_at * local_channels
    gain_piece = lax.dynamic_slice_in_dim(gain_total, first_row, local_channels)
    shift_piece = lax.dynamic_slice_in_dim(shift_total, first_row, local_channels)

    branch_grad = spread(residual_grad.astype(LOW), "mp")
    mixed_grad = plain_rows(matmul(branch_grad, output_weight_all).astype(LOW)).reshape(
        row_count, head_count, head_size
    )
    prob_rows = prob_low.astype(FLOAT)
    value_grad = jnp.einsum("hij,ihd->jhd", prob_low, mixed_grad, preferred_element_type=FLOAT)
    prob_grad = jnp.einsum("ihd,jhd->hij", mixed_grad, value_rows, preferred_element_type=FLOAT)
    inner_term = jnp.sum(prob_grad * prob_rows, axis=-1, keepdims=True)
    score_grad = (prob_rows * (prob_grad - inner_term)).astype(LOW)
    content_part = score_scale * jnp.einsum(
        "hij,jhd->ihd", score_grad, key_rows, preferred_element_type=FLOAT
    )
    key_grad = score_scale * jnp.einsum(
        "hij,ihd->jhd", score_grad, with_content, preferred_element_type=FLOAT
    )
    broad = unshear_rows(score_grad)
    position_part = score_scale * jnp.einsum(
        "yfa,ayt->fyt", broad, relative_offset, preferred_element_type=FLOAT
    )
    position_grad = score_scale * jnp.einsum(
        "nsq,snr->qnr", broad, with_position, preferred_element_type=FLOAT
    )
    position_grad = position_grad.astype(LOW).reshape(2 * row_count - 1, heads)
    qkv_grad = jnp.concatenate(
        [
            (content_part + position_part).astype(LOW).reshape(row_count, heads),
            key_grad.astype(LOW).reshape(row_count, heads),
            value_grad.astype(LOW).reshape(row_count, heads),
        ],
        axis=1,
    )
    qkv_grad = own_rows(qkv_grad)
    content_bias_grad = jnp.sum(content_part, axis=0).T
    position_bias_grad = jnp.sum(position_part, axis=0).T
    normed_grad = reduce_rows(qkv_grad, qkv_weight)
    output_weight_grad = reduce_weight(branch_grad, mixed_rows)
    qkv_weight_grad = reduce_weight(normed_b, qkv_grad)
    position_weight_grad = reduce_weight(sin_table, position_grad)
    input_grad, attention_gain_grad = norm_back(residual_one, attention_gain, normed_grad)
    residual_grad = residual_grad + input_grad

    residual_grad, first_gain_grad, first_up_grad, first_down_grad = ffn_backward(
        residual_grad, residual_zero, first_gain, normed_a, first_up_all, first_down_all,
        first_stored,
    )
    own_inputs_grad = times_transposed(residual_grad.astype(LOW), selection).astype(LOW)
    inputs_grad = plain_rows(spread(own_inputs_grad, "mp").astype(FLOAT))

    plain_grads = jnp.concatenate(
        [
            content_bias_grad.reshape(dp_size, cut),
            position_bias_grad.reshape(dp_size, cut),
            taps_grad.reshape(dp_size, local_channels * tap_count),
        ],
        axis=1,
    )
    plain_grads = lax.dot_general(
        block_selection, plain_grads, (((0,), (0,)), ((), ())),
        precision=lax.Precision.HIGHEST, preferred_element_type=FLOAT,
    )
    gain_grads = jnp.stack(
        [
            first_gain_grad, attention_gain_grad, convolution_gain_grad, second_gain_grad,
            final_gain_grad,
        ]
    )
    gain_grads = gain_grads.reshape(5, dp_size, block).transpose(1, 0, 2)
    small_grads = jnp.concatenate([gain_grads.reshape(dp_size, 5 * block), plain_grads], axis=1)
    small_grads = collect(small_grads, "dp", FLOAT)[0]
    gain_grads = total_over(small_grads[: 5 * block].reshape(5, block), "mp")
    plain_grads = small_grads[5 * block :]

    return (
        result,
        inputs_grad,
        gain_grads[0],
        first_up_grad,
        first_down_grad,
        gain_grads[1],
        qkv_weight_grad[:, :heads],
        qkv_weight_grad[:, heads : 2 * heads],
        qkv_weight_grad[:, 2 * heads :],
        position_weight_grad,
        output_weight_grad,
        plain_grads[:cut].reshape(bias_rows, head_count),
        plain_grads[cut : 2 * cut].reshape(bias_rows, head_count),
        gain_grads[2],
        pointwise_in_grad.reshape(block, 2, channels),
        plain_grads[2 * cut :].reshape(local_channels, tap_count),
        gain_piece,
        shift_piece,
        pointwise_out_grad,
        gain_grads[3],
        second_up_grad,
        second_down_grad,
        gain_grads[4],
    )


def solution(mesh):
    return jax.shard_map(
        per_device,
        mesh=mesh,
        in_specs=(
            P("dp", None),
            P("dp", None),
            P("dp", None),
            P("dp"),
            P("dp", "mp"),
            P("dp", "mp"),
            P("dp"),
            P("dp", "mp"),
            P("dp", "mp"),
            P("dp", "mp"),
            P("dp", "mp"),
            P("dp", "mp"),
            P("dp", "mp"),
            P("dp", "mp"),
            P("dp"),
            P("dp", None, "mp"),
            P(("mp", "dp"), None),
            P(("mp", "dp")),
            P(("mp", "dp")),
            P("dp", "mp"),
            P("dp"),
            P("dp", "mp"),
            P("dp", "mp"),
            P("dp"),
        ),
        out_specs=(
            P("dp", None),
            P("dp", None),
            P("dp"),
            P("dp", "mp"),
            P("dp", "mp"),
            P("dp"),
            P("dp", "mp"),
            P("dp", "mp"),
            P("dp", "mp"),
            P("dp", "mp"),
            P("dp", "mp"),
            P("dp", "mp"),
            P("dp", "mp"),
            P("dp"),
            P("dp", None, "mp"),
            P(("mp", "dp"), None),
            P(("mp", "dp")),
            P(("mp", "dp")),
            P("dp", "mp"),
            P("dp"),
            P("dp", "mp"),
            P("dp", "mp"),
            P("dp"),
        ),
        check_vma=False,
    )
```

time: 1930 us -> 747 us (0.39)
  waiting for transfers between devices: 1210 us -> 410 us
  blocking collectives: 445 us -> 0 us
  starting transfers between devices: 2.17 us -> 79.4 us
  other arithmetic: 56.3 us -> 76.7 us
    reduce_scatter x11 -> x0, waiting for transfers between devices: 791 us -> none  [the longest x1 92.5 us: per_device(): lax.psum_scatter(second_feed_gradients[2], 'dp', scatter_dimension=0, til...]
    ppermute x0 -> x93, waiting for transfers between devices: none -> 410 us  [swap(): return lax.ppermute(values, axis, [(i, i ^ mask) for i in range(size)])]
    all_gather x14 -> x0, blocking collectives: 348 us -> none  [the longest x1 34 us: fetch_convolution(): lax.all_gather(pointwise_out.astype(jnp.bfloat16), 'dp', axis=0, tiled=True)]
    psum x8 -> x0, waiting for transfers between devices: 194 us -> none  [branch_total(): return lax.psum(piece_terms.astype(jnp.bfloat16), 'mp').astype(jnp.float32)]
    unnamed x30 -> x0, waiting for transfers between devices: 131 us -> none
    all_gather x5 -> x0, waiting for transfers between devices: 95.5 us -> none  [the longest x1 49.5 us: fetch_second(): lax.all_gather(up_weight.astype(jnp.bfloat16), 'dp', axis=0, tiled=True)]
    ppermute x0 -> x93, starting transfers between devices: none -> 79.4 us  [swap(): return lax.ppermute(values, axis, [(i, i ^ mask) for i in range(size)])]
    unnamed x2 -> x0, blocking collectives: 54.5 us -> none
  transfers between devices with their start and end apart: 27 -> 93, of which waited for: 23 -> 51; matrix products, arithmetic and copies ran while one was open for 5% -> 18% of each run, Pallas kernels for 0% -> 0%
where the time goes in v1:
time: 747 us; the launch traced here: 736 us
  waiting for transfers between devices  410 us (55%)
  local copies, waits for them, and re-layouts  86.2 us (12%)
  matrix products  79.8 us (11%)
  starting transfers between devices  79.4 us (11%)
  other arithmetic  76.7 us (10%)
    ppermute x93, waiting for transfers between devices, swap(): return lax.ppermute(values, axis, [(i, i ^ mask) for i in range(size)])  410 us
    ppermute x93, starting transfers between devices, swap(): return lax.ppermute(values, axis, [(i, i ^ mask) for i in range(size)])  79.4 us
    dot_general x12, matrix products, matmul(): return jnp.dot(left_side, right_side, preferred_element_type=FLOAT)  26 us
    unnamed x440, local copies, waits for them, and re-layouts  25.7 us
    dot_general x18, matrix products, times_transposed(): lax.dot_general(left_side, right_side, (((1,), (1,)), ((), ())), preferre...  22 us
    concatenate x34, other arithmetic, spread(): values = jnp.concatenate([values, swap(values, axis, mask)], axis=0)  21.4 us
    dot_general x18, matrix products, outer_sum(): lax.dot_general(left_side, right_side, (((0,), (0,)), ((), ())), preferre...  19.6 us
  transfers between devices with their start and end apart: 93, of which 51 were waited for; matrix products, arithmetic and copies ran while one was open for 18% of the time, Pallas kernels for 0%

profile of v1, /device:TPU:0, one launch (start us, length us, event | category | flops | bytes accessed | tf_op | source)
XLA Modules:
  0.0 736.2 jit_solution(13718159695003962790)
XLA Ops:
  34.8 13.3 %collective-permute-done.3 = bf16[128,1024]{1,0:T(8,128)(2,1)} collective-permute-done((bf16[128,1024]{1,0:T(8,128)(2,1)}, bf16[128,1024]{1,0:T(8,128)(2,1)}, u32[]{:S(2)}, u32[]{:S(2)}) %collective-permute-start.3) | collective-permute-done | bytes 262176 | tf_op jit(solution)/shard_map/ppermute | solution.py:40
  52.2 13.0 %collective-permute-done.1 = f32[2,928]{1,0:T(2,128)S(1)} collective-permute-done((f32[2,928]{1,0:T(2,128)S(1)}, f32[2,928]{1,0:T(2,128)S(1)}, u32[]{:S(2)}, u32[]{:S(2)}) %collective-permute-start.1) | collective-permute-done | bytes 7456 | tf_op jit(solution)/shard_map/ppermute | solution.py:40
  70.0 11.7 %collective-permute-done.7 = bf16[256,1024]{1,0:T(8,128)(2,1)S(1)} collective-permute-done((bf16[256,1024]{1,0:T(8,128)(2,1)S(1)}, bf16[256,1024]{1,0:T(8,128)(2,1)S(1)}, u32[]{:S(2)}, u32[]{:S(2)}) %collective-permute-start.7) | collective-permute-done | bytes 524320 | tf_op jit(solution)/shard_map/ppermute | solution.py:40
  84.5 10.9 %collective-permute-done.5 = bf16[512,1024]{1,0:T(8,128)(2,1)S(1)} collective-permute-done((bf16[512,1024]{1,0:T(8,128)(2,1)S(1)}, bf16[512,1024]{1,0:T(8,128)(2,1)S(1)}, u32[]{:S(2)}, u32[]{:S(2)}) %collective-permute-start.5) | collective-permute-done | bytes 1048608 | tf_op jit(solution)/shard_map/ppermute | solution.py:40
  99.7 17.0 %collective-permute-done.8 = bf16[512,1024]{1,0:T(8,128)(2,1)S(1)} collective-permute-done((bf16[512,1024]{1,0:T(8,128)(2,1)S(1)}, bf16[512,1024]{1,0:T(8,128)(2,1)S(1)}, u32[]{:S(2)}, u32[]{:S(2)}) %collective-permute-start.8) | collective-permute-done | bytes 1048608 | tf_op jit(solution)/shard_map/ppermute | solution.py:40
  128.4 10.6 %collective-permute-done.14 = bf16[256,1280]{1,0:T(8,128)(2,1)} collective-permute-done((bf16[256,1280]{1,0:T(8,128)(2,1)}, bf16[256,1280]{1,0:T(8,128)(2,1)}, u32[]{:S(2)}, u32[]{:S(2)}) %collective-permute-start.14) | collective-permute-done | bytes 655392 | tf_op jit(solution)/shard_map/ppermute | solution.py:40
  151.3 20.7 %collective-permute-done.15 = bf16[512,1280]{1,0:T(8,128)(2,1)} collective-permute-done((bf16[512,1280]{1,0:T(8,128)(2,1)}, bf16[512,1280]{1,0:T(8,128)(2,1)}, u32[]{:S(2)}, u32[]{:S(2)}) %collective-permute-start.15) | collective-permute-done | bytes 1310752 | tf_op jit(solution)/shard_map/ppermute | solution.py:40
  185.3 9.7 %reshape.573 = f32[2,523776]{1,0:T(2,128)} reshape(f32[2,512,1023]{2,1,0:T(8,128)} %fusion.129) | data formatting | bytes 8380416 | tf_op jit(solution)/shard_map/reshape | solution.py:118
  202.4 10.0 %reshape.574 = f32[2,512,1022]{2,1,0:T(8,128)} reshape(f32[2,523264]{1,0:T(2,128)} %slice.621) | data formatting | bytes 8372224 | tf_op jit(solution)/shard_map/reshape | solution.py:120
  222.7 10.9 %collective-permute-done.20 = bf16[128,768]{1,0:T(8,128)(2,1)S(1)} collective-permute-done((bf16[128,768]{1,0:T(8,128)(2,1)S(1)}, bf16[128,768]{1,0:T(8,128)(2,1)S(1)}, u32[]{:S(2)}, u32[]{:S(2)}) %collective-permute-start.20) | collective-permute-done | bytes 196640 | tf_op jit(solution)/shard_map/ppermute | solution.py:40
  235.8 8.6 %collective-permute-done.21 = bf16[256,768]{1,0:T(8,128)(2,1)S(1)} collective-permute-done((bf16[256,768]{1,0:T(8,128)(2,1)S(1)}, bf16[256,768]{1,0:T(8,128)(2,1)S(1)}, u32[]{:S(2)}, u32[]{:S(2)}) %collective-permute-start.21) | collective-permute-done | bytes 393248 | tf_op jit(solution)/shard_map/ppermute | solution.py:40
  287.2 14.4 %collective-permute-done.30 = bf16[128,1024]{1,0:T(8,128)(2,1)S(1)} collective-permute-done((bf16[128,1024]{1,0:T(8,128)(2,1)S(1)}, bf16[128,1024]{1,0:T(8,128)(2,1)S(1)}, u32[]{:S(2)}, u32[]{:S(2)}) %collective-permute-start.30) | collective-permute-done | bytes 262176 | tf_op jit(solution)/shard_map/ppermute | solution.py:40
  306.1 12.9 %collective-permute-done.33 = bf16[128,1024]{1,0:T(8,128)(2,1)S(1)} collective-permute-done((bf16[128,1024]{1,0:T(8,128)(2,1)S(1)}, bf16[128,1024]{1,0:T(8,128)(2,1)S(1)}, u32[]{:S(2)}, u32[]{:S(2)}) %collective-permute-start.33) | collective-permute-done | bytes 262176 | tf_op jit(solution)/shard_map/ppermute | solution.py:40
  334.1 13.9 %collective-permute-done.32 = bf16[512,1024]{1,0:T(8,128)(2,1)S(1)} collective-permute-done((bf16[512,1024]{1,0:T(8,128)(2,1)S(1)}, bf16[512,1024]{1,0:T(8,128)(2,1)S(1)}, u32[]{:S(2)}, u32[]{:S(2)}) %collective-permute-start.32) | collective-permute-done | bytes 1048608 | tf_op jit(solution)/shard_map/ppermute | solution.py:40
  350.8 17.8 %collective-permute-done.35 = bf16[512,1024]{1,0:T(8,128)(2,1)S(1)} collective-permute-done((bf16[512,1024]{1,0:T(8,128)(2,1)S(1)}, bf16[512,1024]{1,0:T(8,128)(2,1)S(1)}, u32[]{:S(2)}, u32[]{:S(2)}) %collective-permute-start.35) | collective-permute-done | bytes 1048608 | tf_op jit(solution)/shard_map/ppermute | solution.py:40
  426.3 9.7 %collective-permute-done.87 = bf16[512,1024]{1,0:T(8,128)(2,1)S(1)} collective-permute-done((bf16[512,1024]{1,0:T(8,128)(2,1)S(1)}, bf16[512,1024]{1,0:T(8,128)(2,1)S(1)}, u32[]{:S(2)}, u32[]{:S(2)}) %collective-permute-start.87) | collective-permute-done | bytes 1048608 | tf_op jit(solution)/shard_map/ppermute | solution.py:40
  437.2 20.5 %collective-permute-done.90 = bf16[512,1024]{1,0:T(8,128)(2,1)S(1)} collective-permute-done((bf16[512,1024]{1,0:T(8,128)(2,1)S(1)}, bf16[512,1024]{1,0:T(8,128)(2,1)S(1)}, u32[]{:S(2)}, u32[]{:S(2)}) %collective-permute-start.90) | collective-permute-done | bytes 1048608 | tf_op jit(solution)/shard_map/ppermute | solution.py:40
  466.4 11.1 %collective-permute-done.91 = bf16[256,1024]{1,0:T(8,128)(2,1)S(1)} collective-permute-done((bf16[256,1024]{1,0:T(8,128)(2,1)S(1)}, bf16[256,1024]{1,0:T(8,128)(2,1)S(1)}, u32[]{:S(2)}, u32[]{:S(2)}) %collective-permute-start.91) | collective-permute-done | bytes 524320 | tf_op jit(solution)/shard_map/ppermute | solution.py:40
  483.1 8.4 %collective-permute-done.48 = f32[2,256]{1,0:T(2,128)S(1)} collective-permute-done((f32[2,256]{1,0:T(2,128)S(1)}, f32[2,256]{1,0:T(2,128)S(1)}, u32[]{:S(2)}, u32[]{:S(2)}) %collective-permute-start.48) | collective-permute-done | bytes 2080 | tf_op jit(solution)/shard_map/ppermute | solution.py:40
  610.7 8.9 %collective-permute-done.74 = bf16[128,768]{1,0:T(8,128)(2,1)S(1)} collective-permute-done((bf16[128,768]{1,0:T(8,128)(2,1)S(1)}, bf16[128,768]{1,0:T(8,128)(2,1)S(1)}, u32[]{:S(2)}, u32[]{:S(2)}) %collective-permute-start.74) | collective-permute-done | bytes 196640 | tf_op jit(solution)/shard_map/ppermute | solution.py:40
  641.2 35.3 %collective-permute-done.61 = f32[4,864]{1,0:T(4,128)S(1)} collective-permute-done((f32[4,864]{1,0:T(4,128)S(1)}, f32[4,864]{1,0:T(4,128)S(1)}, u32[]{:S(2)}, u32[]{:S(2)}) %collective-permute-start.61) | collective-permute-done | bytes 13856 | tf_op jit(solution)/shard_map/ppermute | solution.py:40
  697.0 10.1 %collective-permute-done.67 = bf16[256,1024]{1,0:T(8,128)(2,1)S(1)} collective-permute-done((bf16[256,1024]{1,0:T(8,128)(2,1)S(1)}, bf16[256,1024]{1,0:T(8,128)(2,1)S(1)}, u32[]{:S(2)}, u32[]{:S(2)}) %collective-permute-start.67) | collective-permute-done | bytes 524320 | tf_op jit(solution)/shard_map/ppermute | solution.py:40
  709.0 13.3 %collective-permute-done.70 = bf16[256,1024]{1,0:T(8,128)(2,1)S(1)} collective-permute-done((bf16[256,1024]{1,0:T(8,128)(2,1)S(1)}, bf16[256,1024]{1,0:T(8,128)(2,1)S(1)}, u32[]{:S(2)}, u32[]{:S(2)}) %collective-permute-start.70) | collective-permute-done | bytes 524320 | tf_op jit(solution)/shard_map/ppermute | solution.py:40
  725.4 9.8 %collective-permute-done.71 = bf16[128,1024]{1,0:T(8,128)(2,1)S(1)} collective-permute-done((bf16[128,1024]{1,0:T(8,128)(2,1)S(1)}, bf16[128,1024]{1,0:T(8,128)(2,1)S(1)}, u32[]{:S(2)}, u32[]{:S(2)}) %collective-permute-start.71) | collective-permute-done | bytes 262176 | tf_op jit(solution)/shard_map/ppermute | solution.py:40
  (921 shorter events, 409.2 us)
Async XLA Ops:
  8.2 41.7 %collective-permute-start = (f32[1,928]{1,0:T(1,128)S(1)}, f32[1,928]{1,0:T(1,128)S(1)}, u32[]{:S(2)}, u32[]{:S(2)}) collective-permute-start(f32[1,928]{1,0:T(1,128)S(1)} %bitcast.162), channel_id=1, source_target_pairs={{0,16},{4,20},{8,24},{12,28},{16,0},{20,4},{24,8},{28,12},{1,17},{... | collective-permute-start | bytes 11144 | tf_op jit(solution)/shard_map/ppermute | solution.py:40
  14.1 52.8 %collective-permute-start.6 = (bf16[128,1024]{1,0:T(8,128)(2,1)}, bf16[128,1024]{1,0:T(8,128)(2,1)}, u32[]{:S(2)}, u32[]{:S(2)}) collective-permute-start(bf16[128,1024]{1,0:T(8,128)(2,1)} %convert_element_type.457), channel_id=1, source_target_pairs={{0,16},{4,20},{8,24},{12,28},{16,0},{20,4},{24,8},{28,12},{1,17},{... | collective-permute-start | bytes 786440 | tf_op jit(solution)/shard_map/ppermute | solution.py:40
  15.9 32.2 %collective-permute-start.3 = (bf16[128,1024]{1,0:T(8,128)(2,1)}, bf16[128,1024]{1,0:T(8,128)(2,1)}, u32[]{:S(2)}, u32[]{:S(2)}) collective-permute-start(bf16[128,1024]{1,0:T(8,128)(2,1)} %convert_element_type.455), channel_id=1, source_target_pairs={{0,16},{4,20},{8,24},{12,28},{16,0},{20,4},{24,8},{28,12},{1,17},{... | collective-permute-start | bytes 786440 | tf_op jit(solution)/shard_map/ppermute | solution.py:40
  20.7 99.0 %collective-permute-start.13 = (bf16[128,1280]{1,0:T(8,128)(2,1)S(1)}, bf16[128,1280]{1,0:T(8,128)(2,1)}, u32[]{:S(2)}, u32[]{:S(2)}) collective-permute-start(bf16[128,1280]{1,0:T(8,128)(2,1)S(1)} %convert_dynamic-update-slice_fusion), channel_id=1, source_target_pairs={{0,16},{4,20},{8,24},{12,28},{16,0},{20,4},{24,8},{28,12},{1,17},{... | collective-permute-start | bytes 983048 | tf_op jit(solution)/shard_map/ppermute | solution.py:40
  69.3 26.1 %collective-permute-start.5 = (bf16[512,1024]{1,0:T(8,128)(2,1)S(1)}, bf16[512,1024]{1,0:T(8,128)(2,1)S(1)}, u32[]{:S(2)}, u32[]{:S(2)}) collective-permute-start(bf16[512,1024]{1,0:T(8,128)(2,1)S(1)} %pad_maximum_fusion.9), channel_id=1, source_target_pairs={{0,4},{4,0},{8,12},{12,8},{16,20},{20,16},{24,28},{28,24},{1,5},{5... | collective-permute-start | bytes 3145736 | tf_op jit(solution)/shard_map/ppermute | solution.py:40
  83.0 33.8 %collective-permute-start.8 = (bf16[512,1024]{1,0:T(8,128)(2,1)S(1)}, bf16[512,1024]{1,0:T(8,128)(2,1)S(1)}, u32[]{:S(2)}, u32[]{:S(2)}) collective-permute-start(bf16[512,1024]{1,0:T(8,128)(2,1)S(1)} %pad_maximum_fusion.10), channel_id=1, source_target_pairs={{0,4},{4,0},{8,12},{12,8},{16,20},{20,16},{24,28},{28,24},{1,5},{5... | collective-permute-start | bytes 3145736 | tf_op jit(solution)/shard_map/ppermute | solution.py:40
  141.3 30.7 %collective-permute-start.15 = (bf16[512,1280]{1,0:T(8,128)(2,1)}, bf16[512,1280]{1,0:T(8,128)(2,1)}, u32[]{:S(2)}, u32[]{:S(2)}) collective-permute-start(bf16[512,1280]{1,0:T(8,128)(2,1)} %pad_maximum_fusion.8), channel_id=1, source_target_pairs={{0,4},{4,0},{8,12},{12,8},{16,20},{20,16},{24,28},{28,24},{1,5},{5... | collective-permute-start | bytes 3932168 | tf_op jit(solution)/shard_map/ppermute | solution.py:40
  151.3 27.4 %collective-permute-start.12 = (bf16[256,1024]{1,0:T(8,128)(2,1)S(1)}, bf16[256,1024]{1,0:T(8,128)(2,1)S(1)}, u32[]{:S(2)}, u32[]{:S(2)}) collective-permute-start(bf16[256,1024]{1,0:T(8,128)(2,1)S(1)} %pad_maximum_fusion.31), channel_id=1, source_target_pairs={{0,1},{1,0},{2,3},{3,2},{4,5},{5,4},{6,7},{7,6},{8,9},{9,8},{10,11... | collective-permute-start | bytes 1572872 | tf_op jit(solution)/shard_map/ppermute | solution.py:40
  301.6 20.2 %collective-permute-start.31 = (bf16[256,1024]{1,0:T(8,128)(2,1)S(1)}, bf16[256,1024]{1,0:T(8,128)(2,1)S(1)}, u32[]{:S(2)}, u32[]{:S(2)}) collective-permute-start(bf16[256,1024]{1,0:T(8,128)(2,1)S(1)} %pad_maximum_fusion.34), channel_id=1, source_target_pairs={{0,8},{4,12},{8,0},{12,4},{16,24},{20,28},{24,16},{28,20},{1,9},{5... | collective-permute-start | bytes 1572872 | tf_op jit(solution)/shard_map/ppermute | solution.py:40
  321.9 26.2 %collective-permute-start.32 = (bf16[512,1024]{1,0:T(8,128)(2,1)S(1)}, bf16[512,1024]{1,0:T(8,128)(2,1)S(1)}, u32[]{:S(2)}, u32[]{:S(2)}) collective-permute-start(bf16[512,1024]{1,0:T(8,128)(2,1)S(1)} %pad_maximum_fusion.15), channel_id=1, source_target_pairs={{0,4},{4,0},{8,12},{12,8},{16,20},{20,16},{24,28},{28,24},{1,5},{5... | collective-permute-start | bytes 3145736 | tf_op jit(solution)/shard_map/ppermute | solution.py:40
  333.4 35.2 %collective-permute-start.35 = (bf16[512,1024]{1,0:T(8,128)(2,1)S(1)}, bf16[512,1024]{1,0:T(8,128)(2,1)S(1)}, u32[]{:S(2)}, u32[]{:S(2)}) collective-permute-start(bf16[512,1024]{1,0:T(8,128)(2,1)S(1)} %pad_maximum_fusion.16), channel_id=1, source_target_pairs={{0,4},{4,0},{8,12},{12,8},{16,20},{20,16},{24,28},{28,24},{1,5},{5... | collective-permute-start | bytes 3145736 | tf_op jit(solution)/shard_map/ppermute | solution.py:40
  410.0 26.1 %collective-permute-start.87 = (bf16[512,1024]{1,0:T(8,128)(2,1)S(1)}, bf16[512,1024]{1,0:T(8,128)(2,1)S(1)}, u32[]{:S(2)}, u32[]{:S(2)}) collective-permute-start(bf16[512,1024]{1,0:T(8,128)(2,1)S(1)} %convolution_convert_fusion.1), channel_id=1, source_target_pairs={{0,4},{4,0},{8,12},{12,8},{16,20},{20,16},{24,28},{28,24},{1,5},{5... | collective-permute-start | bytes 3145736 | tf_op jit(solution)/shard_map/ppermute | solution.py:40
  410.5 47.2 %collective-permute-start.90 = (bf16[512,1024]{1,0:T(8,128)(2,1)S(1)}, bf16[512,1024]{1,0:T(8,128)(2,1)S(1)}, u32[]{:S(2)}, u32[]{:S(2)}) collective-permute-start(bf16[512,1024]{1,0:T(8,128)(2,1)S(1)} %convolution_convert_fusion), channel_id=1, source_target_pairs={{0,4},{4,0},{8,12},{12,8},{16,20},{20,16},{24,28},{28,24},{1,5},{5... | collective-permute-start | bytes 3145736 | tf_op jit(solution)/shard_map/ppermute | solution.py:40
  426.2 32.7 %collective-permute-start.45 = (bf16[256,1024]{1,0:T(8,128)(2,1)S(1)}, bf16[256,1024]{1,0:T(8,128)(2,1)S(1)}, u32[]{:S(2)}, u32[]{:S(2)}) collective-permute-start(bf16[256,1024]{1,0:T(8,128)(2,1)S(1)} %pad_maximum_fusion.38), channel_id=1, source_target_pairs={{0,1},{1,0},{2,3},{3,2},{4,5},{5,4},{6,7},{7,6},{8,9},{9,8},{10,11... | collective-permute-start | bytes 1572872 | tf_op jit(solution)/shard_map/ppermute | solution.py:40
  436.9 25.0 %collective-permute-start.88 = (bf16[256,1024]{1,0:T(8,128)(2,1)S(1)}, bf16[256,1024]{1,0:T(8,128)(2,1)S(1)}, u32[]{:S(2)}, u32[]{:S(2)}) collective-permute-start(bf16[256,1024]{1,0:T(8,128)(2,1)S(1)} %slice.955), channel_id=1, source_target_pairs={{0,8},{4,12},{8,0},{12,4},{16,24},{20,28},{24,16},{28,20},{1,9},{5... | collective-permute-start | bytes 1572872 | tf_op jit(solution)/shard_map/ppermute | solution.py:40
  462.8 37.4 %collective-permute-start.89 = (bf16[128,1024]{1,0:T(8,128)(2,1)}, bf16[128,1024]{1,0:T(8,128)(2,1)S(1)}, u32[]{:S(2)}, u32[]{:S(2)}) collective-permute-start(bf16[128,1024]{1,0:T(8,128)(2,1)} %slice.960), channel_id=1, source_target_pairs={{0,16},{4,20},{8,24},{12,28},{16,0},{20,4},{24,8},{28,12},{1,17},{... | collective-permute-start | bytes 786440 | tf_op jit(solution)/shard_map/ppermute | solution.py:40
  478.5 26.1 %collective-permute-start.92 = (bf16[128,1024]{1,0:T(8,128)(2,1)}, bf16[128,1024]{1,0:T(8,128)(2,1)}, u32[]{:S(2)}, u32[]{:S(2)}) collective-permute-start(bf16[128,1024]{1,0:T(8,128)(2,1)} %slice.959), channel_id=1, source_target_pairs={{0,16},{4,20},{8,24},{12,28},{16,0},{20,4},{24,8},{28,12},{1,17},{... | collective-permute-start | bytes 786440 | tf_op jit(solution)/shard_map/ppermute | solution.py:40
  482.6 23.8 %collective-permute-start.84 = (bf16[512,256]{1,0:T(8,128)(2,1)}, bf16[512,256]{1,0:T(8,128)(2,1)}, u32[]{:S(2)}, u32[]{:S(2)}) collective-permute-start(bf16[512,256]{1,0:T(8,128)(2,1)} %convolution_convert_fusion.15), channel_id=1, source_target_pairs={{0,4},{4,0},{8,12},{12,8},{16,20},{20,16},{24,28},{28,24},{1,5},{5... | collective-permute-start | bytes 786440 | tf_op jit(solution)/shard_map/ppermute | solution.py:40
  575.9 21.6 %collective-permute-start.72 = (bf16[512,768]{1,0:T(8,128)(2,1)S(1)}, bf16[512,768]{1,0:T(8,128)(2,1)S(1)}, u32[]{:S(2)}, u32[]{:S(2)}) collective-permute-start(bf16[512,768]{1,0:T(8,128)(2,1)S(1)} %convolution_convert_fusion.4), channel_id=1, source_target_pairs={{0,4},{4,0},{8,12},{12,8},{16,20},{20,16},{24,28},{28,24},{1,5},{5... | collective-permute-start | bytes 2359304 | tf_op jit(solution)/shard_map/ppermute | solution.py:40
  627.4 62.2 %collective-permute-start.66 = (bf16[512,1024]{1,0:T(8,128)(2,1)}, bf16[512,1024]{1,0:T(8,128)(2,1)}, u32[]{:S(2)}, u32[]{:S(2)}) collective-permute-start(bf16[512,1024]{1,0:T(8,128)(2,1)} %convolution_convert_fusion.3), channel_id=1, source_target_pairs={{0,4},{4,0},{8,12},{12,8},{16,20},{20,16},{24,28},{28,24},{1,5},{5... | collective-permute-start | bytes 3145736 | tf_op jit(solution)/shard_map/ppermute | solution.py:40
  634.3 58.7 %collective-permute-start.69 = (bf16[512,1024]{1,0:T(8,128)(2,1)}, bf16[512,1024]{1,0:T(8,128)(2,1)}, u32[]{:S(2)}, u32[]{:S(2)}) collective-permute-start(bf16[512,1024]{1,0:T(8,128)(2,1)} %convolution_convert_fusion.2), channel_id=1, source_target_pairs={{0,4},{4,0},{8,12},{12,8},{16,20},{20,16},{24,28},{28,24},{1,5},{5... | collective-permute-start | bytes 3145736 | tf_op jit(solution)/shard_map/ppermute | solution.py:40
  640.9 35.6 %collective-permute-start.61 = (f32[4,864]{1,0:T(4,128)S(1)}, f32[4,864]{1,0:T(4,128)S(1)}, u32[]{:S(2)}, u32[]{:S(2)}) collective-permute-start(f32[4,864]{1,0:T(4,128)S(1)} %pad_maximum_fusion.58), channel_id=1, source_target_pairs={{0,4},{4,0},{8,12},{12,8},{16,20},{20,16},{24,28},{28,24},{1,5},{5... | collective-permute-start | bytes 41480 | tf_op jit(solution)/shard_map/ppermute | solution.py:40
  695.1 27.2 %collective-permute-start.70 = (bf16[256,1024]{1,0:T(8,128)(2,1)S(1)}, bf16[256,1024]{1,0:T(8,128)(2,1)S(1)}, u32[]{:S(2)}, u32[]{:S(2)}) collective-permute-start(bf16[256,1024]{1,0:T(8,128)(2,1)S(1)} %slice.956), channel_id=1, source_target_pairs={{0,8},{4,12},{8,0},{12,4},{16,24},{20,28},{24,16},{28,20},{1,9},{5... | collective-permute-start | bytes 1572872 | tf_op jit(solution)/shard_map/ppermute | solution.py:40
  696.9 25.6 %collective-permute-start.60 = (bf16[256,1024]{1,0:T(8,128)(2,1)S(1)}, bf16[256,1024]{1,0:T(8,128)(2,1)S(1)}, u32[]{:S(2)}, u32[]{:S(2)}) collective-permute-start(bf16[256,1024]{1,0:T(8,128)(2,1)S(1)} %pad_maximum_fusion.41), channel_id=1, source_target_pairs={{0,1},{1,0},{2,3},{3,2},{4,5},{5,4},{6,7},{7,6},{8,9},{9,8},{10,11... | collective-permute-start | bytes 1572872 | tf_op jit(solution)/shard_map/ppermute | solution.py:40
  (283 other events, 3648.8 us)

commit v2 on v1

v2 whole, which is shorter than its diff:
```python
import functools
import math

import jax
import jax.numpy as jnp
from jax import lax
from jax.experimental import pallas as pl
from jax.experimental.pallas import tpu as pltpu
from jax.sharding import PartitionSpec as P

EPSILON = 1e-05
LOW = jnp.bfloat16
FLOAT = jnp.float32


def matmul(left_side, right_side):
    return jnp.dot(left_side, right_side, preferred_element_type=FLOAT)


def times_transposed(left_side, right_side):
    return lax.dot_general(
        left_side, right_side, (((1,), (1,)), ((), ())), preferred_element_type=FLOAT
    )


def outer_sum(left_side, right_side):
    return lax.dot_general(
        left_side, right_side, (((0,), (0,)), ((), ())), preferred_element_type=FLOAT
    )


def reversed_bits(places, size):
    outcome = places * 0
    mask, back = size // 2, 1
    while mask:
        outcome = outcome + ((places // back) % 2) * mask
        mask, back = mask // 2, back * 2
    return outcome


def swap(values, axis, mask):
    size = lax.axis_size(axis)
    return lax.ppermute(values, axis, [(i, i ^ mask) for i in range(size)])


def after(values, *tokens):
    return lax.optimization_barrier((values, tokens))[0] if tokens else values


class Links:
    def __init__(self, depth, apart=False):
        self.depth, self.apart, self.queues = depth, apart, {}

    def swap(self, values, mask):
        queue, depth = self.queues.setdefault(self.apart and mask == 1, []), self.depth
        if len(queue) >= depth:
            values = after(values, *queue[-2 * depth : len(queue) + 1 - depth])
        queue.append(swap(values, "dp", mask))
        return queue[-1]


ORDER = (4, 1, 2, 3, 5, 6, 7)


class Spread:
    def __init__(self, links, own):
        self.links, self.mask = links, lax.axis_size("dp") // 2
        while self.mask > 4:
            own = jnp.concatenate([own, links.swap(own, self.mask)], axis=0)
            self.mask //= 2
        self.blocks = [own] + [None] * (2 * self.mask - 1)

    def go(self, places, *tokens):
        for p in places:
            if p < len(self.blocks):
                top = 1 << (p.bit_length() - 1)
                self.blocks[p] = self.links.swap(
                    after(self.blocks[p - top], *tokens), self.mask // top
                )


def spread(values, axis):
    mask = lax.axis_size(axis) // 2
    while mask:
        values = jnp.concatenate([values, swap(values, axis, mask)], axis=0)
        mask //= 2
    return values


def collect(values, axis, wire, mask=1):
    while mask < lax.axis_size(axis):
        half = values.shape[0] // 2
        values = values[:half] + swap(values[half:].astype(wire), axis, mask).astype(FLOAT)
        mask *= 2
    return values


def total_over(values, axis):
    mask = 1
    while mask < lax.axis_size(axis):
        values = values + swap(values, axis, mask)
        mask *= 2
    return values


def total_hops(values, axis):
    arrivals, mask = [], lax.axis_size(axis) // 2
    while mask:
        arrivals.append(swap(values, axis, mask))
        values = values + arrivals[-1]
        mask //= 2
    return values, arrivals


class WeightSum:
    def __init__(self, *pairs):
        self.pairs, self.mask = pairs, 0

    def advance(self, *tokens, links=None):
        if not self.mask:
            half = self.pairs[0][0].shape[1] // 2
            upper = [outer_sum(left[:, half:], right).astype(LOW) for left, right in self.pairs]
            lower = [outer_sum(left[:, :half], right) for left, right in self.pairs]
            self.upper, self.kept = jnp.concatenate(upper, axis=1), jnp.concatenate(lower, axis=1)
            self.upper, self.mask = after(self.upper, *tokens), 1
        else:
            total = self.kept + after(self.sent, *tokens).astype(FLOAT)
            half = total.shape[0] // 2
            self.upper, self.kept = total[half:].astype(LOW), total[:half]
        if links is None:
            self.sent = swap(self.upper, "dp", self.mask)
        else:
            self.sent = links.swap(self.upper, self.mask)
        self.mask *= 2

    def rest(self, *tokens):
        while self.mask < lax.axis_size("dp"):
            self.advance(*tokens)


def position_table(places, row_count, feature_count):
    rates = jnp.exp(
        jnp.arange(0, feature_count, 2).astype(FLOAT) * (-math.log(10000.0) / feature_count)
    )
    stride = 32
    count = places.shape[0] // stride
    coarse = (row_count - 1 - stride * places[:count]).astype(FLOAT)[:, None] * rates[None, :]
    fine = -places[:stride].astype(FLOAT)[:, None] * rates[None, :]
    coarse_sin, coarse_cos = jnp.sin(coarse)[:, None], jnp.cos(coarse)[:, None]
    fine_sin, fine_cos = jnp.sin(fine)[None], jnp.cos(fine)[None]
    sines = coarse_sin * fine_cos + coarse_cos * fine_sin
    cosines = coarse_cos * fine_cos - coarse_sin * fine_sin
    table = jnp.concatenate([sines, cosines], axis=2).astype(LOW)
    return table.reshape(places.shape[0], feature_count)


def fixed_reversed(place, size):
    outcome, mask = 0, size // 2
    while mask:
        outcome, place, mask = outcome + (place % 2) * mask, place // 2, mask // 2
    return outcome


def relative_window(position_ref, first, row_block, columns):
    row_count = position_ref.shape[0] // 2
    start = pl.multiple_of(row_count - row_block - first, row_block)
    return position_ref.at[pl.ds(start, row_count + row_block), columns]


def in_smem():
    return pl.BlockSpec(memory_space=pltpu.SMEM)


def in_vmem():
    return pl.BlockSpec(memory_space=pltpu.VMEM)


def anywhere():
    return pl.BlockSpec(memory_space=pl.ANY)


def call(kernel, outs, scratch, flops, *operands):
    places = dict(smem=in_smem, vmem=in_vmem, any=anywhere)
    moved = sum(array.size * array.dtype.itemsize for _, array in operands)
    moved += sum(math.prod(shape) * jnp.dtype(kind).itemsize for shape, kind in outs)
    return pl.pallas_call(
        kernel,
        out_shape=tuple(jax.ShapeDtypeStruct(shape, kind) for shape, kind in outs),
        in_specs=[places[place]() for place, _ in operands],
        out_specs=(in_vmem(),) * len(outs),
        scratch_shapes=scratch,
        compiler_params=pltpu.CompilerParams(vmem_limit_bytes=(50 if scratch else 6) * 2**20),
        cost_estimate=pl.CostEstimate(flops=flops, bytes_accessed=0, transcendentals=0),
    )(*[array for _, array in operands])


class Copies:
    def __init__(self, semaphores):
        self.semaphores, self.count = semaphores, 0

    def start(self, source, target):
        copy = pltpu.make_async_copy(source, target, self.semaphores.at[self.count])
        copy.start()
        self.count += 1
        return copy

    def stack(self, sources, target, columns=None):
        copies, block = [], target.shape[0] // len(sources)
        for p, source in enumerate(sources):
            if columns is not None:
                source = source.at[:, columns]
            copies.append(self.start(source, target.at[pl.ds(p * block, block)]))
        return copies

    def weight(self, sources, owners_ref, target, columns):
        if len(sources) > 1:
            return self.stack(sources, target, columns)
        copies, blocks = [], owners_ref.shape[0]
        block = target.shape[0] // blocks
        for p in range(blocks):
            first = pl.multiple_of(owners_ref[p] * block, block)
            copies.append(
                self.start(
                    sources[0].at[pl.ds(first, block), columns],
                    target.at[pl.ds(p * block, block)],
                )
            )
        return copies


def wait(copies):
    for copy in copies:
        copy.wait()


def weight_copies(sources, owners):
    return len(sources) if len(sources) > 1 else owners.shape[0]


TILE = 256


def write_parts(hi_ref, next_ref, own_ref, columns, product):
    half, own = hi_ref.shape[0], own_ref.shape[0]
    hi_ref[:, columns] = product[half:].astype(LOW)
    next_ref[:, columns] = product[own:half].astype(LOW)
    own_ref[:, columns] = product[:own]


def tiles(count):
    def loop(body):
        @pl.loop(0, count // TILE)
        def _(t):
            body(pl.ds(pl.multiple_of(t * TILE, TILE), TILE))

    return loop


def ffn_forward_kernel(*refs, pieces, weights, up_columns, down_columns):
    owners_ref, refs = refs[0], refs[1:]
    row_refs, refs = refs[:pieces], refs[pieces:]
    up_refs, refs = refs[:weights], refs[weights:]
    down_refs, refs = refs[:weights], refs[weights:]
    rows_ref, before_ref, active_ref, hi_ref, next_ref, own_ref, up, down, semaphores = refs
    copies = Copies(semaphores)
    rows_copies = copies.stack(row_refs, rows_ref)
    up_copies = copies.weight(up_refs, owners_ref, up, up_columns)
    down_copies = copies.weight(down_refs, owners_ref, down, down_columns)
    wait(rows_copies + up_copies)

    @tiles(up.shape[1])
    def _(columns):
        before = matmul(rows_ref[...], up[:, columns])
        before_ref[:, columns] = before.astype(LOW)
        active_ref[:, columns] = (before * jax.nn.sigmoid(before)).astype(LOW)

    wait(down_copies)

    @tiles(down.shape[0])
    def _(features):
        write_parts(
            hi_ref, next_ref, own_ref, features, times_transposed(active_ref[...], down[features, :])
        )


def ffn_backward_kernel(*refs, pieces, weights, up_columns, down_columns, gains):
    owners_ref, refs = refs[0], refs[1:]
    if gains:
        hat_ref, gain_grad_ref, refs = refs[-10], refs[-4], refs[:-10] + refs[-9:-4] + refs[-3:]
    row_refs, refs = refs[:pieces], refs[pieces:]
    up_refs, refs = refs[:weights], refs[weights:]
    down_refs, refs = refs[:weights], refs[weights:]
    before_ref, rows_ref, grad_ref, hi_ref, next_ref, own_ref, up, down, semaphores = refs
    copies = Copies(semaphores)
    rows_copies = copies.stack(row_refs, rows_ref)
    down_copies = copies.weight(down_refs, owners_ref, down, down_columns)
    up_copies = copies.weight(up_refs, owners_ref, up, up_columns)
    wait(rows_copies + down_copies)

    @tiles(down.shape[1])
    def _(columns):
        before = before_ref[:, columns].astype(FLOAT)
        squashed = jax.nn.sigmoid(before)
        grad = matmul(rows_ref[...], down[:, columns])
        grad_ref[:, columns] = (grad * squashed * (1.0 + before * (1.0 - squashed))).astype(LOW)

    wait(up_copies)

    @tiles(up.shape[0])
    def _(features):
        product = times_transposed(grad_ref[...], up[features, :])
        write_parts(hi_ref, next_ref, own_ref, features, product)
        if gains:
            gain_grad_ref[:, features] = jnp.sum(
                product * hat_ref[:, features].astype(FLOAT), axis=0, keepdims=True
            )


def row_parts(rows, features):
    return [
        ((rows // 2, features), LOW), ((rows // 4, features), LOW), ((rows // 4, features), FLOAT)
    ]


def ffn_call(
    kernel, owners, rows, ups, downs, up_columns, down_columns, before=None, hat=None
):
    row_count = len(rows) * rows[0].shape[0]
    features = rows[0].shape[1]
    hidden = up_columns.stop - up_columns.start
    outs = [((row_count, features), LOW)]
    outs += [((row_count, hidden), LOW)] * (2 if before is None else 1)
    count = len(rows) + 2 * weight_copies(ups, owners)
    operands = [("smem", owners)]
    operands += [("any", array) for array in list(rows) + list(ups) + list(downs)]
    if before is not None:
        operands.append(("vmem", before))
        kernel = functools.partial(kernel, gains=hat is not None)
    outs += row_parts(row_count, features)
    if hat is not None:
        operands.append(("vmem", hat))
        outs.append(((1, features), FLOAT))
    return call(
        functools.partial(
            kernel, pieces=len(rows), weights=len(ups), up_columns=up_columns,
            down_columns=down_columns,
        ),
        outs,
        [
            pltpu.VMEM((features, hidden), LOW),
            pltpu.VMEM((features, hidden), LOW),
            pltpu.SemaphoreType.DMA((count,)),
        ],
        4 * row_count * features * hidden,
        *operands,
    )


def segment_of(lengths_ref, places):
    bound, segment = 0, jnp.zeros(places.shape, jnp.int32)
    for s in range(lengths_ref.shape[1]):
        bound = bound + lengths_ref[0, s]
        segment = segment + (places >= bound).astype(jnp.int32)
    return segment


def block_firsts(place_ref, blocks, row_block):
    place = place_ref[0]
    return [
        pl.multiple_of((place ^ fixed_reversed(q, blocks)) * row_block, row_block)
        for q in range(blocks)
    ]


def attention_forward_kernel(*refs, pieces, weights):
    place_ref, lengths_ref, owners_ref, content_ref, shift_ref = refs[:5]
    refs = refs[5:]
    row_refs, refs = refs[:pieces], refs[pieces:]
    weight_refs, refs = refs[:weights], refs[weights:]
    (
        table_ref,
        rows_ref, mixed_ref, prob_ref, content_rows_ref, position_rows_ref, key_ref, value_ref,
        position_ref, hi_ref, next_ref, own_ref,
        weight, table, qkv, semaphores,
    ) = refs
    row_count, heads = mixed_ref.shape
    head_count, head_size = content_ref.shape
    row_block = row_count // pieces
    window = row_count + row_block
    copies = Copies(semaphores)
    rows_copies = copies.stack(row_refs, rows_ref)
    everything = slice(0, weight.shape[1])
    weight_copies_ = copies.weight(weight_refs, owners_ref, weight, everything)
    table_copy = copies.start(table_ref, table)
    firsts = block_firsts(place_ref, pieces, row_block)
    wait(rows_copies + weight_copies_)

    @tiles(3 * heads)
    def _(columns):
        qkv[:, columns] = matmul(rows_ref[...], weight[:, columns])

    table_copy.wait()

    @tiles(table.shape[0])
    def _(places):
        position_ref[places, :] = matmul(
            table[places, :], weight[:, 3 * heads : 4 * heads]
        ).astype(LOW)

    for q in range(pieces):
        rows = pl.ds(q * row_block, row_block)
        key_ref[pl.ds(firsts[q], row_block), :] = qkv[rows, heads : 2 * heads].astype(LOW)
        value_ref[pl.ds(firsts[q], row_block), :] = qkv[rows, 2 * heads :].astype(LOW)

    along = lax.broadcasted_iota(jnp.int32, (1, row_count), 1)
    column_segment = segment_of(lengths_ref, along)
    for q in range(pieces):
        rows = pl.ds(q * row_block, row_block)
        down = lax.broadcasted_iota(jnp.int32, (row_block, 1), 0) + firsts[q]
        matching = segment_of(lengths_ref, down) == column_segment
        for h in range(head_count):
            columns = slice(h * head_size, (h + 1) * head_size)
            query = qkv[rows, columns]
            with_content = (query + content_ref[h : h + 1, :]).astype(LOW)
            with_position = (query + shift_ref[h : h + 1, :]).astype(LOW)
            content_rows_ref[rows, columns] = with_content
            position_rows_ref[rows, columns] = with_position
            direct = times_transposed(with_content, key_ref[:, columns])
            relative = relative_window(position_ref, firsts[q], row_block, columns)[...]
            broad = times_transposed(with_position, relative)
            broad = pltpu.roll(
                broad, window - (row_block - 1), axis=1, stride=1, stride_axis=0
            )
            scores = (direct + broad[:, :row_count]) * head_size ** (-0.5)
            scores = jnp.where(matching, scores, -1e30)
            exponent = jnp.exp(scores - jnp.max(scores, axis=1, keepdims=True))
            prob = (exponent / jnp.sum(exponent, axis=1, keepdims=True)).astype(LOW)
            prob_ref[h, rows, :] = prob
            mixed_ref[rows, columns] = matmul(prob, value_ref[:, columns]).astype(LOW)

    @tiles(weight.shape[0])
    def _(features):
        write_parts(
            hi_ref, next_ref, own_ref, features,
            times_transposed(mixed_ref[...], weight[features, 4 * heads : 5 * heads]),
        )


def attention_forward(place, lengths, owners, rows, weights, table, content_bias, position_bias):
    row_count, features = len(rows) * rows[0].shape[0], rows[0].shape[1]
    head_count, head_size = content_bias.shape
    heads = head_count * head_size
    row_array = ((row_count, heads), LOW)
    return call(
        functools.partial(attention_forward_kernel, pieces=len(rows), weights=len(weights)),
        [
            ((row_count, features), LOW), row_array,
            ((head_count, row_count, row_count), LOW),
            row_array, row_array, row_array, row_array,
            ((2 * row_count, heads), LOW),
        ]
        + row_parts(row_count, features),
        [
            pltpu.VMEM((features, 5 * heads), LOW),
            pltpu.VMEM(table.shape, LOW),
            pltpu.VMEM((row_count, 3 * heads), FLOAT),
            pltpu.SemaphoreType.DMA((len(rows) + weight_copies(weights, owners) + 1,)),
        ],
        12 * row_count * features * heads + 9 * heads * row_count**2,
        ("smem", place), ("smem", lengths), ("smem", owners),
        ("vmem", content_bias), ("vmem", position_bias),
        *[("any", array) for array in list(rows) + list(weights) + [table]],
    )


def attention_backward_kernel(*refs, pieces, weights, head_count):
    place_ref, owners_ref, refs = refs[0], refs[1], refs[2:]
    row_refs, refs = refs[:pieces], refs[pieces:]
    weight_refs, refs = refs[:weights], refs[weights:]
    (
        position_ref, prob_ref, content_rows_ref, position_rows_ref, key_ref, value_ref,
        rows_ref, qkv_grad_ref, position_grad_ref, bias_grad_ref, hi_ref, next_ref, own_ref,
        weight, mixed_grad_ref, key_sum, value_sum, position_sum, semaphores,
    ) = refs
    row_count, heads = mixed_grad_ref.shape
    head_size = heads // head_count
    row_block = row_count // pieces
    scale = head_size ** (-0.5)
    copies = Copies(semaphores)
    rows_copies = copies.stack(row_refs, rows_ref)
    everything = slice(0, weight.shape[1])
    weight_copies_ = copies.weight(weight_refs, owners_ref, weight, everything)
    firsts = block_firsts(place_ref, pieces, row_block)
    key_sum[...] = jnp.zeros_like(key_sum)
    value_sum[...] = jnp.zeros_like(value_sum)
    position_sum[...] = jnp.zeros_like(position_sum)
    turn = (
        lax.broadcasted_iota(jnp.int32, (row_block, row_block), 0)
        + lax.broadcasted_iota(jnp.int32, (row_block, row_block), 1)
        == row_block - 1
    ).astype(LOW)
    wait(rows_copies + weight_copies_)
    mixed_grad_ref[...] = matmul(rows_ref[...], weight[:, 4 * heads : 5 * heads]).astype(LOW)
    for h in range(head_count):
        columns = slice(h * head_size, (h + 1) * head_size)
        content_total = jnp.zeros((1, head_size), FLOAT)
        position_total = jnp.zeros((1, head_size), FLOAT)
        for q in range(pieces):
            rows = pl.ds(q * row_block, row_block)
            mixed_grad = mixed_grad_ref[rows, columns]
            prob = prob_ref[h, rows, :]
            prob_float = prob.astype(FLOAT)
            prob_grad = times_transposed(mixed_grad, value_ref[:, columns])
            inner = jnp.sum(prob_grad * prob_float, axis=1, keepdims=True)
            score_grad = (prob_float * (prob_grad - inner)).astype(LOW)
            value_sum[:, columns] += outer_sum(prob, mixed_grad)
            key_sum[:, columns] += outer_sum(score_grad, content_rows_ref[rows, columns])
            turned = matmul(turn, score_grad).astype(LOW)
            content_part = matmul(turned, key_ref[:, columns]) * scale
            broad = jnp.concatenate([turned, jnp.zeros((row_block, row_block), LOW)], axis=1)
            broad = pltpu.roll(broad, 0, axis=1, stride=1, stride_axis=0)
            relative = relative_window(position_ref, firsts[q], row_block, columns)[...]
            position_part = matmul(broad, relative) * scale
            turned_rows = matmul(turn, position_rows_ref[rows, columns]).astype(LOW)
            total_ref = relative_window(position_sum, firsts[q], row_block, columns)
            total_ref[...] += outer_sum(broad, turned_rows)
            query_grad = (content_part + position_part).astype(LOW)
            qkv_grad_ref[rows, columns] = matmul(turn, query_grad).astype(LOW)
            content_total += jnp.sum(content_part, axis=0, keepdims=True)
            position_total += jnp.sum(position_part, axis=0, keepdims=True)
        bias_grad_ref[h : h + 1, :] = content_total
        bias_grad_ref[head_count + h : head_count + h + 1, :] = position_total
    for q in range(pieces):
        rows, plain = pl.ds(q * row_block, row_block), pl.ds(firsts[q], row_block)
        qkv_grad_ref[rows, heads : 2 * heads] = (key_sum[plain, :] * scale).astype(LOW)
        qkv_grad_ref[rows, 2 * heads :] = value_sum[plain, :].astype(LOW)
    position_grad_ref[...] = (position_sum[...] * scale).astype(LOW)

    @tiles(weight.shape[0])
    def _(features):
        write_parts(
            hi_ref, next_ref, own_ref, features,
            times_transposed(qkv_grad_ref[...], weight[features, : 3 * heads]),
        )


def attention_backward(place, owners, rows, weights, stored, head_count):
    row_count, features = len(rows) * rows[0].shape[0], rows[0].shape[1]
    position = stored[0]
    heads = position.shape[1]
    return call(
        functools.partial(
            attention_backward_kernel, pieces=len(rows), weights=len(weights),
            head_count=head_count,
        ),
        [
            ((row_count, features), LOW),
            ((row_count, 3 * heads), LOW),
            (position.shape, LOW),
            ((2 * head_count, heads // head_count), FLOAT),
        ]
        + row_parts(row_count, features),
        [
            pltpu.VMEM((features, 5 * heads), LOW),
            pltpu.VMEM((row_count, heads), LOW),
            pltpu.VMEM((row_count, heads), FLOAT),
            pltpu.VMEM((row_count, heads), FLOAT),
            pltpu.VMEM(position.shape, FLOAT),
            pltpu.SemaphoreType.DMA((len(rows) + weight_copies(weights, owners),)),
        ],
        8 * row_count * features * heads + 16 * heads * row_count**2,
        ("smem", place), ("smem", owners),
        *[("any", array) for array in list(rows) + list(weights)],
        *[("vmem", array) for array in stored],
    )


MARGIN = 8


def conv_matches(lengths_ref, row_count, taps):
    places = lax.broadcasted_iota(jnp.int32, (row_count, 1), 0)
    segment = segment_of(lengths_ref, places)
    valid = (segment < lengths_ref.shape[1]).astype(FLOAT)
    matches = []
    for t in range(taps):
        other = segment_of(lengths_ref, places + (t - taps // 2))
        matches.append((other == segment).astype(FLOAT))
    return valid, matches


def conv_lift_kernel(*refs, pieces, weights):
    place_ref, lengths_ref, owners_ref, taps_ref = refs[:4]
    refs = refs[4:]
    row_refs, refs = refs[:pieces], refs[pieces:]
    weight_refs, refs = refs[:weights], refs[weights:]
    rows_ref, lifted_ref, convolved_ref, sums_ref, weight, padded, semaphores = refs
    row_count, channels = convolved_ref.shape
    taps = taps_ref.shape[0]
    row_block = row_count // pieces
    copies = Copies(semaphores)
    rows_copies = copies.stack(row_refs, rows_ref)
    weight_copies_ = copies.weight(weight_refs, owners_ref, weight, slice(0, 2 * channels))
    firsts = block_firsts(place_ref, pieces, row_block)
    valid, matches = conv_matches(lengths_ref, row_count, taps)
    padded[:MARGIN, :] = jnp.zeros((MARGIN, channels), FLOAT)
    padded[MARGIN + row_count :, :] = jnp.zeros((MARGIN, channels), FLOAT)
    wait(rows_copies + weight_copies_)
    lifted = matmul(rows_ref[...], weight[...])
    for q in range(pieces):
        lifted_ref[pl.ds(firsts[q], row_block), :] = lifted[q * row_block : (q + 1) * row_block]
    gated = lifted_ref[:, :channels] * jax.nn.sigmoid(lifted_ref[:, channels:]) * valid
    padded[MARGIN : MARGIN + row_count, :] = gated
    convolved = jnp.zeros((row_count, channels), FLOAT)
    for t in range(taps):
        first = MARGIN + t - taps // 2
        convolved += taps_ref[t : t + 1, :] * matches[t] * padded[first : first + row_count, :]
    convolved_ref[...] = convolved
    masked = convolved * valid
    sums_ref[...] = jnp.zeros_like(sums_ref)
    sums_ref[0:1, :] = jnp.sum(masked, axis=0, keepdims=True)
    sums_ref[1:2, :] = jnp.sum(masked * convolved, axis=0, keepdims=True)
    sums_ref[2:3, :] = jnp.zeros((1, channels), FLOAT) + jnp.sum(valid, axis=0, keepdims=True)


def conv_lift(place, lengths, owners, taps, rows, weights):
    row_count, features = len(rows) * rows[0].shape[0], rows[0].shape[1]
    channels = taps.shape[1]
    return call(
        functools.partial(conv_lift_kernel, pieces=len(rows), weights=len(weights)),
        [
            ((row_count, features), LOW),
            ((row_count, 2 * channels), FLOAT),
            ((row_count, channels), FLOAT),
            ((8, channels), FLOAT),
        ],
        [
            pltpu.VMEM((features, 2 * channels), LOW),
            pltpu.VMEM((row_count + 2 * MARGIN, channels), FLOAT),
            pltpu.SemaphoreType.DMA((len(rows) + weight_copies(weights, owners),)),
        ],
        4 * row_count * features * channels,
        ("smem", place), ("smem", lengths), ("smem", owners), ("vmem", taps),
        *[("any", array) for array in list(rows) + list(weights)],
    )


def batch_scales(sums_ref):
    count = sums_ref[2:3, :]
    average = sums_ref[0:1, :] / count
    return count, average, lax.rsqrt(sums_ref[1:2, :] / count - average * average + EPSILON)


def conv_out_kernel(*refs, pieces, weights):
    place_ref, lengths_ref, owners_ref, affine_ref, sums_ref, convolved_ref = refs[:6]
    refs = refs[6:]
    weight_refs, refs = refs[:weights], refs[weights:]
    swished_ref, hi_ref, next_ref, own_ref, weight, plain, semaphores = refs
    row_count, channels = convolved_ref.shape
    row_block = row_count // pieces
    copies = Copies(semaphores)
    weight_copies_ = copies.weight(
        weight_refs, owners_ref, weight, slice(2 * channels, 3 * channels)
    )
    firsts = block_firsts(place_ref, pieces, row_block)
    places = lax.broadcasted_iota(jnp.int32, (row_count, 1), 0)
    valid = (segment_of(lengths_ref, places) < lengths_ref.shape[1]).astype(FLOAT)
    _, average, inverse = batch_scales(sums_ref)
    hatted = (convolved_ref[...] - average) * inverse
    normalized = hatted * affine_ref[0:1, :] + affine_ref[1:2, :]
    plain[...] = (normalized * jax.nn.sigmoid(normalized) * valid).astype(LOW)
    for q in range(pieces):
        swished_ref[q * row_block : (q + 1) * row_block, :] = plain[
            pl.ds(firsts[q], row_block), :
        ]
    wait(weight_copies_)

    @tiles(weight.shape[0])
    def _(features):
        write_parts(
            hi_ref, next_ref, own_ref, features, times_transposed(swished_ref[...], weight[features, :])
        )


def conv_out(place, lengths, owners, affine, sums, convolved, weights, pieces, features):
    row_count, channels = convolved.shape
    return call(
        functools.partial(conv_out_kernel, pieces=pieces, weights=len(weights)),
        [((row_count, channels), LOW)] + row_parts(row_count, features),
        [
            pltpu.VMEM((features, channels), LOW),
            pltpu.VMEM((row_count, channels), LOW),
            pltpu.SemaphoreType.DMA((weight_copies(weights, owners),)),
        ],
        2 * row_count * features * channels,
        ("smem", place), ("smem", lengths), ("smem", owners),
        ("vmem", affine), ("vmem", sums), ("vmem", convolved),
        *[("any", array) for array in weights],
    )


def conv_back_sums_kernel(*refs, pieces, weights):
    place_ref, lengths_ref, owners_ref, affine_ref, sums_ref, convolved_ref = refs[:6]
    refs = refs[6:]
    row_refs, refs = refs[:pieces], refs[pieces:]
    weight_refs, refs = refs[:weights], refs[weights:]
    rows_ref, normal_ref, back_ref, weight, plain, semaphores = refs
    row_count, channels = convolved_ref.shape
    row_block = row_count // pieces
    copies = Copies(semaphores)
    rows_copies = copies.stack(row_refs, rows_ref)
    weight_copies_ = copies.weight(
        weight_refs, owners_ref, weight, slice(2 * channels, 3 * channels)
    )
    firsts = block_firsts(place_ref, pieces, row_block)
    places = lax.broadcasted_iota(jnp.int32, (row_count, 1), 0)
    valid = (segment_of(lengths_ref, places) < lengths_ref.shape[1]).astype(FLOAT)
    _, average, inverse = batch_scales(sums_ref)
    hatted = (convolved_ref[...] - average) * inverse
    normalized = hatted * affine_ref[0:1, :] + affine_ref[1:2, :]
    squashed = jax.nn.sigmoid(normalized)
    wait(rows_copies + weight_copies_)
    product = matmul(rows_ref[...], weight[...])
    for q in range(pieces):
        plain[pl.ds(firsts[q], row_block), :] = product[q * row_block : (q + 1) * row_block]
    normal = plain[...] * valid * squashed * (1.0 + normalized * (1.0 - squashed))
    normal_ref[...] = normal
    back_ref[...] = jnp.zeros_like(back_ref)
    back_ref[0:1, :] = jnp.sum(normal, axis=0, keepdims=True)
    back_ref[1:2, :] = jnp.sum(normal * hatted, axis=0, keepdims=True)


def conv_back_sums(place, lengths, owners, affine, sums, convolved, rows, weights):
    row_count, channels = convolved.shape
    features = rows[0].shape[1]
    return call(
        functools.partial(conv_back_sums_kernel, pieces=len(rows), weights=len(weights)),
        [
            ((row_count, features), LOW), ((row_count, channels), FLOAT), ((8, channels), FLOAT)
        ],
        [
            pltpu.VMEM((features, channels), LOW),
            pltpu.VMEM((row_count, channels), FLOAT),
            pltpu.SemaphoreType.DMA((len(rows) + weight_copies(weights, owners),)),
        ],
        2 * row_count * features * channels,
        ("smem", place), ("smem", lengths), ("smem", owners),
        ("vmem", affine), ("vmem", sums), ("vmem", convolved),
        *[("any", array) for array in list(rows) + list(weights)],
    )


def conv_back_kernel(*refs, pieces, weights):
    (
        place_ref, lengths_ref, owners_ref, taps_ref, affine_ref, sums_ref, back_ref,
        convolved_ref, normal_ref, lifted_ref,
    ) = refs[:10]
    refs = refs[10:]
    weight_refs, refs = refs[:weights], refs[weights:]
    lifted_grad_ref, taps_grad_ref, hi_ref, next_ref, own_ref, weight, padded, padded_grad, plain, semaphores = refs
    row_count, channels = convolved_ref.shape
    taps = taps_ref.shape[0]
    row_block = row_count // pieces
    copies = Copies(semaphores)
    weight_copies_ = copies.weight(weight_refs, owners_ref, weight, slice(0, 2 * channels))
    firsts = block_firsts(place_ref, pieces, row_block)
    valid, matches = conv_matches(lengths_ref, row_count, taps)
    count, average, inverse = batch_scales(sums_ref)
    gain = affine_ref[0:1, :]
    hatted = (convolved_ref[...] - average) * inverse
    conv_grad = inverse * (
        normal_ref[...] * gain
        - valid * gain * (back_ref[0:1, :] + hatted * back_ref[1:2, :]) / count
    )
    value = lifted_ref[:, :channels]
    gate = jax.nn.sigmoid(lifted_ref[:, channels:])
    for scratch in (padded, padded_grad):
        scratch[:MARGIN, :] = jnp.zeros((MARGIN, channels), FLOAT)
        scratch[MARGIN + row_count :, :] = jnp.zeros((MARGIN, channels), FLOAT)
    padded[MARGIN : MARGIN + row_count, :] = value * gate * valid
    padded_grad[MARGIN : MARGIN + row_count, :] = conv_grad
    taps_grad_ref[...] = jnp.zeros_like(taps_grad_ref)
    gated_grad = jnp.zeros((row_count, channels), FLOAT)
    for t in range(taps):
        offset = t - taps // 2
        read = padded[MARGIN + offset : MARGIN + offset + row_count, :]
        taps_grad_ref[t : t + 1, :] = jnp.sum(
            matches[t] * read * conv_grad, axis=0, keepdims=True
        )
        back = padded_grad[MARGIN - offset : MARGIN - offset + row_count, :]
        gated_grad += taps_ref[t : t + 1, :] * matches[taps - 1 - t] * back
    gated_grad = gated_grad * valid
    plain[:, :channels] = (gated_grad * gate).astype(LOW)
    plain[:, channels:] = (gated_grad * value * gate * (1.0 - gate)).astype(LOW)
    for q in range(pieces):
        lifted_grad_ref[q * row_block : (q + 1) * row_block, :] = plain[
            pl.ds(firsts[q], row_block), :
        ]
    wait(weight_copies_)

    @tiles(weight.shape[0])
    def _(features):
        write_parts(
            hi_ref, next_ref, own_ref, features,
            times_transposed(lifted_grad_ref[...], weight[features, :]),
        )


def conv_back(
    place, lengths, owners, taps, affine, sums, back, convolved, normal, lifted, weights, pieces,
    features,
):
    row_count, channels = convolved.shape
    return call(
        functools.partial(conv_back_kernel, pieces=pieces, weights=len(weights)),
        [((row_count, 2 * channels), LOW), ((8, channels), FLOAT)] + row_parts(row_count, features),
        [
            pltpu.VMEM((features, 2 * channels), LOW),
            pltpu.VMEM((row_count + 2 * MARGIN, channels), FLOAT),
            pltpu.VMEM((row_count + 2 * MARGIN, channels), FLOAT),
            pltpu.VMEM((row_count, 2 * channels), LOW),
            pltpu.SemaphoreType.DMA((weight_copies(weights, owners),)),
        ],
        4 * row_count * features * channels,
        ("smem", place), ("smem", lengths), ("smem", owners),
        *[
            ("vmem", array)
            for array in (taps, affine, sums, back, convolved, normal, lifted)
        ],
        *[("any", array) for array in weights],
    )


def standardize(values):
    average = jnp.mean(values, axis=-1, keepdims=True)
    centred = values - average
    spread_of = jnp.mean(centred * centred, axis=-1, keepdims=True)
    scale = lax.rsqrt(spread_of + EPSILON)
    return centred * scale, scale


def norm_back(values, norm_gain, normed_grad):
    hat, scale = standardize(values)
    gained = normed_grad * norm_gain
    first = jnp.mean(gained, axis=-1, keepdims=True)
    second = jnp.mean(gained * hat, axis=-1, keepdims=True)
    grad = (gained - first - hat * second) * scale
    return grad, jnp.sum(normed_grad * hat, axis=0, keepdims=True)


def middle_kernel(next_ref, arrived_ref, sent_ref):
    first = next_ref.shape[0]
    sent_ref[...] = (
        next_ref[...].astype(FLOAT) + arrived_ref[first:, :].astype(FLOAT)
    ).astype(LOW)


def sum_rows(hi, next_part, own_part):
    arrived = swap(hi, "mp", 1)
    (sent,) = call(
        middle_kernel, [(next_part.shape, LOW)], [], next_part.size,
        ("vmem", next_part), ("vmem", arrived),
    )
    return own_part, arrived, swap(sent, "mp", 2)


def summed(own_ref, near_ref, far_ref):
    rows = own_ref.shape[0]
    return own_ref[...] + near_ref[:rows, :].astype(FLOAT) + far_ref[...].astype(FLOAT)


def all_rows(own):
    across = swap(own, "mp", 2)
    return [own, across, swap(own, "mp", 1), swap(across, "mp", 1)]


def step_kernel(
    own_ref, near_ref, far_ref, residual_ref, gain_ref, next_ref, normed_ref, *, factor
):
    residual = residual_ref[...].astype(FLOAT) + factor * summed(own_ref, near_ref, far_ref)
    next_ref[...] = residual
    normed_ref[...] = (standardize(residual)[0] * gain_ref[...]).astype(LOW)


def step(parts, residual, gain, factor):
    shape = parts[0].shape
    return call(
        functools.partial(step_kernel, factor=factor), [(shape, FLOAT), (shape, LOW)], [],
        8 * math.prod(shape),
        *[("vmem", array) for array in (*parts, residual, gain)],
    )


def turn_kernel(
    own_ref, near_ref, far_ref, residual_ref, gain_ref, out_grad_ref,
    result_ref, grad_ref, branch_ref, gain_grad_ref,
):
    residual = residual_ref[...] + 0.5 * summed(own_ref, near_ref, far_ref)
    gain = gain_ref[...]
    result_ref[...] = (standardize(residual)[0] * gain).astype(LOW)
    grad, gain_grad = norm_back(residual, gain, out_grad_ref[...].astype(FLOAT))
    grad_ref[...] = grad
    branch_ref[...] = (0.5 * grad).astype(LOW)
    gain_grad_ref[...] = gain_grad


def turn(parts, residual, gain, out_grad):
    shape = parts[0].shape
    return call(
        turn_kernel,
        [(shape, LOW), (shape, FLOAT), (shape, LOW), ((1, shape[1]), FLOAT)], [],
        16 * math.prod(shape),
        *[("vmem", array) for array in (*parts, residual, gain, out_grad)],
    )


def step_back_kernel(
    own_ref, near_ref, far_ref, residual_ref, gain_ref, grad_ref,
    next_ref, branch_ref, gain_grad_ref, *, factor,
):
    normed_grad = summed(own_ref, near_ref, far_ref)
    grad, gain_grad = norm_back(residual_ref[...].astype(FLOAT), gain_ref[...], normed_grad)
    grad = grad_ref[...] + grad
    next_ref[...] = grad
    branch_ref[...] = (factor * grad).astype(LOW)
    gain_grad_ref[...] = gain_grad


def step_back(parts, residual, gain, grad, factor):
    shape = parts[0].shape
    return call(
        functools.partial(step_back_kernel, factor=factor),
        [(shape, FLOAT), (shape, LOW), ((1, shape[1]), FLOAT)], [],
        16 * math.prod(shape),
        *[("vmem", array) for array in (*parts, residual, gain, grad)],
    )


def select_kernel(place_ref, *refs):
    pieces, target_ref = refs[:-1], refs[-1]
    row_block = pieces[0].shape[0]
    for piece, first in zip(pieces, block_firsts(place_ref, len(pieces), row_block)):
        target_ref[pl.ds(first, row_block), :] = piece[...]


def select_rows(place, pieces):
    row_block, features = pieces[0].shape
    (outcome,) = call(
        select_kernel, [((len(pieces) * row_block, features), pieces[0].dtype)], [], 0,
        ("smem", place), *[("vmem", piece) for piece in pieces],
    )
    return outcome


def finish_kernel(*refs, counts):
    sources, targets = refs[: 2 * len(counts)], refs[2 * len(counts) :]
    at = 0
    for i, count in enumerate(counts):
        total = sources[2 * i][...] + sources[2 * i + 1][...].astype(FLOAT)
        first = 0
        for target in targets[at : at + count]:
            last = first + target.shape[1]
            target[...] = total[:, first:last]
            first = last
        at += count


def finish(sums, widths, *tokens):
    rows = sums[0].kept.shape[0]
    parts, counts, left = [], [], list(widths)
    for part in sums:
        parts += [("vmem", part.kept), ("vmem", after(part.sent, *tokens))]
        count, total = 0, 0
        while total < part.kept.shape[1]:
            total, count = total + left.pop(0), count + 1
        counts.append(count)
    return call(
        functools.partial(finish_kernel, counts=tuple(counts)),
        [((rows, width), FLOAT) for width in widths], [], 0, *parts,
    )


def join_kernel(*refs):
    target, first = refs[-1], 0
    for kept, arrived in zip(refs[0:-1:2], refs[1:-1:2]):
        last = first + kept.shape[1]
        target[:, first:last] = kept[...] + arrived[...].astype(FLOAT)
        first = last


def join(sums):
    rows, width = sums[0].kept.shape[0], sum(part.kept.shape[1] for part in sums)
    parts = []
    for part in sums:
        parts += [("vmem", part.kept), ("vmem", part.sent)]
    return call(join_kernel, [((rows, width), FLOAT)], [], 0, *parts)[0]


def per_device(
    inputs,
    lengths,
    out_grad,
    first_norm,
    first_up,
    first_down,
    attention_norm,
    query_weight,
    key_weight,
    value_weight,
    position_weight,
    output_weight,
    content_bias,
    position_bias,
    convolution_norm,
    pointwise_in,
    depthwise_kernel,
    batch_gain,
    batch_shift,
    pointwise_out,
    second_norm,
    second_up,
    second_down,
    final_norm,
):
    row_count, feature_count = inputs.shape
    dp_size, mp_size = lax.axis_size("dp"), lax.axis_size("mp")
    dp_at, mp_at = lax.axis_index("dp"), lax.axis_index("mp")
    block, hidden = first_up.shape
    row_block = row_count // mp_size
    bias_rows, head_count = content_bias.shape
    head_size = bias_rows * dp_size
    heads = head_count * head_size
    local_channels, tap_count = depthwise_kernel.shape
    channels = local_channels * dp_size
    place = mp_at.reshape(1).astype(jnp.int32)

    places = jnp.arange(feature_count, dtype=jnp.int32)
    owners = dp_at ^ reversed_bits(places // block, dp_size)
    source = owners * block + places % block
    selection = (places[:, None] == source[None, :]).astype(LOW)
    block_places = jnp.arange(dp_size, dtype=jnp.int32)
    block_owners = (dp_at ^ reversed_bits(block_places, dp_size)).astype(jnp.int32)
    block_selection = (block_places[:, None] == block_owners[None, :]).astype(LOW)

    up_own = first_up.astype(LOW)
    small_own = jnp.concatenate(
        [
            part.reshape(-1)
            for part in (
                first_norm, attention_norm, convolution_norm, second_norm, final_norm,
                content_bias, position_bias, depthwise_kernel, batch_gain, batch_shift,
            )
        ]
    )
    small_own = after(small_own, up_own).astype(LOW)
    links = Links(4)
    up_spread = Spread(links, up_own)
    up_spread.go(ORDER)
    ups = up_spread.blocks
    down_own = after(first_down, ups[1]).astype(LOW)
    down_spread = Spread(links, down_own)
    down_spread.go(ORDER)
    downs = down_spread.blocks
    gates, mask = [downs[1], ups[5], ups[3]], dp_size // 2
    small_all = small_own[None]
    while mask:
        arrived = swap(small_all, "dp", mask)
        if gates:
            arrived = after(arrived, gates.pop())
        small_all = jnp.concatenate([small_all, arrived], axis=0)
        mask //= 2

    def gather(values, *tokens):
        return [lax.all_gather(after(values, *tokens), "dp", axis=0, tiled=True)]

    attention_own = jnp.concatenate(
        after(
            (query_weight, key_weight, value_weight, position_weight, output_weight), ups[3]
        ),
        axis=1,
    ).astype(LOW)
    attention_spread = Spread(links, attention_own)
    attention_spread.go(ORDER[:3])
    pointwise_in, pointwise_out, second_up, second_down = after(
        (pointwise_in, pointwise_out, second_up, second_down), downs[3]
    )
    convolution_own = jnp.concatenate(
        [pointwise_in.reshape(block, 2 * channels), pointwise_out], axis=1
    ).astype(LOW)
    second_own = jnp.concatenate([second_up, second_down], axis=1).astype(LOW)

    whole, first_half, second_half = (
        slice(0, hidden), slice(0, hidden), slice(hidden, 2 * hidden)
    )

    norms = small_all[:, : 5 * block].astype(FLOAT).reshape(dp_size, 5, block)
    norms = norms.transpose(1, 0, 2).reshape(5, 1, feature_count)
    first_gain, attention_gain, convolution_gain, second_gain, final_gain = norms
    plain_small = matmul(block_selection, small_all[:, 5 * block :])
    cut = bias_rows * head_count
    content_all = plain_small[:, :cut].reshape(head_size, head_count).T
    position_all = plain_small[:, cut : 2 * cut].reshape(head_size, head_count).T
    at = 2 * cut + local_channels * tap_count
    taps = plain_small[:, 2 * cut : at].reshape(channels, tap_count).T
    affine = jnp.stack(
        [
            plain_small[:, at : at + local_channels].reshape(channels),
            plain_small[:, at + local_channels :].reshape(channels),
        ]
    )

    arranged = matmul(
        jnp.concatenate(
            [
                lax.dynamic_slice_in_dim(
                    inputs, (mp_at ^ fixed_reversed(q, mp_size)) * row_block, row_block, axis=0
                )
                for q in range(mp_size)
            ],
            axis=0,
        ),
        selection,
    )
    own_out_grad = matmul(
        lax.dynamic_slice_in_dim(out_grad, mp_at * row_block, row_block, axis=0), selection
    ).astype(LOW)
    table_places = after(jnp.arange(2 * row_count, dtype=jnp.int32), ups[3])
    sin_table = position_table(table_places, row_count, feature_count)
    sin_table = matmul(sin_table, selection).astype(LOW)

    residual_zero = arranged[:row_block].astype(LOW)
    hat_a = standardize(arranged)[0]
    normed_a = (hat_a * first_gain).astype(LOW)
    hat_a = hat_a.astype(LOW)
    _, before_a, active_a, hi, next_part, own_part = ffn_call(
        ffn_forward_kernel, block_owners, [normed_a], ups, downs, whole, whole
    )
    attention_spread.go(ORDER[3:], hi)
    attention_all = attention_spread.blocks
    residual_one, own_b = step(sum_rows(hi, next_part, own_part), residual_zero, attention_gain, 0.5)
    second_all = gather(second_own, attention_all[3])
    convolution_spread = Spread(links, after(convolution_own, hi))
    convolution_spread.go(ORDER[:2])

    normed_b, mixed_rows, prob, content_rows, position_rows, keys, values, position, hi, next_part, own_part = (
        attention_forward(
            place, lengths, block_owners, all_rows(own_b), attention_all, sin_table, content_all,
            position_all,
        )
    )
    convolution_spread.go(ORDER[2:], hi)
    convolution_all = convolution_spread.blocks
    residual_two, own_c = step(sum_rows(hi, next_part, own_part), residual_one, convolution_gain, 1.0)

    normed_c, lifted, convolved, sums = conv_lift(
        place, lengths, block_owners, taps, all_rows(own_c), convolution_all
    )
    sums, _ = total_hops(sums, "dp")
    swished, hi, next_part, own_part = conv_out(
        place, lengths, block_owners, affine, sums, convolved, convolution_all, mp_size,
        feature_count,
    )
    residual_three, own_d = step(sum_rows(hi, next_part, own_part), residual_two, second_gain, 1.0)

    normed_d, before_d, active_d, hi, next_part, own_part = ffn_call(
        ffn_forward_kernel, block_owners, all_rows(own_d), second_all, second_all, first_half,
        second_half,
    )
    own_result, residual_grad, branch, final_gain_grad = turn(
        sum_rows(hi, next_part, own_part), residual_three, final_gain, own_out_grad
    )

    branch_rows, before_grad, hi, next_part, own_part = ffn_call(
        ffn_backward_kernel, block_owners, all_rows(branch), second_all, second_all, first_half,
        second_half, before_d,
    )
    second_down_sum, second_up_sum = (
        WeightSum((branch_rows, active_d)), WeightSum((normed_d, before_grad))
    )
    links = Links(2, apart=True)
    second_down_sum.advance(links=links)
    residual_grad, branch, second_gain_grad = step_back(
        sum_rows(hi, next_part, own_part), residual_three, second_gain, residual_grad, 1.0
    )

    branch_rows, normal, back_sums = conv_back_sums(
        place, lengths, block_owners, affine, sums, convolved, all_rows(branch), convolution_all
    )
    back_sums, hops = total_hops(back_sums, "dp")
    second_down_sum.advance(hops[-2], links=links)
    second_up_sum.advance(hops[-1], links=links)
    lifted_grad, taps_grad, hi, next_part, own_part = conv_back(
        place, lengths, block_owners, taps, affine, sums, back_sums, convolved, normal, lifted,
        convolution_all, mp_size, feature_count,
    )
    convolution_sum = WeightSum((normed_c, lifted_grad), (branch_rows, swished))
    convolution_sum.advance(second_up_sum.upper, links=links)
    parts = sum_rows(hi, next_part, own_part)
    second_down_sum.advance(parts[1], links=links)
    residual_grad, branch, convolution_gain_grad = step_back(
        parts, residual_two, convolution_gain, residual_grad, 1.0
    )
    first_row = dp_at * local_channels
    gain_piece = lax.dynamic_slice_in_dim(back_sums[1], first_row, local_channels)
    shift_piece = lax.dynamic_slice_in_dim(back_sums[0], first_row, local_channels)

    rows = all_rows(branch)
    second_up_sum.advance(rows[1], links=links)
    branch_rows, qkv_grad, position_grad, bias_grads, hi, next_part, own_part = attention_backward(
        place, block_owners, rows, attention_all,
        (position, prob, content_rows, position_rows, keys, values), head_count,
    )
    convolution_sum.advance(hi, links=links)
    attention_sum = WeightSum(
        (normed_b, qkv_grad), (sin_table, position_grad), (branch_rows, mixed_rows)
    )
    attention_sum.advance(hi, links=links)
    parts = sum_rows(hi, next_part, own_part)
    second_up_sum.advance(parts[1], links=links)
    residual_grad, branch, attention_gain_grad = step_back(
        parts, residual_one, attention_gain, residual_grad, 0.5
    )
    convolution_sum.advance(branch, links=links)

    branch_rows, before_grad, hi, next_part, own_part, first_gain_grad = ffn_call(
        ffn_backward_kernel, block_owners, all_rows(branch), ups, downs, whole, whole, before_a,
        hat_a,
    )
    half = hidden // 2
    first_sums = [
        WeightSum((branch_rows, active_a[:, :half])),
        WeightSum((branch_rows, active_a[:, half:])),
        WeightSum((normed_a, before_grad[:, :half])),
        WeightSum((normed_a, before_grad[:, half:])),
    ]

    plain_grads = jnp.concatenate(
        [
            bias_grads[:head_count].T.reshape(dp_size, cut),
            bias_grads[head_count:].T.reshape(dp_size, cut),
            taps_grad[:tap_count].T.reshape(dp_size, local_channels * tap_count),
        ],
        axis=1,
    )
    plain_grads = lax.dot_general(
        block_selection.astype(FLOAT), plain_grads, (((0,), (0,)), ((), ())),
        precision=lax.Precision.HIGHEST, preferred_element_type=FLOAT,
    )
    gain_grads = jnp.concatenate(
        [
            first_gain_grad, attention_gain_grad, convolution_gain_grad, second_gain_grad,
            final_gain_grad,
        ],
        axis=0,
    )
    gain_grads = gain_grads.reshape(5, dp_size, block).transpose(1, 0, 2)
    small_grads = jnp.concatenate([gain_grads.reshape(dp_size, 5 * block), plain_grads], axis=1)

    smalls, mask = [small_grads], [1]

    def small_step():
        if mask[0] < dp_size:
            kept = smalls[0].shape[0] // 2
            smalls[0] = smalls[0][:kept] + links.swap(smalls[0][kept:], mask[0])
            mask[0] *= 2

    down_a, down_b, up_a, up_b = first_sums
    small_step()
    for part in (
        down_a, attention_sum, down_b, attention_sum, None, down_a, up_a, down_b, up_b, down_a,
        None, up_a, down_b, up_b, up_a, up_b,
    ):
        if part is None:
            small_step()
        else:
            part.advance(links=links)
    while mask[0] < dp_size:
        small_step()
    for part in (second_down_sum, second_up_sum, convolution_sum, attention_sum, *first_sums):
        part.rest()

    parts = sum_rows(hi, next_part, own_part)
    residual_grad, _, _ = step_back(parts, residual_zero, first_gain, residual_grad, 1.0)
    second_down_grad, second_up_grad, convolution_in_grad, convolution_out_grad = finish(
        [second_down_sum, second_up_sum, convolution_sum],
        [hidden, hidden, 2 * channels, channels], parts[2],
    )
    attention_grads = finish([attention_sum], [heads] * 5)
    first_down_grad, first_up_grad = join(first_sums[:2]), join(first_sums[2:])

    def plain_order(own):
        pieces = all_rows(times_transposed(own, selection).astype(LOW))
        return select_rows(place, pieces)

    result = plain_order(after(own_result, hi))
    inputs_grad = plain_order(residual_grad.astype(LOW)).astype(FLOAT)

    small_grads = smalls[0][0]
    gain_grads = total_over(small_grads[: 5 * block].reshape(5, block), "mp")
    plain_grads = small_grads[5 * block :]

    return (
        result,
        inputs_grad,
        gain_grads[0],
        first_up_grad,
        first_down_grad,
        gain_grads[1],
        *attention_grads,
        plain_grads[:cut].reshape(bias_rows, head_count),
        plain_grads[cut : 2 * cut].reshape(bias_rows, head_count),
        gain_grads[2],
        convolution_in_grad.reshape(block, 2, channels),
        plain_grads[2 * cut :].reshape(local_channels, tap_count),
        gain_piece,
        shift_piece,
        convolution_out_grad,
        gain_grads[3],
        second_up_grad,
        second_down_grad,
        gain_grads[4],
    )


def solution(mesh):
    return jax.shard_map(
        per_device,
        mesh=mesh,
        in_specs=(
            P("dp", None),
            P("dp", None),
            P("dp", None),
            P("dp"),
            P("dp", "mp"),
            P("dp", "mp"),
            P("dp"),
            P("dp", "mp"),
            P("dp", "mp"),
            P("dp", "mp"),
            P("dp", "mp"),
            P("dp", "mp"),
            P("dp", "mp"),
            P("dp", "mp"),
            P("dp"),
            P("dp", None, "mp"),
            P(("mp", "dp"), None),
            P(("mp", "dp")),
            P(("mp", "dp")),
            P("dp", "mp"),
            P("dp"),
            P("dp", "mp"),
            P("dp", "mp"),
            P("dp"),
        ),
        out_specs=(
            P("dp", None),
            P("dp", None),
            P("dp"),
            P("dp", "mp"),
            P("dp", "mp"),
            P("dp"),
            P("dp", "mp"),
            P("dp", "mp"),
            P("dp", "mp"),
            P("dp", "mp"),
            P("dp", "mp"),
            P("dp", "mp"),
            P("dp", "mp"),
            P("dp"),
            P("dp", None, "mp"),
            P(("mp", "dp"), None),
            P(("mp", "dp")),
            P(("mp", "dp")),
            P("dp", "mp"),
            P("dp"),
            P("dp", "mp"),
            P("dp", "mp"),
            P("dp"),
        ),
        check_vma=False,
    )
```

time: 747 us -> 521 us (0.70)
  waiting for transfers between devices: 410 us -> 227 us
  Pallas kernels: 0 us -> 83.3 us
  other arithmetic: 76.7 us -> 15.3 us
  local copies, waits for them, and re-layouts: 86.2 us -> 42.6 us
  matrix products: 79.8 us -> 40.9 us
  between operations: 4.57 us -> 16.5 us
  starting transfers between devices: 79.4 us -> 90 us
    ppermute x93 -> x109, waiting for transfers between devices: 410 us -> 227 us  [swap(): return lax.ppermute(values, axis, [(i, i ^ mask) for i in range(size)])]
    pallas_call x0 -> x32, Pallas kernels: none -> 83.3 us  [call(): pl.pallas_call(kernel, out_shape=tuple((jax.ShapeDtypeStruct(shape, kind)...]
    reshape x12 -> x13, local copies, waits for them, and re-layouts: 30.6 us -> 3.55 us  [the longest x2 1.77 us: per_device(): taps = plain_small[:, 2 * cut:at].reshape(channels, tap_count).T]
    concatenate x41 -> x6, other arithmetic: 24.2 us -> 2.17 us  [the longest x2 1.29 us: advance(): jnp.concatenate(upper, axis=1)]
    dot_general x12 -> x4, matrix products: 26 us -> 6.16 us  [matmul(): return jnp.dot(left_side, right_side, preferred_element_type=FLOAT)]
    dot_general x18 -> x2, matrix products: 22 us -> 3.09 us  [times_transposed(): lax.dot_general(left_side, right_side, (((1,), (1,)), ((), ())), preferre...]
    convert_element_type x29 -> x5, other arithmetic: 17.3 us -> 4.45 us  [the longest x1 1.7 us: per_device(): hat_a = hat_a.astype(LOW)]
    dot_general x18 -> x22, matrix products: 19.6 us -> 31.5 us  [outer_sum(): lax.dot_general(left_side, right_side, (((0,), (0,)), ((), ())), preferre...]
  transfers between devices with their start and end apart: 93 -> 110, of which waited for: 51 -> 58; matrix products, arithmetic and copies ran while one was open for 18% -> 15% of each run, Pallas kernels for 0% -> 13%
where the time goes in v2:
time: 521 us; the launch traced here: 516 us
  waiting for transfers between devices  227 us (44%)
  starting transfers between devices  90 us (17%)
  Pallas kernels  83.3 us (16%)
  local copies, waits for them, and re-layouts  42.6 us (8%)
  matrix products  40.9 us (8%)
  between operations  16.5 us (3%)
  other arithmetic  15.3 us (3%)
    ppermute x109, waiting for transfers between devices, swap(): return lax.ppermute(values, axis, [(i, i ^ mask) for i in range(size)])  227 us
    ppermute x109, starting transfers between devices, swap(): return lax.ppermute(values, axis, [(i, i ^ mask) for i in range(size)])  90 us
    pallas_call x32, Pallas kernels, call(): pl.pallas_call(kernel, out_shape=tuple((jax.ShapeDtypeStruct(shape, kind)...  83.3 us
    dot_general x22, matrix products, outer_sum(): lax.dot_general(left_side, right_side, (((0,), (0,)), ((), ())), preferre...  31.5 us
    unnamed x278, local copies, waits for them, and re-layouts  23.8 us
  transfers between devices with their start and end apart: 110, of which 58 were waited for; matrix products, arithmetic and copies ran while one was open for 15% of the time, Pallas kernels for 13%

profile of v2, /device:TPU:0, one launch (start us, length us, event | category | flops | bytes accessed | tf_op | source)
XLA Modules:
  0.0 515.8 jit_solution(8314725586496961155)
XLA Ops:
  29.3 6.3 %collective-permute-done.2.refs_5_.refs_8_ = bf16[128,1024]{1,0:T(8,128)(2,1)S(1)} collective-permute-done((bf16[128,1024]{1,0:T(8,128)(2,1)S(1)}, bf16[128,1024]{1,0:T(8,128)(2,1)S(1)}, u32[]{:S(2)}, u32[]{:S(2)}) %collective-permute-start.2) | collective-permute-done | bytes 262176 | tf_op jit(solution)/shard_map/ppermute | solution.py:43
  45.1 8.3 %collective-permute-done.6 = bf16[4,928]{1,0:T(4,128)(2,1)S(1)} collective-permute-done((bf16[4,928]{1,0:T(4,128)(2,1)S(1)}, bf16[4,928]{1,0:T(4,128)(2,1)S(1)}, u32[]{:S(2)}, u32[]{:S(2)}) %collective-permute-start.6) | collective-permute-done | bytes 7456 | tf_op jit(solution)/shard_map/ppermute | solution.py:43
  71.2 7.2 %shard_map.407 = (bf16[512,1024]{1,0:T(8,128)(2,1)}, bf16[512,1024]{1,0:T(8,128)(2,1)}, bf16[512,1024]{1,0:T(8,128)(2,1)}, bf16[256,1024]{1,0:T(8,128)(2,1)}, bf...) custom-call(s32[8]{0:T(128)S(1)} %fusion.111.refs_0_.refs_2_.refs_1_, bf16[512,1024]{1,0:T(8,128)(2,1)} %get-tuple-element.410.refs_1_, ...), custom_call_target="tpu_custom_call" | custom-call | flops 2147483648 | tf_op jit(solution)/shard_map/pallas_call | solution.py:186
  103.8 9.2 %collective-permute-done.23.refs_11_.refs_8_ = bf16[128,1280]{1,0:T(8,128)(2,1)S(1)} collective-permute-done((bf16[128,1280]{1,0:T(8,128)(2,1)S(1)}, bf16[128,1280]{1,0:T(8,128)(2,1)S(1)}, u32[]{:S(2)}, u32[]{:S(2)}) %collective-permute-start.23) | collective-permute-done | bytes 327712 | tf_op jit(solution)/shard_map/ppermute | solution.py:43
  118.0 6.1 %collective-permute-done.26.refs_14_.refs_11_ = bf16[128,1280]{1,0:T(8,128)(2,1)} collective-permute-done((bf16[128,1280]{1,0:T(8,128)(2,1)S(1)}, bf16[128,1280]{1,0:T(8,128)(2,1)}, u32[]{:S(2)}, u32[]{:S(2)}) %collective-permute-start.26) | collective-permute-done | bytes 327712 | tf_op jit(solution)/shard_map/ppermute | solution.py:43
  124.1 10.9 %collective-permute-done.27.refs_15_.refs_12_ = bf16[128,1280]{1,0:T(8,128)(2,1)} collective-permute-done((bf16[128,1280]{1,0:T(8,128)(2,1)S(1)}, bf16[128,1280]{1,0:T(8,128)(2,1)}, u32[]{:S(2)}, u32[]{:S(2)}) %collective-permute-start.27) | collective-permute-done | bytes 327712 | tf_op jit(solution)/shard_map/ppermute | solution.py:43
  135.0 10.5 %collective-permute-done.28.refs_16_.refs_13_ = bf16[128,1280]{1,0:T(8,128)(2,1)} collective-permute-done((bf16[128,1280]{1,0:T(8,128)(2,1)S(1)}, bf16[128,1280]{1,0:T(8,128)(2,1)}, u32[]{:S(2)}, u32[]{:S(2)}) %collective-permute-start.28) | collective-permute-done | bytes 327712 | tf_op jit(solution)/shard_map/ppermute | solution.py:43
  145.6 11.7 %shard_map.410 = (bf16[512,1024]{1,0:T(8,128)(2,1)}, bf16[512,256]{1,0:T(8,128)(2,1)S(1)}, bf16[2,512,512]{2,1,0:T(8,128)(2,1)}, bf16[512,256]{1,0:T(8,128)(2,1)...) custom-call(s32[1]{0:T(128)} %bitcast.refs_0_.place_ref, ...), custom_call_target="tpu_custom_call" | custom-call | flops 2214592512 | tf_op jit(solution)/shard_map/pallas_call | solution.py:186
  160.0 8.1 %collective-permute-done.30.far_ref = bf16[128,1024]{1,0:T(8,128)(2,1)S(1)} collective-permute-done((bf16[128,1024]{1,0:T(8,128)(2,1)S(1)}, bf16[128,1024]{1,0:T(8,128)(2,1)S(1)}, u32[]{:S(2)}, u32[]{:S(2)}) %collective-permute-start.30) | collective-permute-done | bytes 262176 | tf_op jit(solution)/shard_map/ppermute | solution.py:43
  217.0 7.9 %collective-permute-done.45.far_ref = bf16[128,1024]{1,0:T(8,128)(2,1)S(1)} collective-permute-done((bf16[128,1024]{1,0:T(8,128)(2,1)S(1)}, bf16[128,1024]{1,0:T(8,128)(2,1)S(1)}, u32[]{:S(2)}, u32[]{:S(2)}) %collective-permute-start.45) | collective-permute-done | bytes 262176 | tf_op jit(solution)/shard_map/ppermute | solution.py:43
  227.1 6.3 %collective-permute-done.46.refs_2_ = bf16[128,1024]{1,0:T(8,128)(2,1)S(1)} collective-permute-done((bf16[128,1024]{1,0:T(8,128)(2,1)S(1)}, bf16[128,1024]{1,0:T(8,128)(2,1)S(1)}, u32[]{:S(2)}, u32[]{:S(2)}) %collective-permute-start.46) | collective-permute-done | bytes 262176 | tf_op jit(solution)/shard_map/ppermute | solution.py:43
  239.5 7.0 %shard_map.417 = (bf16[512,1024]{1,0:T(8,128)(2,1)S(1)}, bf16[512,1024]{1,0:T(8,128)(2,1)}, bf16[512,1024]{1,0:T(8,128)(2,1)}, bf16[256,1024]{1,0:T(8,128)(2,1)S...) custom-call(s32[8]{0:T(128)S(1)} %fusion.111.refs_0_.refs_2_.refs_1_, bf16[128,1024]{1,0:T(8,128)(2,1)S(1)} %copy-done.31, ...), custom_call_target="tpu_custom_call" | custom-call | flops 2147483648 | tf_op jit(solution)/shard_map/pallas_call | solution.py:186
  250.9 7.1 %collective-permute-done.50.far_ref = bf16[128,1024]{1,0:T(8,128)(2,1)S(1)} collective-permute-done((bf16[128,1024]{1,0:T(8,128)(2,1)S(1)}, bf16[128,1024]{1,0:T(8,128)(2,1)S(1)}, u32[]{:S(2)}, u32[]{:S(2)}) %collective-permute-start.50) | collective-permute-done | bytes 262176 | tf_op jit(solution)/shard_map/ppermute | solution.py:43
  259.2 7.3 %collective-permute-done.51.refs_2_ = bf16[128,1024]{1,0:T(8,128)(2,1)S(1)} collective-permute-done((bf16[128,1024]{1,0:T(8,128)(2,1)S(1)}, bf16[128,1024]{1,0:T(8,128)(2,1)S(1)}, u32[]{:S(2)}, u32[]{:S(2)}) %collective-permute-start.51) | collective-permute-done | bytes 262176 | tf_op jit(solution)/shard_map/ppermute | solution.py:43
  268.0 7.4 %shard_map.420 = (bf16[512,1024]{1,0:T(8,128)(2,1)S(1)}, bf16[512,1024]{1,0:T(8,128)(2,1)}, bf16[256,1024]{1,0:T(8,128)(2,1)S(1)}, bf16[128,1024]{1,0:T(8,128)(2,1)S(1)}, f32[128,1024]{1,0:T(8,128)S(1)}) custom-call(s32[8]{0:T(128)S(1)} %fusion.111.refs_0_.refs_2_.refs_1_, bf16[128,1024]{1,0:T(8,128)(2,1)S(1)} %get-tuple-element.261.refs_1_, ...), custom_call_target="tpu_custom_call" | custom-call | flops 2147483648 | tf_op jit(solution)/shard_map/pallas_call | solution.py:186
  278.0 7.9 %collective-permute-done.55.far_ref = bf16[128,1024]{1,0:T(8,128)(2,1)S(1)} collective-permute-done((bf16[128,1024]{1,0:T(8,128)(2,1)S(1)}, bf16[128,1024]{1,0:T(8,128)(2,1)S(1)}, u32[]{:S(2)}, u32[]{:S(2)}) %collective-permute-start.55) | collective-permute-done | bytes 262176 | tf_op jit(solution)/shard_map/ppermute | solution.py:43
  317.2 6.5 %shard_map.424 = (bf16[512,512]{1,0:T(8,128)(2,1)S(1)}, f32[8,256]{1,0:T(8,128)S(1)}, bf16[256,1024]{1,0:T(8,128)(2,1)}, bf16[128,1024]{1,0:T(8,128)(2,1)S(1)}, f32[128,1024]{1,0:T(8,128)S(1)}) custom-call(s32[1]{0:T(128)} %bitcast.refs_0_.place_ref, s32[1,4]{1,0:T(1,128)S(1)} %copy-done.48, s32[8]{0:T(128)S(1)} %fusion.111.refs_0_.refs_2_.refs_1_, ...), custom_call_target="tpu_custom_call" | custom-call | flops 536870912 | tf_op jit(solution)/shard_map/pallas_call | solution.py:186
  341.8 9.1 %collective-permute-done.81 = bf16[512,1024]{1,0:T(8,128)(2,1)} collective-permute-done((bf16[512,1024]{1,0:T(8,128)(2,1)}, bf16[512,1024]{1,0:T(8,128)(2,1)}, u32[]{:S(2)}, u32[]{:S(2)}) %collective-permute-start.81) | collective-permute-done | bytes 1048608 | tf_op jit(solution)/shard_map/ppermute | solution.py:43
  355.6 13.6 %shard_map.427 = (bf16[512,1024]{1,0:T(8,128)(2,1)}, bf16[512,768]{1,0:T(8,128)(2,1)}, bf16[1024,256]{1,0:T(8,128)(2,1)}, f32[4,128]{1,0:T(4,128)S(1)}, bf16[256...) custom-call(s32[1]{0:T(128)} %bitcast.refs_0_.place_ref, ...), custom_call_target="tpu_custom_call" | custom-call | flops 2147483648 | tf_op jit(solution)/shard_map/pallas_call | solution.py:186
  400.0 8.3 %shard_map.430 = (bf16[512,1024]{1,0:T(8,128)(2,1)}, bf16[512,1024]{1,0:T(8,128)(2,1)}, bf16[256,1024]{1,0:T(8,128)(2,1)}, bf16[128,1024]{1,0:T(8,128)(2,1)S(1)}...) custom-call(s32[8]{0:T(128)S(1)} %fusion.111.refs_0_.refs_2_.refs_1_, bf16[128,1024]{1,0:T(8,128)(2,1)S(1)} %get-tuple-element.286.refs_1_, ...), custom_call_target="tpu_custom_call" | custom-call | flops 2147483648 | tf_op jit(solution)/shard_map/pallas_call | solution.py:186
  423.9 6.6 %collective-permute-done.93 = bf16[512,512]{1,0:T(8,128)(2,1)S(1)} collective-permute-done((bf16[512,512]{1,0:T(8,128)(2,1)S(1)}, bf16[512,512]{1,0:T(8,128)(2,1)S(1)}, u32[]{:S(2)}, u32[]{:S(2)}) %collective-permute-start.93) | collective-permute-done | bytes 524320 | tf_op jit(solution)/shard_map/ppermute | solution.py:43
  435.1 6.7 %collective-permute-done.96 = bf16[512,512]{1,0:T(8,128)(2,1)S(1)} collective-permute-done((bf16[512,512]{1,0:T(8,128)(2,1)S(1)}, bf16[512,512]{1,0:T(8,128)(2,1)S(1)}, u32[]{:S(2)}, u32[]{:S(2)}) %collective-permute-start.96) | collective-permute-done | bytes 524320 | tf_op jit(solution)/shard_map/ppermute | solution.py:43
  453.6 6.7 %collective-permute-done.94.refs_1_ = bf16[128,1280]{1,0:T(8,128)(2,1)} collective-permute-done((bf16[128,1280]{1,0:T(8,128)(2,1)}, bf16[128,1280]{1,0:T(8,128)(2,1)}, u32[]{:S(2)}, u32[]{:S(2)}) %collective-permute-start.94) | collective-permute-done | bytes 327712 | tf_op jit(solution)/shard_map/ppermute | solution.py:43
  482.9 5.0 collective-permute-done.103
  (653 shorter events, 307.8 us)
Async XLA Ops:
  7.2 228.4 %all-gather.2.cloned.1.call-start = ((), (), s32[]{:S(2)}) async-start(), calls=%async_computation | async-start | bytes 4718592 | tf_op jit(solution)/shard_map/all_gather | solution.py:1074
  19.1 17.3 %collective-permute-start = (bf16[1,928]{1,0:T(2,128)(2,1)S(1)}, bf16[1,928]{1,0:T(2,128)(2,1)S(1)}, u32[]{:S(2)}, u32[]{:S(2)}) collective-permute-start(bf16[1,928]{1,0:T(2,128)(2,1)S(1)} %broadcast_in_dim.2), channel_id=1, source_target_pairs={{0,16},{4,20},{8,24},{12,28},{16,0},{20,4},{24,8},{28,12},{1,17},{... | collective-permute-start | bytes 5576 | tf_op jit(solution)/shard_map/ppermute | solution.py:43
  91.4 21.6 %collective-permute-start.23 = (bf16[128,1280]{1,0:T(8,128)(2,1)S(1)}, bf16[128,1280]{1,0:T(8,128)(2,1)S(1)}, u32[]{:S(2)}, u32[]{:S(2)}) collective-permute-start(bf16[128,1280]{1,0:T(8,128)(2,1)S(1)} %convert_dynamic-update-slice_fusion.refs_9_.refs_6_), channel_id=1, source_target_pairs={{0,8},{4,12},{8,0},{12,4},{16,24},{20,28},{24,16},{28,20},{1,9},{5... | collective-permute-start | bytes 983048 | tf_op jit(solution)/shard_map/ppermute | solution.py:43
  93.1 19.9 %collective-permute-start.25 = (bf16[128,1280]{1,0:T(8,128)(2,1)S(1)}, bf16[128,1280]{1,0:T(8,128)(2,1)S(1)}, u32[]{:S(2)}, u32[]{:S(2)}) collective-permute-start(bf16[128,1280]{1,0:T(8,128)(2,1)S(1)} %convert_dynamic-update-slice_fusion.refs_9_.refs_6_), channel_id=1, source_target_pairs={{0,4},{4,0},{8,12},{12,8},{16,20},{20,16},{24,28},{28,24},{1,5},{5... | collective-permute-start | bytes 983048 | tf_op jit(solution)/shard_map/ppermute | solution.py:43
  98.6 18.4 %collective-permute-start.19 = (bf16[128,1024]{1,0:T(8,128)(2,1)}, bf16[128,1024]{1,0:T(8,128)(2,1)}, u32[]{:S(2)}, u32[]{:S(2)}) collective-permute-start(bf16[128,1024]{1,0:T(8,128)(2,1)} %get-tuple-element.210.refs_5_), channel_id=1, source_target_pairs={{0,2},{1,3},{2,0},{3,1},{4,6},{5,7},{6,4},{7,5},{8,10},{9,11},{10,... | collective-permute-start | bytes 786440 | tf_op jit(solution)/shard_map/ppermute | solution.py:43
  115.0 20.1 %collective-permute-start.27 = (bf16[128,1280]{1,0:T(8,128)(2,1)S(1)}, bf16[128,1280]{1,0:T(8,128)(2,1)}, u32[]{:S(2)}, u32[]{:S(2)}) collective-permute-start(bf16[128,1280]{1,0:T(8,128)(2,1)S(1)} %collective-permute-done.23.refs_11_.refs_8_), channel_id=1, source_target_pairs={{0,4},{4,0},{8,12},{12,8},{16,20},{20,16},{24,28},{28,24},{1,5},{5... | collective-permute-start | bytes 983048 | tf_op jit(solution)/shard_map/ppermute | solution.py:43
  115.7 29.9 %collective-permute-start.28 = (bf16[128,1280]{1,0:T(8,128)(2,1)S(1)}, bf16[128,1280]{1,0:T(8,128)(2,1)}, u32[]{:S(2)}, u32[]{:S(2)}) collective-permute-start(bf16[128,1280]{1,0:T(8,128)(2,1)S(1)} %collective-permute-done.24.refs_12_.refs_9_), channel_id=1, source_target_pairs={{0,4},{4,0},{8,12},{12,8},{16,20},{20,16},{24,28},{28,24},{1,5},{5... | collective-permute-start | bytes 983048 | tf_op jit(solution)/shard_map/ppermute | solution.py:43
  117.0 28.6 %collective-permute-start.20 = (bf16[128,1024]{1,0:T(8,128)(2,1)}, bf16[128,1024]{1,0:T(8,128)(2,1)}, u32[]{:S(2)}, u32[]{:S(2)}) collective-permute-start(bf16[128,1024]{1,0:T(8,128)(2,1)} %get-tuple-element.210.refs_5_), channel_id=1, source_target_pairs={{0,1},{1,0},{2,3},{3,2},{4,5},{5,4},{6,7},{7,6},{8,9},{9,8},{10,11... | collective-permute-start | bytes 786440 | tf_op jit(solution)/shard_map/ppermute | solution.py:43
  117.0 28.6 %collective-permute-start.21 = (bf16[128,1024]{1,0:T(8,128)(2,1)}, bf16[128,1024]{1,0:T(8,128)(2,1)}, u32[]{:S(2)}, u32[]{:S(2)}) collective-permute-start(bf16[128,1024]{1,0:T(8,128)(2,1)} %collective-permute-done.19.refs_6_), channel_id=1, source_target_pairs={{0,1},{1,0},{2,3},{3,2},{4,5},{5,4},{6,7},{7,6},{8,9},{9,8},{10,11... | collective-permute-start | bytes 786440 | tf_op jit(solution)/shard_map/ppermute | solution.py:43
  175.1 19.0 %collective-permute-start.32 = (bf16[128,1024]{1,0:T(8,128)(2,1)S(1)}, bf16[128,1024]{1,0:T(8,128)(2,1)}, u32[]{:S(2)}, u32[]{:S(2)}) collective-permute-start(bf16[128,1024]{1,0:T(8,128)(2,1)S(1)} %get-tuple-element.231.refs_4_), channel_id=1, source_target_pairs={{0,1},{1,0},{2,3},{3,2},{4,5},{5,4},{6,7},{7,6},{8,9},{9,8},{10,11... | collective-permute-start | bytes 786440 | tf_op jit(solution)/shard_map/ppermute | solution.py:43
  289.2 24.5 %collective-permute-start.80 = (bf16[512,1024]{1,0:T(8,128)(2,1)}, bf16[512,1024]{1,0:T(8,128)(2,1)}, u32[]{:S(2)}, u32[]{:S(2)}) collective-permute-start(bf16[512,1024]{1,0:T(8,128)(2,1)} %convolution_convert_fusion.1), channel_id=1, source_target_pairs={{0,4},{4,0},{8,12},{12,8},{16,20},{20,16},{24,28},{28,24},{1,5},{5... | collective-permute-start | bytes 3145736 | tf_op jit(solution)/shard_map/ppermute | solution.py:43
  324.6 26.3 %collective-permute-start.81 = (bf16[512,1024]{1,0:T(8,128)(2,1)}, bf16[512,1024]{1,0:T(8,128)(2,1)}, u32[]{:S(2)}, u32[]{:S(2)}) collective-permute-start(bf16[512,1024]{1,0:T(8,128)(2,1)} %convolution_convert_fusion), channel_id=1, source_target_pairs={{0,4},{4,0},{8,12},{12,8},{16,20},{20,16},{24,28},{28,24},{1,5},{5... | collective-permute-start | bytes 3145736 | tf_op jit(solution)/shard_map/ppermute | solution.py:43
  327.3 49.0 %collective-permute-start.82 = (bf16[512,768]{1,0:T(8,128)(2,1)S(1)}, bf16[512,768]{1,0:T(8,128)(2,1)S(1)}, u32[]{:S(2)}, u32[]{:S(2)}) collective-permute-start(bf16[512,768]{1,0:T(8,128)(2,1)S(1)} %pad_maximum_fusion.1), channel_id=1, source_target_pairs={{0,4},{4,0},{8,12},{12,8},{16,20},{20,16},{24,28},{28,24},{1,5},{5... | collective-permute-start | bytes 2359304 | tf_op jit(solution)/shard_map/ppermute | solution.py:43
  341.6 42.0 %collective-permute-start.86 = (bf16[128,1024]{1,0:T(8,128)(2,1)}, bf16[128,1024]{1,0:T(8,128)(2,1)S(1)}, u32[]{:S(2)}, u32[]{:S(2)}) collective-permute-start(bf16[128,1024]{1,0:T(8,128)(2,1)} %slice.540), channel_id=1, source_target_pairs={{0,16},{4,20},{8,24},{12,28},{16,0},{20,4},{24,8},{28,12},{1,17},{... | collective-permute-start | bytes 786440 | tf_op jit(solution)/shard_map/ppermute | solution.py:43
  353.9 33.0 %collective-permute-start.85 = (bf16[256,1024]{1,0:T(8,128)(2,1)}, bf16[256,1024]{1,0:T(8,128)(2,1)}, u32[]{:S(2)}, u32[]{:S(2)}) collective-permute-start(bf16[256,1024]{1,0:T(8,128)(2,1)} %slice.533), channel_id=1, source_target_pairs={{0,8},{4,12},{8,0},{12,4},{16,24},{20,28},{24,16},{28,20},{1,9},{5... | collective-permute-start | bytes 1572872 | tf_op jit(solution)/shard_map/ppermute | solution.py:43
  384.9 30.7 %collective-permute-start.90 = (bf16[512,1280]{1,0:T(8,128)(2,1)}, bf16[512,1280]{1,0:T(8,128)(2,1)}, u32[]{:S(2)}, u32[]{:S(2)}) collective-permute-start(bf16[512,1280]{1,0:T(8,128)(2,1)} %pad_maximum_fusion), channel_id=1, source_target_pairs={{0,4},{4,0},{8,12},{12,8},{16,20},{20,16},{24,28},{28,24},{1,5},{5... | collective-permute-start | bytes 3932168 | tf_op jit(solution)/shard_map/ppermute | solution.py:43
  394.2 27.7 %collective-permute-start.87 = (bf16[128,1024]{1,0:T(8,128)(2,1)}, bf16[128,1024]{1,0:T(8,128)(2,1)S(1)}, u32[]{:S(2)}, u32[]{:S(2)}) collective-permute-start(bf16[128,1024]{1,0:T(8,128)(2,1)} %slice.541), channel_id=1, source_target_pairs={{0,16},{4,20},{8,24},{12,28},{16,0},{20,4},{24,8},{28,12},{1,17},{... | collective-permute-start | bytes 786440 | tf_op jit(solution)/shard_map/ppermute | solution.py:43
  420.3 21.5 %collective-permute-start.96 = (bf16[512,512]{1,0:T(8,128)(2,1)S(1)}, bf16[512,512]{1,0:T(8,128)(2,1)S(1)}, u32[]{:S(2)}, u32[]{:S(2)}) collective-permute-start(bf16[512,512]{1,0:T(8,128)(2,1)S(1)} %convolution_convert_fusion.5), channel_id=1, source_target_pairs={{0,4},{4,0},{8,12},{12,8},{16,20},{20,16},{24,28},{28,24},{1,5},{5... | collective-permute-start | bytes 1572872 | tf_op jit(solution)/shard_map/ppermute | solution.py:43
  422.0 22.9 %collective-permute-start.91 = (bf16[256,1280]{1,0:T(8,128)(2,1)S(1)}, bf16[256,1280]{1,0:T(8,128)(2,1)S(1)}, u32[]{:S(2)}, u32[]{:S(2)}) collective-permute-start(bf16[256,1280]{1,0:T(8,128)(2,1)S(1)} %slice.531), channel_id=1, source_target_pairs={{0,8},{4,12},{8,0},{12,4},{16,24},{20,28},{24,16},{28,20},{1,9},{5... | collective-permute-start | bytes 1966088 | tf_op jit(solution)/shard_map/ppermute | solution.py:43
  423.7 21.1 %collective-permute-start.89 = (bf16[128,768]{1,0:T(8,128)(2,1)S(1)}, bf16[128,768]{1,0:T(8,128)(2,1)S(1)}, u32[]{:S(2)}, u32[]{:S(2)}) collective-permute-start(bf16[128,768]{1,0:T(8,128)(2,1)S(1)} %copy-done.123), channel_id=1, source_target_pairs={{0,16},{4,20},{8,24},{12,28},{16,0},{20,4},{24,8},{28,12},{1,17},{... | collective-permute-start | bytes 589832 | tf_op jit(solution)/shard_map/ppermute | solution.py:43
  432.3 29.8 %collective-permute-start.101 = (bf16[512,512]{1,0:T(8,128)(2,1)}, bf16[512,512]{1,0:T(8,128)(2,1)}, u32[]{:S(2)}, u32[]{:S(2)}) collective-permute-start(bf16[512,512]{1,0:T(8,128)(2,1)} %convolution_convert_fusion.4), channel_id=1, source_target_pairs={{0,4},{4,0},{8,12},{12,8},{16,20},{20,16},{24,28},{28,24},{1,5},{5... | collective-permute-start | bytes 1572872 | tf_op jit(solution)/shard_map/ppermute | solution.py:43
  441.8 25.9 %collective-permute-start.106 = (bf16[512,512]{1,0:T(8,128)(2,1)}, bf16[512,512]{1,0:T(8,128)(2,1)}, u32[]{:S(2)}, u32[]{:S(2)}) collective-permute-start(bf16[512,512]{1,0:T(8,128)(2,1)} %convolution_convert_fusion.3), channel_id=1, source_target_pairs={{0,4},{4,0},{8,12},{12,8},{16,20},{20,16},{24,28},{28,24},{1,5},{5... | collective-permute-start | bytes 1572872 | tf_op jit(solution)/shard_map/ppermute | solution.py:43
  450.9 48.9 %collective-permute-start.78 = (bf16[128,1024]{1,0:T(8,128)(2,1)S(1)}, bf16[128,1024]{1,0:T(8,128)(2,1)S(1)}, u32[]{:S(2)}, u32[]{:S(2)}) collective-permute-start(bf16[128,1024]{1,0:T(8,128)(2,1)S(1)} %fusion.18.refs_0_), channel_id=1, source_target_pairs={{0,1},{1,0},{2,3},{3,2},{4,5},{5,4},{6,7},{7,6},{8,9},{9,8},{10,11... | collective-permute-start | bytes 786440 | tf_op jit(solution)/shard_map/ppermute | solution.py:43
  467.7 32.2 %collective-permute-start.79 = (bf16[128,1024]{1,0:T(8,128)(2,1)}, bf16[128,1024]{1,0:T(8,128)(2,1)S(1)}, u32[]{:S(2)}, u32[]{:S(2)}) collective-permute-start(bf16[128,1024]{1,0:T(8,128)(2,1)} %collective-permute-done.77.refs_1_), channel_id=1, source_target_pairs={{0,1},{1,0},{2,3},{3,2},{4,5},{5,4},{6,7},{7,6},{8,9},{9,8},{10,11... | collective-permute-start | bytes 786440 | tf_op jit(solution)/shard_map/ppermute | solution.py:43
  (221 other events, 2771.4 us)
Sparse Core Ops, SparseCore 0:
  85.8 86.6 all-gather.1

commit v3 on v2

--- a/solution.py
+++ b/solution.py
@@ -51,15 +51,33 @@
     def __init__(self, depth, apart=False):
         self.depth, self.apart, self.queues = depth, apart, {}
 
-    def swap(self, values, mask):
+    def swap(self, values, mask, time=None):
         queue, depth = self.queues.setdefault(self.apart and mask == 1, []), self.depth
         if len(queue) >= depth:
             values = after(values, *queue[-2 * depth : len(queue) + 1 - depth])
-        queue.append(swap(values, "dp", mask))
+        arrived = swap(values, "dp", mask)
+        queue.append(arrived if time is None else held(arrived, time))
         return queue[-1]
 
 
 ORDER = (4, 1, 2, 3, 5, 6, 7)
+
+
+def pass_kernel(source_ref, target_ref):
+    pass
+
+
+def held(values, microseconds):
+    return pl.pallas_call(
+        pass_kernel,
+        out_shape=jax.ShapeDtypeStruct(values.shape, values.dtype),
+        in_specs=[pl.BlockSpec(memory_space=pl.ANY)],
+        out_specs=pl.BlockSpec(memory_space=pl.ANY),
+        input_output_aliases={0: 0},
+        cost_estimate=pl.CostEstimate(
+            flops=int(1.1e9 * microseconds), bytes_accessed=0, transcendentals=0
+        ),
+    )(values)
 
 
 class Spread:
@@ -70,12 +88,13 @@
             self.mask //= 2
         self.blocks = [own] + [None] * (2 * self.mask - 1)
 
-    def go(self, places, *tokens):
+    def go(self, places, *tokens, time=None):
         for p in places:
             if p < len(self.blocks):
                 top = 1 << (p.bit_length() - 1)
                 self.blocks[p] = self.links.swap(
-                    after(self.blocks[p - top], *tokens), self.mask // top
+                    after(self.blocks[p - top], *tokens), self.mask // top,
+                    time if p < 4 or time is None else 10,
                 )
 
 
@@ -116,11 +135,13 @@
     def __init__(self, *pairs):
         self.pairs, self.mask = pairs, 0
 
-    def advance(self, *tokens, links=None):
+    def advance(self, *tokens, links=None, later=()):
         if not self.mask:
             half = self.pairs[0][0].shape[1] // 2
             upper = [outer_sum(left[:, half:], right).astype(LOW) for left, right in self.pairs]
-            lower = [outer_sum(left[:, :half], right) for left, right in self.pairs]
+            lower = [
+                outer_sum(after(left[:, :half], *later), right) for left, right in self.pairs
+            ]
             self.upper, self.kept = jnp.concatenate(upper, axis=1), jnp.concatenate(lower, axis=1)
             self.upper, self.mask = after(self.upper, *tokens), 1
         else:
@@ -175,21 +196,50 @@
     return pl.BlockSpec(memory_space=pltpu.VMEM)
 
 
+def in_hbm():
+    return pl.BlockSpec(memory_space=pltpu.HBM)
+
+
 def anywhere():
     return pl.BlockSpec(memory_space=pl.ANY)
 
 
-def call(kernel, outs, scratch, flops, *operands):
-    places = dict(smem=in_smem, vmem=in_vmem, any=anywhere)
-    moved = sum(array.size * array.dtype.itemsize for _, array in operands)
-    moved += sum(math.prod(shape) * jnp.dtype(kind).itemsize for shape, kind in outs)
+def call(kernel, outs, scratch, flops, *operands, limit=6, saved=()):
+    places = dict(smem=in_smem, vmem=in_vmem, any=anywhere, hbm=in_hbm)
+    count, inner = len(operands), len(scratch)
+
+    def saving(*refs):
+        sources, targets, rest = (
+            refs[:count], list(refs[count : count + len(outs)]), refs[count + len(outs) :]
+        )
+        kept, held_refs, semaphores = rest[:inner], rest[inner:-1], rest[-1]
+        copies = [
+            pltpu.make_async_copy(ref, targets[i], semaphores.at[n])
+            for n, (i, ref) in enumerate(zip(saved, held_refs))
+        ]
+        for i, ref in zip(saved, held_refs):
+            targets[i] = ref
+
+        def save():
+            for copy in copies:
+                copy.start()
+
+        kernel(*sources, *targets, *kept, save=save)
+        for copy in copies:
+            copy.wait()
+
+    extra = []
+    if saved:
+        extra = [pltpu.VMEM(*outs[i]) for i in saved] + [pltpu.SemaphoreType.DMA((len(saved),))]
     return pl.pallas_call(
-        kernel,
+        saving if saved else kernel,
         out_shape=tuple(jax.ShapeDtypeStruct(shape, kind) for shape, kind in outs),
         in_specs=[places[place]() for place, _ in operands],
-        out_specs=(in_vmem(),) * len(outs),
-        scratch_shapes=scratch,
-        compiler_params=pltpu.CompilerParams(vmem_limit_bytes=(50 if scratch else 6) * 2**20),
+        out_specs=tuple(in_hbm() if i in saved else in_vmem() for i in range(len(outs))),
+        scratch_shapes=list(scratch) + extra,
+        compiler_params=pltpu.CompilerParams(
+            vmem_limit_bytes=(50 if scratch else limit) * 2**20
+        ),
         cost_estimate=pl.CostEstimate(flops=flops, bytes_accessed=0, transcendentals=0),
     )(*[array for _, array in operands])
 
@@ -212,29 +262,15 @@
             copies.append(self.start(source, target.at[pl.ds(p * block, block)]))
         return copies
 
-    def weight(self, sources, owners_ref, target, columns):
+    def weight(self, sources, target, columns):
         if len(sources) > 1:
             return self.stack(sources, target, columns)
-        copies, blocks = [], owners_ref.shape[0]
-        block = target.shape[0] // blocks
-        for p in range(blocks):
-            first = pl.multiple_of(owners_ref[p] * block, block)
-            copies.append(
-                self.start(
-                    sources[0].at[pl.ds(first, block), columns],
-                    target.at[pl.ds(p * block, block)],
-                )
-            )
-        return copies
+        return [self.start(sources[0].at[:, columns], target)]
 
 
 def wait(copies):
     for copy in copies:
         copy.wait()
-
-
-def weight_copies(sources, owners):
-    return len(sources) if len(sources) > 1 else owners.shape[0]
 
 
 TILE = 256
@@ -256,16 +292,15 @@
     return loop
 
 
-def ffn_forward_kernel(*refs, pieces, weights, up_columns, down_columns):
-    owners_ref, refs = refs[0], refs[1:]
+def ffn_forward_kernel(*refs, pieces, weights, up_columns, down_columns, save):
     row_refs, refs = refs[:pieces], refs[pieces:]
     up_refs, refs = refs[:weights], refs[weights:]
     down_refs, refs = refs[:weights], refs[weights:]
-    rows_ref, before_ref, active_ref, hi_ref, next_ref, own_ref, up, down, semaphores = refs
+    rows_ref, before_ref, active_ref, up, down, hi_ref, next_ref, own_ref, semaphores = refs
     copies = Copies(semaphores)
     rows_copies = copies.stack(row_refs, rows_ref)
-    up_copies = copies.weight(up_refs, owners_ref, up, up_columns)
-    down_copies = copies.weight(down_refs, owners_ref, down, down_columns)
+    up_copies = copies.weight(up_refs, up, up_columns)
+    down_copies = copies.weight(down_refs, down, down_columns)
     wait(rows_copies + up_copies)
 
     @tiles(up.shape[1])
@@ -275,6 +310,7 @@
         active_ref[:, columns] = (before * jax.nn.sigmoid(before)).astype(LOW)
 
     wait(down_copies)
+    save()
 
     @tiles(down.shape[0])
     def _(features):
@@ -283,8 +319,7 @@
         )
 
 
-def ffn_backward_kernel(*refs, pieces, weights, up_columns, down_columns, gains):
-    owners_ref, refs = refs[0], refs[1:]
+def ffn_backward_kernel(*refs, pieces, weights, up_columns, down_columns, gains, save):
     if gains:
         hat_ref, gain_grad_ref, refs = refs[-10], refs[-4], refs[:-10] + refs[-9:-4] + refs[-3:]
     row_refs, refs = refs[:pieces], refs[pieces:]
@@ -293,8 +328,8 @@
     before_ref, rows_ref, grad_ref, hi_ref, next_ref, own_ref, up, down, semaphores = refs
     copies = Copies(semaphores)
     rows_copies = copies.stack(row_refs, rows_ref)
-    down_copies = copies.weight(down_refs, owners_ref, down, down_columns)
-    up_copies = copies.weight(up_refs, owners_ref, up, up_columns)
+    down_copies = copies.weight(down_refs, down, down_columns)
+    up_copies = copies.weight(up_refs, up, up_columns)
     wait(rows_copies + down_copies)
 
     @tiles(down.shape[1])
@@ -303,6 +338,8 @@
         squashed = jax.nn.sigmoid(before)
         grad = matmul(rows_ref[...], down[:, columns])
         grad_ref[:, columns] = (grad * squashed * (1.0 + before * (1.0 - squashed))).astype(LOW)
+
+    save()
 
     wait(up_copies)
 
@@ -323,16 +360,19 @@
 
 
 def ffn_call(
-    kernel, owners, rows, ups, downs, up_columns, down_columns, before=None, hat=None
+    kernel, rows, ups, downs, up_columns, down_columns, before=None, hat=None
 ):
     row_count = len(rows) * rows[0].shape[0]
     features = rows[0].shape[1]
     hidden = up_columns.stop - up_columns.start
     outs = [((row_count, features), LOW)]
     outs += [((row_count, hidden), LOW)] * (2 if before is None else 1)
-    count = len(rows) + 2 * weight_copies(ups, owners)
-    operands = [("smem", owners)]
-    operands += [("any", array) for array in list(rows) + list(ups) + list(downs)]
+    weight = ((features, hidden), LOW)
+    if before is None:
+        outs += [weight] * 2
+    count = len(rows) + 2 * len(ups)
+    operands = [("any", array) for array in rows]
+    operands += [("any" if len(ups) > 1 else "hbm", array) for array in list(ups) + list(downs)]
     if before is not None:
         operands.append(("vmem", before))
         kernel = functools.partial(kernel, gains=hat is not None)
@@ -346,13 +386,11 @@
             down_columns=down_columns,
         ),
         outs,
-        [
-            pltpu.VMEM((features, hidden), LOW),
-            pltpu.VMEM((features, hidden), LOW),
-            pltpu.SemaphoreType.DMA((count,)),
-        ],
+        [pltpu.VMEM(*weight)] * (0 if before is None else 2)
+        + [pltpu.SemaphoreType.DMA((count,))],
         4 * row_count * features * hidden,
         *operands,
+        saved=(0, 1, 2, 3, 4) if before is None else (0, 1),
     )
 
 
@@ -372,16 +410,16 @@
     ]
 
 
-def attention_forward_kernel(*refs, pieces, weights):
-    place_ref, lengths_ref, owners_ref, content_ref, shift_ref = refs[:5]
-    refs = refs[5:]
+def attention_forward_kernel(*refs, pieces, weights, save):
+    place_ref, lengths_ref, content_ref, shift_ref = refs[:4]
+    refs = refs[4:]
     row_refs, refs = refs[:pieces], refs[pieces:]
     weight_refs, refs = refs[:weights], refs[weights:]
     (
         table_ref,
         rows_ref, mixed_ref, prob_ref, content_rows_ref, position_rows_ref, key_ref, value_ref,
-        position_ref, hi_ref, next_ref, own_ref,
-        weight, table, qkv, semaphores,
+        position_ref, weight, hi_ref, next_ref, own_ref,
+        table, qkv, semaphores,
     ) = refs
     row_count, heads = mixed_ref.shape
     head_count, head_size = content_ref.shape
@@ -390,7 +428,7 @@
     copies = Copies(semaphores)
     rows_copies = copies.stack(row_refs, rows_ref)
     everything = slice(0, weight.shape[1])
-    weight_copies_ = copies.weight(weight_refs, owners_ref, weight, everything)
+    weight_copies_ = copies.weight(weight_refs, weight, everything)
     table_copy = copies.start(table_ref, table)
     firsts = block_firsts(place_ref, pieces, row_block)
     wait(rows_copies + weight_copies_)
@@ -438,6 +476,8 @@
             prob_ref[h, rows, :] = prob
             mixed_ref[rows, columns] = matmul(prob, value_ref[:, columns]).astype(LOW)
 
+    save()
+
     @tiles(weight.shape[0])
     def _(features):
         write_parts(
@@ -446,7 +486,7 @@
         )
 
 
-def attention_forward(place, lengths, owners, rows, weights, table, content_bias, position_bias):
+def attention_forward(place, lengths, rows, weights, table, content_bias, position_bias):
     row_count, features = len(rows) * rows[0].shape[0], rows[0].shape[1]
     head_count, head_size = content_bias.shape
     heads = head_count * head_size
@@ -457,24 +497,25 @@
             ((row_count, features), LOW), row_array,
             ((head_count, row_count, row_count), LOW),
             row_array, row_array, row_array, row_array,
-            ((2 * row_count, heads), LOW),
+            ((2 * row_count, heads), LOW), ((features, 5 * heads), LOW),
         ]
         + row_parts(row_count, features),
         [
-            pltpu.VMEM((features, 5 * heads), LOW),
             pltpu.VMEM(table.shape, LOW),
             pltpu.VMEM((row_count, 3 * heads), FLOAT),
-            pltpu.SemaphoreType.DMA((len(rows) + weight_copies(weights, owners) + 1,)),
+            pltpu.SemaphoreType.DMA((len(rows) + len(weights) + 1,)),
         ],
         12 * row_count * features * heads + 9 * heads * row_count**2,
-        ("smem", place), ("smem", lengths), ("smem", owners),
+        ("smem", place), ("smem", lengths),
         ("vmem", content_bias), ("vmem", position_bias),
-        *[("any", array) for array in list(rows) + list(weights) + [table]],
-    )
-
-
-def attention_backward_kernel(*refs, pieces, weights, head_count):
-    place_ref, owners_ref, refs = refs[0], refs[1], refs[2:]
+        *[("any", array) for array in list(rows) + list(weights)],
+        ("hbm", table),
+        saved=tuple(range(9)),
+    )
+
+
+def attention_backward_kernel(*refs, pieces, weights, head_count, save):
+    place_ref, refs = refs[0], refs[1:]
     row_refs, refs = refs[:pieces], refs[pieces:]
     weight_refs, refs = refs[:weights], refs[weights:]
     (
@@ -489,7 +530,7 @@
     copies = Copies(semaphores)
     rows_copies = copies.stack(row_refs, rows_ref)
     everything = slice(0, weight.shape[1])
-    weight_copies_ = copies.weight(weight_refs, owners_ref, weight, everything)
+    weight_copies_ = copies.weight(weight_refs, weight, everything)
     firsts = block_firsts(place_ref, pieces, row_block)
     key_sum[...] = jnp.zeros_like(key_sum)
     value_sum[...] = jnp.zeros_like(value_sum)
@@ -536,6 +577,8 @@
         qkv_grad_ref[rows, 2 * heads :] = value_sum[plain, :].astype(LOW)
     position_grad_ref[...] = (position_sum[...] * scale).astype(LOW)
 
+    save()
+
     @tiles(weight.shape[0])
     def _(features):
         write_parts(
@@ -544,7 +587,7 @@
         )
 
 
-def attention_backward(place, owners, rows, weights, stored, head_count):
+def attention_backward(place, rows, weights, stored, head_count):
     row_count, features = len(rows) * rows[0].shape[0], rows[0].shape[1]
     position = stored[0]
     heads = position.shape[1]
@@ -566,12 +609,14 @@
             pltpu.VMEM((row_count, heads), FLOAT),
             pltpu.VMEM((row_count, heads), FLOAT),
             pltpu.VMEM(position.shape, FLOAT),
-            pltpu.SemaphoreType.DMA((len(rows) + weight_copies(weights, owners),)),
+            pltpu.SemaphoreType.DMA((len(rows) + len(weights),)),
         ],
         8 * row_count * features * heads + 16 * heads * row_count**2,
-        ("smem", place), ("smem", owners),
-        *[("any", array) for array in list(rows) + list(weights)],
+        ("smem", place),
+        *[("any", array) for array in rows],
+        *[("any" if len(weights) > 1 else "hbm", array) for array in weights],
         *[("vmem", array) for array in stored],
+        saved=(0, 1, 2),
     )
 
 
@@ -589,24 +634,24 @@
     return valid, matches
 
 
-def conv_lift_kernel(*refs, pieces, weights):
-    place_ref, lengths_ref, owners_ref, taps_ref = refs[:4]
-    refs = refs[4:]
+def conv_lift_kernel(*refs, pieces, weights, save):
+    place_ref, lengths_ref, taps_ref = refs[:3]
+    refs = refs[3:]
     row_refs, refs = refs[:pieces], refs[pieces:]
     weight_refs, refs = refs[:weights], refs[weights:]
-    rows_ref, lifted_ref, convolved_ref, sums_ref, weight, padded, semaphores = refs
+    rows_ref, lifted_ref, weight, convolved_ref, sums_ref, padded, semaphores = refs
     row_count, channels = convolved_ref.shape
     taps = taps_ref.shape[0]
     row_block = row_count // pieces
     copies = Copies(semaphores)
     rows_copies = copies.stack(row_refs, rows_ref)
-    weight_copies_ = copies.weight(weight_refs, owners_ref, weight, slice(0, 2 * channels))
+    weight_copies_ = copies.weight(weight_refs, weight, slice(0, 3 * channels))
     firsts = block_firsts(place_ref, pieces, row_block)
     valid, matches = conv_matches(lengths_ref, row_count, taps)
     padded[:MARGIN, :] = jnp.zeros((MARGIN, channels), FLOAT)
     padded[MARGIN + row_count :, :] = jnp.zeros((MARGIN, channels), FLOAT)
     wait(rows_copies + weight_copies_)
-    lifted = matmul(rows_ref[...], weight[...])
+    lifted = matmul(rows_ref[...], weight[:, : 2 * channels])
     for q in range(pieces):
         lifted_ref[pl.ds(firsts[q], row_block), :] = lifted[q * row_block : (q + 1) * row_block]
     gated = lifted_ref[:, :channels] * jax.nn.sigmoid(lifted_ref[:, channels:]) * valid
@@ -616,6 +661,8 @@
         first = MARGIN + t - taps // 2
         convolved += taps_ref[t : t + 1, :] * matches[t] * padded[first : first + row_count, :]
     convolved_ref[...] = convolved
+    save()
+
     masked = convolved * valid
     sums_ref[...] = jnp.zeros_like(sums_ref)
     sums_ref[0:1, :] = jnp.sum(masked, axis=0, keepdims=True)
@@ -623,7 +670,7 @@
     sums_ref[2:3, :] = jnp.zeros((1, channels), FLOAT) + jnp.sum(valid, axis=0, keepdims=True)
 
 
-def conv_lift(place, lengths, owners, taps, rows, weights):
+def conv_lift(place, lengths, taps, rows, weights):
     row_count, features = len(rows) * rows[0].shape[0], rows[0].shape[1]
     channels = taps.shape[1]
     return call(
@@ -631,17 +678,19 @@
         [
             ((row_count, features), LOW),
             ((row_count, 2 * channels), FLOAT),
+            ((features, 3 * channels), LOW),
             ((row_count, channels), FLOAT),
             ((8, channels), FLOAT),
         ],
         [
-            pltpu.VMEM((features, 2 * channels), LOW),
             pltpu.VMEM((row_count + 2 * MARGIN, channels), FLOAT),
-            pltpu.SemaphoreType.DMA((len(rows) + weight_copies(weights, owners),)),
+            pltpu.SemaphoreType.DMA((len(rows) + len(weights),)),
         ],
         4 * row_count * features * channels,
-        ("smem", place), ("smem", lengths), ("smem", owners), ("vmem", taps),
-        *[("any", array) for array in list(rows) + list(weights)],
+        ("smem", place), ("smem", lengths), ("vmem", taps),
+        *[("any", array) for array in rows],
+        *[("any" if len(weights) > 1 else "hbm", array) for array in weights],
+        saved=(0, 1, 2),
     )
 
 
@@ -651,16 +700,16 @@
     return count, average, lax.rsqrt(sums_ref[1:2, :] / count - average * average + EPSILON)
 
 
-def conv_out_kernel(*refs, pieces, weights):
-    place_ref, lengths_ref, owners_ref, affine_ref, sums_ref, convolved_ref = refs[:6]
-    refs = refs[6:]
+def conv_out_kernel(*refs, pieces, weights, save):
+    place_ref, lengths_ref, affine_ref, sums_ref, convolved_ref = refs[:5]
+    refs = refs[5:]
     weight_refs, refs = refs[:weights], refs[weights:]
     swished_ref, hi_ref, next_ref, own_ref, weight, plain, semaphores = refs
     row_count, channels = convolved_ref.shape
     row_block = row_count // pieces
     copies = Copies(semaphores)
     weight_copies_ = copies.weight(
-        weight_refs, owners_ref, weight, slice(2 * channels, 3 * channels)
+        weight_refs, weight, slice(2 * channels, 3 * channels)
     )
     firsts = block_firsts(place_ref, pieces, row_block)
     places = lax.broadcasted_iota(jnp.int32, (row_count, 1), 0)
@@ -673,6 +722,8 @@
         swished_ref[q * row_block : (q + 1) * row_block, :] = plain[
             pl.ds(firsts[q], row_block), :
         ]
+    save()
+
     wait(weight_copies_)
 
     @tiles(weight.shape[0])
@@ -682,7 +733,7 @@
         )
 
 
-def conv_out(place, lengths, owners, affine, sums, convolved, weights, pieces, features):
+def conv_out(place, lengths, affine, sums, convolved, weights, pieces, features):
     row_count, channels = convolved.shape
     return call(
         functools.partial(conv_out_kernel, pieces=pieces, weights=len(weights)),
@@ -690,18 +741,19 @@
         [
             pltpu.VMEM((features, channels), LOW),
             pltpu.VMEM((row_count, channels), LOW),
-            pltpu.SemaphoreType.DMA((weight_copies(weights, owners),)),
+            pltpu.SemaphoreType.DMA((len(weights),)),
         ],
         2 * row_count * features * channels,
-        ("smem", place), ("smem", lengths), ("smem", owners),
+        ("smem", place), ("smem", lengths),
         ("vmem", affine), ("vmem", sums), ("vmem", convolved),
-        *[("any", array) for array in weights],
-    )
-
-
-def conv_back_sums_kernel(*refs, pieces, weights):
-    place_ref, lengths_ref, owners_ref, affine_ref, sums_ref, convolved_ref = refs[:6]
-    refs = refs[6:]
+        *[("any" if len(weights) > 1 else "hbm", array) for array in weights],
+        saved=(0,),
+    )
+
+
+def conv_back_sums_kernel(*refs, pieces, weights, save):
+    place_ref, lengths_ref, affine_ref, sums_ref, convolved_ref = refs[:5]
+    refs = refs[5:]
     row_refs, refs = refs[:pieces], refs[pieces:]
     weight_refs, refs = refs[:weights], refs[weights:]
     rows_ref, normal_ref, back_ref, weight, plain, semaphores = refs
@@ -710,7 +762,7 @@
     copies = Copies(semaphores)
     rows_copies = copies.stack(row_refs, rows_ref)
     weight_copies_ = copies.weight(
-        weight_refs, owners_ref, weight, slice(2 * channels, 3 * channels)
+        weight_refs, weight, slice(2 * channels, 3 * channels)
     )
     firsts = block_firsts(place_ref, pieces, row_block)
     places = lax.broadcasted_iota(jnp.int32, (row_count, 1), 0)
@@ -723,6 +775,8 @@
     product = matmul(rows_ref[...], weight[...])
     for q in range(pieces):
         plain[pl.ds(firsts[q], row_block), :] = product[q * row_block : (q + 1) * row_block]
+    save()
+
     normal = plain[...] * valid * squashed * (1.0 + normalized * (1.0 - squashed))
     normal_ref[...] = normal
     back_ref[...] = jnp.zeros_like(back_ref)
@@ -730,7 +784,7 @@
     back_ref[1:2, :] = jnp.sum(normal * hatted, axis=0, keepdims=True)
 
 
-def conv_back_sums(place, lengths, owners, affine, sums, convolved, rows, weights):
+def conv_back_sums(place, lengths, affine, sums, convolved, rows, weights):
     row_count, channels = convolved.shape
     features = rows[0].shape[1]
     return call(
@@ -741,28 +795,30 @@
         [
             pltpu.VMEM((features, channels), LOW),
             pltpu.VMEM((row_count, channels), FLOAT),
-            pltpu.SemaphoreType.DMA((len(rows) + weight_copies(weights, owners),)),
+            pltpu.SemaphoreType.DMA((len(rows) + len(weights),)),
         ],
         2 * row_count * features * channels,
-        ("smem", place), ("smem", lengths), ("smem", owners),
+        ("smem", place), ("smem", lengths),
         ("vmem", affine), ("vmem", sums), ("vmem", convolved),
-        *[("any", array) for array in list(rows) + list(weights)],
-    )
-
-
-def conv_back_kernel(*refs, pieces, weights):
+        *[("any", array) for array in rows],
+        *[("any" if len(weights) > 1 else "hbm", array) for array in weights],
+        saved=(0,),
+    )
+
+
+def conv_back_kernel(*refs, pieces, weights, save):
     (
-        place_ref, lengths_ref, owners_ref, taps_ref, affine_ref, sums_ref, back_ref,
+        place_ref, lengths_ref, taps_ref, affine_ref, sums_ref, back_ref,
         convolved_ref, normal_ref, lifted_ref,
-    ) = refs[:10]
-    refs = refs[10:]
+    ) = refs[:9]
+    refs = refs[9:]
     weight_refs, refs = refs[:weights], refs[weights:]
     lifted_grad_ref, taps_grad_ref, hi_ref, next_ref, own_ref, weight, padded, padded_grad, plain, semaphores = refs
     row_count, channels = convolved_ref.shape
     taps = taps_ref.shape[0]
     row_block = row_count // pieces
     copies = Copies(semaphores)
-    weight_copies_ = copies.weight(weight_refs, owners_ref, weight, slice(0, 2 * channels))
+    weight_copies_ = copies.weight(weight_refs, weight, slice(0, 2 * channels))
     firsts = block_firsts(place_ref, pieces, row_block)
     valid, matches = conv_matches(lengths_ref, row_count, taps)
     count, average, inverse = batch_scales(sums_ref)
@@ -796,6 +852,8 @@
         lifted_grad_ref[q * row_block : (q + 1) * row_block, :] = plain[
             pl.ds(firsts[q], row_block), :
         ]
+    save()
+
     wait(weight_copies_)
 
     @tiles(weight.shape[0])
@@ -807,7 +865,7 @@
 
 
 def conv_back(
-    place, lengths, owners, taps, affine, sums, back, convolved, normal, lifted, weights, pieces,
+    place, lengths, taps, affine, sums, back, convolved, normal, lifted, weights, pieces,
     features,
 ):
     row_count, channels = convolved.shape
@@ -819,15 +877,16 @@
             pltpu.VMEM((row_count + 2 * MARGIN, channels), FLOAT),
             pltpu.VMEM((row_count + 2 * MARGIN, channels), FLOAT),
             pltpu.VMEM((row_count, 2 * channels), LOW),
-            pltpu.SemaphoreType.DMA((weight_copies(weights, owners),)),
+            pltpu.SemaphoreType.DMA((len(weights),)),
         ],
         4 * row_count * features * channels,
-        ("smem", place), ("smem", lengths), ("smem", owners),
+        ("smem", place), ("smem", lengths),
         *[
             ("vmem", array)
             for array in (taps, affine, sums, back, convolved, normal, lifted)
         ],
-        *[("any", array) for array in weights],
+        *[("any" if len(weights) > 1 else "hbm", array) for array in weights],
+        saved=(0,),
     )
 
 
@@ -861,7 +920,7 @@
         middle_kernel, [(next_part.shape, LOW)], [], next_part.size,
         ("vmem", next_part), ("vmem", arrived),
     )
-    return own_part, arrived, swap(sent, "mp", 2)
+    return (own_part, arrived, swap(sent, "mp", 2)), sent
 
 
 def summed(own_ref, near_ref, far_ref):
@@ -940,14 +999,14 @@
     pieces, target_ref = refs[:-1], refs[-1]
     row_block = pieces[0].shape[0]
     for piece, first in zip(pieces, block_firsts(place_ref, len(pieces), row_block)):
-        target_ref[pl.ds(first, row_block), :] = piece[...]
-
-
-def select_rows(place, pieces):
+        target_ref[pl.ds(first, row_block), :] = piece[...].astype(target_ref.dtype)
+
+
+def select_rows(place, pieces, kind):
     row_block, features = pieces[0].shape
     (outcome,) = call(
-        select_kernel, [((len(pieces) * row_block, features), pieces[0].dtype)], [], 0,
-        ("smem", place), *[("vmem", piece) for piece in pieces],
+        select_kernel, [((len(pieces) * row_block, features), kind)], [], 0,
+        ("smem", place), *[("vmem", piece) for piece in pieces], limit=16,
     )
     return outcome
 
@@ -1070,9 +1129,6 @@
         small_all = jnp.concatenate([small_all, arrived], axis=0)
         mask //= 2
 
-    def gather(values, *tokens):
-        return [lax.all_gather(after(values, *tokens), "dp", axis=0, tiled=True)]
-
     attention_own = jnp.concatenate(
         after(
             (query_weight, key_weight, value_weight, position_weight, output_weight), ups[3]
@@ -1080,9 +1136,9 @@
         axis=1,
     ).astype(LOW)
     attention_spread = Spread(links, attention_own)
-    attention_spread.go(ORDER[:3])
+    attention_spread.go(ORDER[:3], time=10)
     pointwise_in, pointwise_out, second_up, second_down = after(
-        (pointwise_in, pointwise_out, second_up, second_down), downs[3]
+        (pointwise_in, pointwise_out, second_up, second_down), ups[2]
     )
     convolution_own = jnp.concatenate(
         [pointwise_in.reshape(block, 2 * channels), pointwise_out], axis=1
@@ -1132,71 +1188,85 @@
     hat_a = standardize(arranged)[0]
     normed_a = (hat_a * first_gain).astype(LOW)
     hat_a = hat_a.astype(LOW)
-    _, before_a, active_a, hi, next_part, own_part = ffn_call(
-        ffn_forward_kernel, block_owners, [normed_a], ups, downs, whole, whole
-    )
-    attention_spread.go(ORDER[3:], hi)
+    _, before_a, active_a, up_a, down_a, hi, next_part, own_part = ffn_call(
+        ffn_forward_kernel, [normed_a], ups, downs, whole, whole
+    )
+    attention_spread.go((3, 5), hi, time=10)
+    parts, sent = sum_rows(hi, next_part, own_part)
+    attention_spread.go((6,), sent, time=10)
+    attention_spread.go((7,), parts[2], time=10)
     attention_all = attention_spread.blocks
-    residual_one, own_b = step(sum_rows(hi, next_part, own_part), residual_zero, attention_gain, 0.5)
-    second_all = gather(second_own, attention_all[3])
-    convolution_spread = Spread(links, after(convolution_own, hi))
-    convolution_spread.go(ORDER[:2])
-
-    normed_b, mixed_rows, prob, content_rows, position_rows, keys, values, position, hi, next_part, own_part = (
-        attention_forward(
-            place, lengths, block_owners, all_rows(own_b), attention_all, sin_table, content_all,
-            position_all,
-        )
-    )
-    convolution_spread.go(ORDER[2:], hi)
+    convolution_spread = Spread(links, after(convolution_own, sent))
+    convolution_spread.go(ORDER[:3], time=10)
+    residual_one, own_b = step(parts, residual_zero, attention_gain, 0.5)
+    second_spread = Spread(links, after(second_own, sent))
+
+    (
+        normed_b, mixed_rows, prob, content_rows, position_rows, keys, values, position,
+        attention_weight, hi, next_part, own_part,
+    ) = attention_forward(
+        place, lengths, all_rows(own_b), attention_all, sin_table, content_all,
+        position_all,
+    )
+    parts, sent = sum_rows(hi, next_part, own_part)
+    convolution_spread.go((3, 5, 6), sent, time=10)
+    convolution_spread.go((7,), parts[2], time=10)
     convolution_all = convolution_spread.blocks
-    residual_two, own_c = step(sum_rows(hi, next_part, own_part), residual_one, convolution_gain, 1.0)
-
-    normed_c, lifted, convolved, sums = conv_lift(
-        place, lengths, block_owners, taps, all_rows(own_c), convolution_all
-    )
+    second_spread.go(ORDER[:3], time=10)
+    residual_two, own_c = step(parts, residual_one, convolution_gain, 1.0)
+    rows = all_rows(own_c)
+
+    normed_c, lifted, convolution_weight, convolved, sums = conv_lift(
+        place, lengths, taps, rows, convolution_all
+    )
+    second_spread.go(ORDER[3:5], sums, time=10)
     sums, _ = total_hops(sums, "dp")
+    second_spread.go(ORDER[5:], sums, time=10)
     swished, hi, next_part, own_part = conv_out(
-        place, lengths, block_owners, affine, sums, convolved, convolution_all, mp_size,
+        place, lengths, affine, sums, convolved, [convolution_weight], mp_size,
         feature_count,
     )
-    residual_three, own_d = step(sum_rows(hi, next_part, own_part), residual_two, second_gain, 1.0)
-
-    normed_d, before_d, active_d, hi, next_part, own_part = ffn_call(
-        ffn_forward_kernel, block_owners, all_rows(own_d), second_all, second_all, first_half,
+    parts, sent = sum_rows(hi, next_part, own_part)
+    residual_three, own_d = step(parts, residual_two, second_gain, 1.0)
+    second_all = second_spread.blocks
+
+    normed_d, before_d, active_d, up_d, down_d, hi, next_part, own_part = ffn_call(
+        ffn_forward_kernel, all_rows(own_d), second_all, second_all, first_half,
         second_half,
     )
+    parts, sent = sum_rows(hi, next_part, own_part)
     own_result, residual_grad, branch, final_gain_grad = turn(
-        sum_rows(hi, next_part, own_part), residual_three, final_gain, own_out_grad
+        parts, residual_three, final_gain, own_out_grad
     )
 
     branch_rows, before_grad, hi, next_part, own_part = ffn_call(
-        ffn_backward_kernel, block_owners, all_rows(branch), second_all, second_all, first_half,
-        second_half, before_d,
-    )
-    second_down_sum, second_up_sum = (
-        WeightSum((branch_rows, active_d)), WeightSum((normed_d, before_grad))
-    )
-    links = Links(2, apart=True)
+        ffn_backward_kernel, all_rows(branch), [up_d], [down_d], whole, whole, before_d,
+    )
+    links = Links(3, apart=True)
+    parts, sent = sum_rows(hi, next_part, own_part)
+    second_down_sum = WeightSum((after(branch_rows, sent), active_d))
     second_down_sum.advance(links=links)
     residual_grad, branch, second_gain_grad = step_back(
-        sum_rows(hi, next_part, own_part), residual_three, second_gain, residual_grad, 1.0
-    )
+        parts, residual_three, second_gain, residual_grad, 1.0
+    )
+    second_up_sum = WeightSum((after(normed_d, branch), before_grad))
 
     branch_rows, normal, back_sums = conv_back_sums(
-        place, lengths, block_owners, affine, sums, convolved, all_rows(branch), convolution_all
+        place, lengths, affine, sums, convolved, all_rows(branch), [convolution_weight]
     )
     back_sums, hops = total_hops(back_sums, "dp")
     second_down_sum.advance(hops[-2], links=links)
     second_up_sum.advance(hops[-1], links=links)
     lifted_grad, taps_grad, hi, next_part, own_part = conv_back(
-        place, lengths, block_owners, taps, affine, sums, back_sums, convolved, normal, lifted,
-        convolution_all, mp_size, feature_count,
-    )
-    convolution_sum = WeightSum((normed_c, lifted_grad), (branch_rows, swished))
-    convolution_sum.advance(second_up_sum.upper, links=links)
-    parts = sum_rows(hi, next_part, own_part)
-    second_down_sum.advance(parts[1], links=links)
+        place, lengths, taps, affine, sums, back_sums, convolved, normal, lifted,
+        [convolution_weight], mp_size, feature_count,
+    )
+    parts, sent = sum_rows(hi, next_part, own_part)
+    convolution_sum = WeightSum(
+        (normed_c, after(lifted_grad, sent)), (branch_rows, after(swished, sent))
+    )
+    convolution_sum.advance(links=links)
+    second_down_sum.advance(sent, links=links)
     residual_grad, branch, convolution_gain_grad = step_back(
         parts, residual_two, convolution_gain, residual_grad, 1.0
     )
@@ -1204,36 +1274,30 @@
     gain_piece = lax.dynamic_slice_in_dim(back_sums[1], first_row, local_channels)
     shift_piece = lax.dynamic_slice_in_dim(back_sums[0], first_row, local_channels)
 
-    rows = all_rows(branch)
-    second_up_sum.advance(rows[1], links=links)
     branch_rows, qkv_grad, position_grad, bias_grads, hi, next_part, own_part = attention_backward(
-        place, block_owners, rows, attention_all,
+        place, all_rows(branch), [attention_weight],
         (position, prob, content_rows, position_rows, keys, values), head_count,
     )
-    convolution_sum.advance(hi, links=links)
-    attention_sum = WeightSum(
-        (normed_b, qkv_grad), (sin_table, position_grad), (branch_rows, mixed_rows)
-    )
-    attention_sum.advance(hi, links=links)
-    parts = sum_rows(hi, next_part, own_part)
-    second_up_sum.advance(parts[1], links=links)
+    parts, sent = sum_rows(hi, next_part, own_part)
+    convolution_sum.advance(sent, links=links)
     residual_grad, branch, attention_gain_grad = step_back(
         parts, residual_one, attention_gain, residual_grad, 0.5
     )
-    convolution_sum.advance(branch, links=links)
+    attention_sum = WeightSum(
+        (normed_b, after(qkv_grad, sent)), (sin_table, after(position_grad, sent)),
+        (branch_rows, after(mixed_rows, sent)),
+    )
+    attention_sum.advance(links=links, later=(branch,))
+    second_up_sum.advance(branch, links=links)
 
     branch_rows, before_grad, hi, next_part, own_part, first_gain_grad = ffn_call(
-        ffn_backward_kernel, block_owners, all_rows(branch), ups, downs, whole, whole, before_a,
+        ffn_backward_kernel, all_rows(branch), [up_a], [down_a], whole, whole, before_a,
         hat_a,
     )
-    half = hidden // 2
-    first_sums = [
-        WeightSum((branch_rows, active_a[:, :half])),
-        WeightSum((branch_rows, active_a[:, half:])),
-        WeightSum((normed_a, before_grad[:, :half])),
-        WeightSum((normed_a, before_grad[:, half:])),
-    ]
-
+    first_down_sum = WeightSum((branch_rows, active_a))
+    first_up_sum = WeightSum((normed_a, before_grad))
+
+    bias_grads, taps_grad = after((bias_grads, taps_grad), branch)
     plain_grads = jnp.concatenate(
         [
             bias_grads[:head_count].T.reshape(dp_size, cut),
@@ -1246,6 +1310,8 @@
         block_selection.astype(FLOAT), plain_grads, (((0,), (0,)), ((), ())),
         precision=lax.Precision.HIGHEST, preferred_element_type=FLOAT,
     )
+    parts, sent = sum_rows(hi, next_part, own_part)
+    first_gain_grad = after(first_gain_grad, sent)
     gain_grads = jnp.concatenate(
         [
             first_gain_grad, attention_gain_grad, convolution_gain_grad, second_gain_grad,
@@ -1256,46 +1322,47 @@
     gain_grads = gain_grads.reshape(5, dp_size, block).transpose(1, 0, 2)
     small_grads = jnp.concatenate([gain_grads.reshape(dp_size, 5 * block), plain_grads], axis=1)
 
-    smalls, mask = [small_grads], [1]
-
-    def small_step():
-        if mask[0] < dp_size:
-            kept = smalls[0].shape[0] // 2
-            smalls[0] = smalls[0][:kept] + links.swap(smalls[0][kept:], mask[0])
-            mask[0] *= 2
-
-    down_a, down_b, up_a, up_b = first_sums
-    small_step()
+    first_down_sum.advance(later=(sent,))
+    convolution_sum.advance(first_down_sum.upper)
+    attention_sum.advance()
+    first_up_sum.advance(attention_sum.sent, later=(sent,))
+    second_up_sum.advance(first_down_sum.upper)
+    residual_grad, _, _ = step_back(parts, residual_zero, first_gain, residual_grad, 1.0)
+    inputs_rows = all_rows(
+        times_transposed(residual_grad.astype(LOW), selection).astype(LOW)
+    )
+    result_rows = all_rows(
+        times_transposed(after(own_result, parts[2]), selection).astype(LOW)
+    )
+    mask, small_grads, down_hop = 1, after(small_grads, first_down_sum.upper), first_down_sum.sent
+    while mask < dp_size:
+        kept = small_grads.shape[0] // 2
+        small_token = after(swap(small_grads[kept:], "dp", mask), down_hop)
+        small_grads = small_grads[:kept] + small_token
+        mask *= 2
+    first_down_sum.advance()
+    attention_sum.advance(first_down_sum.upper)
+    down_hop = first_down_sum.sent
+    first_down_sum.advance(attention_sum.upper)
+    first_up_sum.advance(down_hop, inputs_rows[3], result_rows[3], small_token)
+    first_up_sum.advance(attention_sum.sent, first_down_sum.sent)
     for part in (
-        down_a, attention_sum, down_b, attention_sum, None, down_a, up_a, down_b, up_b, down_a,
-        None, up_a, down_b, up_b, up_a, up_b,
+        second_down_sum, second_up_sum, convolution_sum, attention_sum, first_down_sum,
+        first_up_sum,
     ):
-        if part is None:
-            small_step()
-        else:
-            part.advance(links=links)
-    while mask[0] < dp_size:
-        small_step()
-    for part in (second_down_sum, second_up_sum, convolution_sum, attention_sum, *first_sums):
         part.rest()
 
-    parts = sum_rows(hi, next_part, own_part)
-    residual_grad, _, _ = step_back(parts, residual_zero, first_gain, residual_grad, 1.0)
     second_down_grad, second_up_grad, convolution_in_grad, convolution_out_grad = finish(
         [second_down_sum, second_up_sum, convolution_sum],
         [hidden, hidden, 2 * channels, channels], parts[2],
     )
     attention_grads = finish([attention_sum], [heads] * 5)
-    first_down_grad, first_up_grad = join(first_sums[:2]), join(first_sums[2:])
-
-    def plain_order(own):
-        pieces = all_rows(times_transposed(own, selection).astype(LOW))
-        return select_rows(place, pieces)
-
-    result = plain_order(after(own_result, hi))
-    inputs_grad = plain_order(residual_grad.astype(LOW)).astype(FLOAT)
-
-    small_grads = smalls[0][0]
+    first_down_grad, first_up_grad = join([first_down_sum]), join([first_up_sum])
+
+    result = select_rows(place, result_rows, LOW)
+    inputs_grad = select_rows(place, inputs_rows, FLOAT)
+
+    small_grads = small_grads[0]
     gain_grads = total_over(small_grads[: 5 * block].reshape(5, block), "mp")
     plain_grads = small_grads[5 * block :]
 

time: 521 us -> 482 us (0.925)
  waiting for transfers between devices: 227 us -> 168 us
  local copies, waits for them, and re-layouts: 42.6 us -> 63.9 us
  starting transfers between devices: 90 us -> 108 us
  between operations: 16.5 us -> 2.81 us
  matrix products: 40.9 us -> 30.1 us
    ppermute x109 -> x110, waiting for transfers between devices: 227 us -> 168 us  [swap(): return lax.ppermute(values, axis, [(i, i ^ mask) for i in range(size)])]
    unnamed x278 -> x258, local copies, waits for them, and re-layouts: 23.8 us -> 42.4 us
    ppermute x109 -> x110, starting transfers between devices: 90 us -> 108 us  [swap(): return lax.ppermute(values, axis, [(i, i ^ mask) for i in range(size)])]
    dot_general x22 -> x18, matrix products: 31.5 us -> 21 us  [outer_sum(): lax.dot_general(left_side, right_side, (((0,), (0,)), ((), ())), preferre...]
    slice x2 -> x8, local copies, waits for them, and re-layouts: 0.01 us -> 6.75 us  [the longest x5 6.14 us: advance(): left[:, :half]]
    pallas_call x32 -> x53, Pallas kernels: 83.3 us -> 84.8 us  [the longest x32 84.8 us: call(): pl.pallas_call(saving if saved else kernel, out_shape=tuple((jax.ShapeDty...]
  transfers between devices with their start and end apart: 110 -> 110, of which waited for: 58 -> 48; matrix products, arithmetic and copies ran while one was open for 15% -> 15% of each run, Pallas kernels for 13% -> 15%
where the time goes in v3:
time: 482 us; the launch traced here: 475 us
  waiting for transfers between devices  168 us (35%)
  starting transfers between devices  108 us (22%)
  Pallas kernels  84.8 us (18%)
  local copies, waits for them, and re-layouts  63.9 us (13%)
  matrix products  30.1 us (6%)
  other arithmetic  16.7 us (3%)
    ppermute x110, waiting for transfers between devices, swap(): return lax.ppermute(values, axis, [(i, i ^ mask) for i in range(size)])  168 us
    ppermute x110, starting transfers between devices, swap(): return lax.ppermute(values, axis, [(i, i ^ mask) for i in range(size)])  108 us
    pallas_call x32, Pallas kernels, call(): pl.pallas_call(saving if saved else kernel, out_shape=tuple((jax.ShapeDty...  84.8 us
    unnamed x258, local copies, waits for them, and re-layouts  42.4 us
    dot_general x18, matrix products, outer_sum(): lax.dot_general(left_side, right_side, (((0,), (0,)), ((), ())), preferre...  21 us
  transfers between devices with their start and end apart: 110, of which 48 were waited for; matrix products, arithmetic and copies ran while one was open for 15% of the time, Pallas kernels for 15%

profile of v3, /device:TPU:0, one launch (start us, length us, event | category | flops | bytes accessed | tf_op | source)
XLA Modules:
  0.0 474.7 jit_solution(4750102880041613317)
XLA Ops:
  22.5 4.8 %collective-permute-done.5.refs_6_ = bf16[128,1024]{1,0:T(8,128)(2,1)S(1)} collective-permute-done((bf16[128,1024]{1,0:T(8,128)(2,1)S(1)}, bf16[128,1024]{1,0:T(8,128)(2,1)S(1)}, u32[]{:S(2)}, u32[]{:S(2)}) %collective-permute-start.5) | collective-permute-done | bytes 262176 | tf_op jit(solution)/shard_map/ppermute | solution.py:43
  52.1 5.9 %collective-permute-start.22 = (bf16[128,1280]{1,0:T(8,128)(2,1)S(1)}, bf16[128,1280]{1,0:T(8,128)(2,1)}, u32[]{:S(2)}, u32[]{:S(2)}) collective-permute-start(bf16[128,1280]{1,0:T(8,128)(2,1)S(1)} %convert_dynamic-update-slice_fusion.refs_8_), channel_id=1, source_target_pairs={{0,16},{4,20},{8,24},{12,28},{16,0},{20,4},{24,8},{28,12},{1,17},{... | collective-permute-start | bytes 983048 | tf_op jit(solution)/shard_map/ppermute | solution.py:43
  73.8 7.4 %shard_map.407 = (bf16[512,1024]{1,0:T(8,128)(2,1)}, bf16[512,1024]{1,0:T(8,128)(2,1)}, bf16[512,1024]{1,0:T(8,128)(2,1)}, bf16[1024,1024]{1,0:T(8,128)(2,1)}, b...) custom-call(bf16[512,1024]{1,0:T(8,128)(2,1)} %get-tuple-element.442, ...), custom_call_target="tpu_custom_call" | custom-call | flops 2147483648 | tf_op jit(solution)/shard_map/pallas_call | solution.py:234
  84.0 7.8 %collective-permute-done.24.source_ref = bf16[128,1280]{1,0:T(8,128)(2,1)S(1)} collective-permute-done((bf16[128,1280]{1,0:T(8,128)(2,1)}, bf16[128,1280]{1,0:T(8,128)(2,1)S(1)}, u32[]{:S(2)}, u32[]{:S(2)}) %collective-permute-start.24) | collective-permute-done | bytes 327712 | tf_op jit(solution)/shard_map/ppermute | solution.py:43
  109.5 5.0 %collective-permute-done.28.source_ref = bf16[128,1280]{1,0:T(8,128)(2,1)} collective-permute-done((bf16[128,1280]{1,0:T(8,128)(2,1)}, bf16[128,1280]{1,0:T(8,128)(2,1)}, u32[]{:S(2)}, u32[]{:S(2)}) %collective-permute-start.28) | collective-permute-done | bytes 327712 | tf_op jit(solution)/shard_map/ppermute | solution.py:43
  117.2 12.0 %shard_map.417 = (bf16[512,1024]{1,0:T(8,128)(2,1)}, bf16[512,256]{1,0:T(8,128)(2,1)S(1)}, bf16[2,512,512]{2,1,0:T(8,128)(2,1)}, bf16[512,256]{1,0:T(8,128)(2,1)...) custom-call(s32[1]{0:T(128)} %bitcast.refs_0_.place_ref, ...), custom_call_target="tpu_custom_call" | custom-call | flops 2214592512 | tf_op jit(solution)/shard_map/pallas_call | solution.py:234
  156.6 7.8 %collective-permute-done.40.source_ref = bf16[128,768]{1,0:T(8,128)(2,1)} collective-permute-done((bf16[128,768]{1,0:T(8,128)(2,1)}, bf16[128,768]{1,0:T(8,128)(2,1)}, u32[]{:S(2)}, u32[]{:S(2)}) %collective-permute-start.40) | collective-permute-done | bytes 196640 | tf_op jit(solution)/shard_map/ppermute | solution.py:43
  168.2 5.0 %shard_map.427 = (bf16[512,1024]{1,0:T(8,128)(2,1)}, f32[512,512]{1,0:T(8,128)}, bf16[1024,768]{1,0:T(8,128)(2,1)}, f32[512,256]{1,0:T(8,128)S(1)}, f32[8,256]{1,0:T(8,128)S(1)}) custom-call(s32[1]{0:T(128)} %bitcast.refs_0_.place_ref, s32[1,4]{1,0:T(1,128)S(1)} %copy-done.39, f32[5,256]{1,0:T(8,128)S(1)} %bitcast.79, ...), custom_call_target="tpu_custom_call" | custom-call | flops 536870912 | tf_op jit(solution)/shard_map/pallas_call | solution.py:234
  198.9 5.6 %collective-permute-done.45.far_ref = bf16[128,1024]{1,0:T(8,128)(2,1)S(1)} collective-permute-done((bf16[128,1024]{1,0:T(8,128)(2,1)S(1)}, bf16[128,1024]{1,0:T(8,128)(2,1)S(1)}, u32[]{:S(2)}, u32[]{:S(2)}) %collective-permute-start.45) | collective-permute-done | bytes 262176 | tf_op jit(solution)/shard_map/ppermute | solution.py:43
  210.2 5.9 %collective-permute-done.46.refs_1_ = bf16[128,1024]{1,0:T(8,128)(2,1)S(1)} collective-permute-done((bf16[128,1024]{1,0:T(8,128)(2,1)}, bf16[128,1024]{1,0:T(8,128)(2,1)S(1)}, u32[]{:S(2)}, u32[]{:S(2)}) %collective-permute-start.46) | collective-permute-done | bytes 262176 | tf_op jit(solution)/shard_map/ppermute | solution.py:43
  218.0 6.7 %shard_map.438 = (bf16[512,1024]{1,0:T(8,128)(2,1)}, bf16[512,1024]{1,0:T(8,128)(2,1)}, bf16[512,1024]{1,0:T(8,128)(2,1)}, bf16[1024,1024]{1,0:T(8,128)(2,1)}, b...) custom-call(bf16[128,1024]{1,0:T(8,128)(2,1)} %get-tuple-element.268, ...), custom_call_target="tpu_custom_call" | custom-call | flops 2147483648 | tf_op jit(solution)/shard_map/pallas_call | solution.py:234
  228.2 7.0 %collective-permute-done.57.far_ref = bf16[128,1024]{1,0:T(8,128)(2,1)S(1)} collective-permute-done((bf16[128,1024]{1,0:T(8,128)(2,1)S(1)}, bf16[128,1024]{1,0:T(8,128)(2,1)S(1)}, u32[]{:S(2)}, u32[]{:S(2)}) %collective-permute-start.57) | collective-permute-done | bytes 262176 | tf_op jit(solution)/shard_map/ppermute | solution.py:43
  236.2 7.1 %collective-permute-done.58.refs_1_ = bf16[128,1024]{1,0:T(8,128)(2,1)S(1)} collective-permute-done((bf16[128,1024]{1,0:T(8,128)(2,1)S(1)}, bf16[128,1024]{1,0:T(8,128)(2,1)S(1)}, u32[]{:S(2)}, u32[]{:S(2)}) %collective-permute-start.58) | collective-permute-done | bytes 262176 | tf_op jit(solution)/shard_map/ppermute | solution.py:43
  244.8 6.9 %shard_map.441 = (bf16[512,1024]{1,0:T(8,128)(2,1)S(1)}, bf16[512,1024]{1,0:T(8,128)(2,1)}, bf16[256,1024]{1,0:T(8,128)(2,1)S(1)}, bf16[128,1024]{1,0:T(8,128)(2,1)S(1)}, f32[128,1024]{1,0:T(8,128)S(1)}) custom-call(bf16[128,1024]{1,0:T(8,128)(2,1)S(1)} %get-tuple-element.287.refs_0_, bf16[128,1024]{1,0:T(8,128)(2,1)S(1)} %collective-permute-done.58.refs_1_, ...), custom_call_target="tpu_custom_call" | custom-call | flops 2147483648 | tf_op jit(solution)/shard_map/pallas_call | solution.py:234
  254.3 8.0 %collective-permute-done.62.far_ref = bf16[128,1024]{1,0:T(8,128)(2,1)S(1)} collective-permute-done((bf16[128,1024]{1,0:T(8,128)(2,1)S(1)}, bf16[128,1024]{1,0:T(8,128)(2,1)S(1)}, u32[]{:S(2)}, u32[]{:S(2)}) %collective-permute-start.62) | collective-permute-done | bytes 262176 | tf_op jit(solution)/shard_map/ppermute | solution.py:43
  289.6 5.0 %shard_map.445 = (bf16[512,512]{1,0:T(8,128)(2,1)S(1)}, f32[8,256]{1,0:T(8,128)S(1)}, bf16[256,1024]{1,0:T(8,128)(2,1)S(1)}, bf16[128,1024]{1,0:T(8,128)(2,1)S(1)}, f32[128,1024]{1,0:T(8,128)S(1)}) custom-call(s32[1]{0:T(128)} %bitcast.refs_0_.place_ref, s32[1,4]{1,0:T(1,128)S(1)} %copy-done.39, f32[5,256]{1,0:T(8,128)S(1)} %bitcast.80, ...), custom_call_target="tpu_custom_call" | custom-call | flops 536870912 | tf_op jit(solution)/shard_map/pallas_call | solution.py:234
  302.6 6.6 %collective-permute-done.70.far_ref = bf16[128,1024]{1,0:T(8,128)(2,1)S(1)} collective-permute-done((bf16[128,1024]{1,0:T(8,128)(2,1)S(1)}, bf16[128,1024]{1,0:T(8,128)(2,1)S(1)}, u32[]{:S(2)}, u32[]{:S(2)}) %collective-permute-start.70) | collective-permute-done | bytes 262176 | tf_op jit(solution)/shard_map/ppermute | solution.py:43
  318.6 12.2 %shard_map.448 = (bf16[512,1024]{1,0:T(8,128)(2,1)}, bf16[512,768]{1,0:T(8,128)(2,1)}, bf16[1024,256]{1,0:T(8,128)(2,1)S(1)}, f32[4,128]{1,0:T(4,128)S(1)}, bf16...) custom-call(s32[1]{0:T(128)} %bitcast.refs_0_.place_ref, ...), custom_call_target="tpu_custom_call" | custom-call | flops 2147483648 | tf_op jit(solution)/shard_map/pallas_call | solution.py:234
  357.2 7.6 %shard_map.451 = (bf16[512,1024]{1,0:T(8,128)(2,1)S(1)}, bf16[512,1024]{1,0:T(8,128)(2,1)}, bf16[256,1024]{1,0:T(8,128)(2,1)S(1)}, bf16[128,1024]{1,0:T(8,128)(2...) custom-call(bf16[128,1024]{1,0:T(8,128)(2,1)S(1)} %get-tuple-element.315.refs_0_, ...), custom_call_target="tpu_custom_call" | custom-call | flops 2147483648 | tf_op jit(solution)/shard_map/pallas_call | solution.py:234
  391.7 5.7 %collective-permute-done.87 = f32[4,864]{1,0:T(4,128)S(1)} collective-permute-done((f32[4,864]{1,0:T(4,128)S(1)}, f32[4,864]{1,0:T(4,128)S(1)}, u32[]{:S(2)}, u32[]{:S(2)}) %collective-permute-start.87) | collective-permute-done | bytes 13856 | tf_op jit(solution)/shard_map/ppermute | solution.py:43
  406.1 6.9 %collective-permute-done.89 = f32[2,864]{1,0:T(2,128)} collective-permute-done((f32[2,864]{1,0:T(2,128)}, f32[2,864]{1,0:T(2,128)}, u32[]{:S(2)}, u32[]{:S(2)}) %collective-permute-start.89) | collective-permute-done | bytes 6944 | tf_op jit(solution)/shard_map/ppermute | solution.py:43
  421.6 7.5 %collective-permute-done.97 = bf16[256,1024]{1,0:T(8,128)(2,1)S(1)} collective-permute-done((bf16[256,1024]{1,0:T(8,128)(2,1)S(1)}, bf16[256,1024]{1,0:T(8,128)(2,1)S(1)}, u32[]{:S(2)}, u32[]{:S(2)}) %collective-permute-start.97) | collective-permute-done | bytes 524320 | tf_op jit(solution)/shard_map/ppermute | solution.py:43
  431.5 5.7 %collective-permute-done.96 = bf16[512,1024]{1,0:T(8,128)(2,1)S(1)} collective-permute-done((bf16[512,1024]{1,0:T(8,128)(2,1)}, bf16[512,1024]{1,0:T(8,128)(2,1)S(1)}, u32[]{:S(2)}, u32[]{:S(2)}) %collective-permute-start.96) | collective-permute-done | bytes 1048608 | tf_op jit(solution)/shard_map/ppermute | solution.py:43
  449.0 9.6 %collective-permute-done.100.refs_1_ = bf16[128,1024]{1,0:T(8,128)(2,1)S(1)} collective-permute-done((bf16[128,1024]{1,0:T(8,128)(2,1)}, bf16[128,1024]{1,0:T(8,128)(2,1)S(1)}, u32[]{:S(2)}, u32[]{:S(2)}) %collective-permute-start.100) | collective-permute-done | bytes 262176 | tf_op jit(solution)/shard_map/ppermute | solution.py:43
  (646 shorter events, 302.2 us)
Async XLA Ops:
  12.5 21.6 %collective-permute-start = (bf16[1,928]{1,0:T(2,128)(2,1)S(1)}, bf16[1,928]{1,0:T(2,128)(2,1)S(1)}, u32[]{:S(2)}, u32[]{:S(2)}) collective-permute-start(bf16[1,928]{1,0:T(2,128)(2,1)S(1)} %broadcast_in_dim.2), channel_id=1, source_target_pairs={{0,16},{4,20},{8,24},{12,28},{16,0},{20,4},{24,8},{28,12},{1,17},{... | collective-permute-start | bytes 5576 | tf_op jit(solution)/shard_map/ppermute | solution.py:43
  52.1 29.2 %collective-permute-start.22 = (bf16[128,1280]{1,0:T(8,128)(2,1)S(1)}, bf16[128,1280]{1,0:T(8,128)(2,1)}, u32[]{:S(2)}, u32[]{:S(2)}) collective-permute-start(bf16[128,1280]{1,0:T(8,128)(2,1)S(1)} %convert_dynamic-update-slice_fusion.refs_8_), channel_id=1, source_target_pairs={{0,16},{4,20},{8,24},{12,28},{16,0},{20,4},{24,8},{28,12},{1,17},{... | collective-permute-start | bytes 983048 | tf_op jit(solution)/shard_map/ppermute | solution.py:43
  58.9 25.1 %collective-permute-start.23 = (bf16[128,1280]{1,0:T(8,128)(2,1)S(1)}, bf16[128,1280]{1,0:T(8,128)(2,1)}, u32[]{:S(2)}, u32[]{:S(2)}) collective-permute-start(bf16[128,1280]{1,0:T(8,128)(2,1)S(1)} %convert_dynamic-update-slice_fusion.refs_8_), channel_id=1, source_target_pairs={{0,8},{4,12},{8,0},{12,4},{16,24},{20,28},{24,16},{28,20},{1,9},{5... | collective-permute-start | bytes 983048 | tf_op jit(solution)/shard_map/ppermute | solution.py:43
  61.9 21.5 %collective-permute-start.25 = (bf16[128,1280]{1,0:T(8,128)(2,1)S(1)}, bf16[128,1280]{1,0:T(8,128)(2,1)}, u32[]{:S(2)}, u32[]{:S(2)}) collective-permute-start(bf16[128,1280]{1,0:T(8,128)(2,1)S(1)} %convert_dynamic-update-slice_fusion.refs_8_), channel_id=1, source_target_pairs={{0,4},{4,0},{8,12},{12,8},{16,20},{20,16},{24,28},{28,24},{1,5},{5... | collective-permute-start | bytes 983048 | tf_op jit(solution)/shard_map/ppermute | solution.py:43
  95.3 36.7 %collective-permute-start.34 = (bf16[128,768]{1,0:T(8,128)(2,1)S(1)}, bf16[128,768]{1,0:T(8,128)(2,1)}, u32[]{:S(2)}, u32[]{:S(2)}) collective-permute-start(bf16[128,768]{1,0:T(8,128)(2,1)S(1)} %pad_maximum_fusion.3.refs_7_), channel_id=1, source_target_pairs={{0,16},{4,20},{8,24},{12,28},{16,0},{20,4},{24,8},{28,12},{1,17},{... | collective-permute-start | bytes 589832 | tf_op jit(solution)/shard_map/ppermute | solution.py:43
  107.6 28.9 %collective-permute-start.35 = (bf16[128,768]{1,0:T(8,128)(2,1)S(1)}, bf16[128,768]{1,0:T(8,128)(2,1)S(1)}, u32[]{:S(2)}, u32[]{:S(2)}) collective-permute-start(bf16[128,768]{1,0:T(8,128)(2,1)S(1)} %pad_maximum_fusion.3.refs_7_), channel_id=1, source_target_pairs={{0,8},{4,12},{8,0},{12,4},{16,24},{20,28},{24,16},{28,20},{1,9},{5... | collective-permute-start | bytes 589832 | tf_op jit(solution)/shard_map/ppermute | solution.py:43
  144.4 30.4 %collective-permute-start.49 = (bf16[128,2048]{1,0:T(8,128)(2,1)S(1)}, bf16[128,2048]{1,0:T(8,128)(2,1)}, u32[]{:S(2)}, u32[]{:S(2)}) collective-permute-start(bf16[128,2048]{1,0:T(8,128)(2,1)S(1)} %copy-done.2), channel_id=1, source_target_pairs={{0,16},{4,20},{8,24},{12,28},{16,0},{20,4},{24,8},{28,12},{1,17},{... | collective-permute-start | bytes 1572872 | tf_op jit(solution)/shard_map/ppermute | solution.py:43
  148.0 32.4 %collective-permute-start.52 = (bf16[128,2048]{1,0:T(8,128)(2,1)S(1)}, bf16[128,2048]{1,0:T(8,128)(2,1)}, u32[]{:S(2)}, u32[]{:S(2)}) collective-permute-start(bf16[128,2048]{1,0:T(8,128)(2,1)S(1)} %copy-done.2), channel_id=1, source_target_pairs={{0,4},{4,0},{8,12},{12,8},{16,20},{20,16},{24,28},{28,24},{1,5},{5... | collective-permute-start | bytes 1572872 | tf_op jit(solution)/shard_map/ppermute | solution.py:43
  155.0 28.7 %collective-permute-start.50 = (bf16[128,2048]{1,0:T(8,128)(2,1)S(1)}, bf16[128,2048]{1,0:T(8,128)(2,1)}, u32[]{:S(2)}, u32[]{:S(2)}) collective-permute-start(bf16[128,2048]{1,0:T(8,128)(2,1)S(1)} %copy-done.2), channel_id=1, source_target_pairs={{0,8},{4,12},{8,0},{12,4},{16,24},{20,28},{24,16},{28,20},{1,9},{5... | collective-permute-start | bytes 1572872 | tf_op jit(solution)/shard_map/ppermute | solution.py:43
  186.1 24.1 %collective-permute-start.54 = (bf16[128,2048]{1,0:T(8,128)(2,1)}, bf16[128,2048]{1,0:T(8,128)(2,1)}, u32[]{:S(2)}, u32[]{:S(2)}) collective-permute-start(bf16[128,2048]{1,0:T(8,128)(2,1)} %shard_map.432.refs_6_.refs_14_), channel_id=1, source_target_pairs={{0,4},{4,0},{8,12},{12,8},{16,20},{20,16},{24,28},{28,24},{1,5},{5... | collective-permute-start | bytes 1572872 | tf_op jit(solution)/shard_map/ppermute | solution.py:43
  193.9 24.1 %collective-permute-start.55 = (bf16[128,2048]{1,0:T(8,128)(2,1)}, bf16[128,2048]{1,0:T(8,128)(2,1)}, u32[]{:S(2)}, u32[]{:S(2)}) collective-permute-start(bf16[128,2048]{1,0:T(8,128)(2,1)} %shard_map.433.refs_7_.refs_15_), channel_id=1, source_target_pairs={{0,4},{4,0},{8,12},{12,8},{16,20},{20,16},{24,28},{28,24},{1,5},{5... | collective-permute-start | bytes 1572872 | tf_op jit(solution)/shard_map/ppermute | solution.py:43
  264.9 31.6 %collective-permute-start.93 = (bf16[512,1024]{1,0:T(8,128)(2,1)}, bf16[512,1024]{1,0:T(8,128)(2,1)}, u32[]{:S(2)}, u32[]{:S(2)}) collective-permute-start(bf16[512,1024]{1,0:T(8,128)(2,1)} %convolution_convert_fusion.1), channel_id=1, source_target_pairs={{0,4},{4,0},{8,12},{12,8},{16,20},{20,16},{24,28},{28,24},{1,5},{5... | collective-permute-start | bytes 3145736 | tf_op jit(solution)/shard_map/ppermute | solution.py:43
  294.7 53.9 %collective-permute-start.104 = (bf16[512,1024]{1,0:T(8,128)(2,1)}, bf16[512,1024]{1,0:T(8,128)(2,1)S(1)}, u32[]{:S(2)}, u32[]{:S(2)}) collective-permute-start(bf16[512,1024]{1,0:T(8,128)(2,1)} %convolution_convert_fusion), channel_id=1, source_target_pairs={{0,4},{4,0},{8,12},{12,8},{16,20},{20,16},{24,28},{28,24},{1,5},{5... | collective-permute-start | bytes 3145736 | tf_op jit(solution)/shard_map/ppermute | solution.py:43
  299.4 32.0 %collective-permute-start.102 = (bf16[256,1024]{1,0:T(8,128)(2,1)}, bf16[256,1024]{1,0:T(8,128)(2,1)}, u32[]{:S(2)}, u32[]{:S(2)}) collective-permute-start(bf16[256,1024]{1,0:T(8,128)(2,1)} %slice.420), channel_id=1, source_target_pairs={{0,8},{4,12},{8,0},{12,4},{16,24},{20,28},{24,16},{28,20},{1,9},{5... | collective-permute-start | bytes 1572872 | tf_op jit(solution)/shard_map/ppermute | solution.py:43
  311.2 26.2 %collective-permute-start.107 = (bf16[512,768]{1,0:T(8,128)(2,1)S(1)}, bf16[512,768]{1,0:T(8,128)(2,1)}, u32[]{:S(2)}, u32[]{:S(2)}) collective-permute-start(bf16[512,768]{1,0:T(8,128)(2,1)S(1)} %pad_maximum_fusion.1), channel_id=1, source_target_pairs={{0,4},{4,0},{8,12},{12,8},{16,20},{20,16},{24,28},{28,24},{1,5},{5... | collective-permute-start | bytes 2359304 | tf_op jit(solution)/shard_map/ppermute | solution.py:43
  333.5 69.2 %collective-permute-start.103 = (bf16[128,1024]{1,0:T(8,128)(2,1)}, bf16[128,1024]{1,0:T(8,128)(2,1)}, u32[]{:S(2)}, u32[]{:S(2)}) collective-permute-start(bf16[128,1024]{1,0:T(8,128)(2,1)} %slice.426), channel_id=1, source_target_pairs={{0,16},{4,20},{8,24},{12,28},{16,0},{20,4},{24,8},{28,12},{1,17},{... | collective-permute-start | bytes 786440 | tf_op jit(solution)/shard_map/ppermute | solution.py:43
  339.6 29.1 %collective-permute-start.108 = (bf16[256,768]{1,0:T(8,128)(2,1)}, bf16[256,768]{1,0:T(8,128)(2,1)}, u32[]{:S(2)}, u32[]{:S(2)}) collective-permute-start(bf16[256,768]{1,0:T(8,128)(2,1)} %slice.423), channel_id=1, source_target_pairs={{0,8},{4,12},{8,0},{12,4},{16,24},{20,28},{24,16},{28,20},{1,9},{5... | collective-permute-start | bytes 1179656 | tf_op jit(solution)/shard_map/ppermute | solution.py:43
  344.4 32.7 %collective-permute-start.94 = (bf16[512,1280]{1,0:T(8,128)(2,1)}, bf16[512,1280]{1,0:T(8,128)(2,1)}, u32[]{:S(2)}, u32[]{:S(2)}) collective-permute-start(bf16[512,1280]{1,0:T(8,128)(2,1)} %pad_maximum_fusion), channel_id=1, source_target_pairs={{0,4},{4,0},{8,12},{12,8},{16,20},{20,16},{24,28},{28,24},{1,5},{5... | collective-permute-start | bytes 3932168 | tf_op jit(solution)/shard_map/ppermute | solution.py:43
  367.3 30.6 %collective-permute-start.88 = (bf16[512,1024]{1,0:T(8,128)(2,1)}, bf16[512,1024]{1,0:T(8,128)(2,1)}, u32[]{:S(2)}, u32[]{:S(2)}) collective-permute-start(bf16[512,1024]{1,0:T(8,128)(2,1)} %convolution_convert_fusion.3), channel_id=1, source_target_pairs={{0,4},{4,0},{8,12},{12,8},{16,20},{20,16},{24,28},{28,24},{1,5},{5... | collective-permute-start | bytes 3145736 | tf_op jit(solution)/shard_map/ppermute | solution.py:43
  370.6 30.5 %collective-permute-start.109 = (bf16[128,768]{1,0:T(8,128)(2,1)}, bf16[128,768]{1,0:T(8,128)(2,1)}, u32[]{:S(2)}, u32[]{:S(2)}) collective-permute-start(bf16[128,768]{1,0:T(8,128)(2,1)} %slice.430), channel_id=1, source_target_pairs={{0,16},{4,20},{8,24},{12,28},{16,0},{20,4},{24,8},{28,12},{1,17},{... | collective-permute-start | bytes 589832 | tf_op jit(solution)/shard_map/ppermute | solution.py:43
  374.1 28.6 %collective-permute-start.106 = (bf16[128,1024]{1,0:T(8,128)(2,1)}, bf16[128,1024]{1,0:T(8,128)(2,1)S(1)}, u32[]{:S(2)}, u32[]{:S(2)}) collective-permute-start(bf16[128,1024]{1,0:T(8,128)(2,1)} %slice.425), channel_id=1, source_target_pairs={{0,16},{4,20},{8,24},{12,28},{16,0},{20,4},{24,8},{28,12},{1,17},{... | collective-permute-start | bytes 786440 | tf_op jit(solution)/shard_map/ppermute | solution.py:43
  402.7 60.9 %collective-permute-start.85 = (bf16[128,1024]{1,0:T(8,128)(2,1)S(1)}, bf16[128,1024]{1,0:T(8,128)(2,1)}, u32[]{:S(2)}, u32[]{:S(2)}) collective-permute-start(bf16[128,1024]{1,0:T(8,128)(2,1)S(1)} %fusion.18.refs_0_), channel_id=1, source_target_pairs={{0,1},{1,0},{2,3},{3,2},{4,5},{5,4},{6,7},{7,6},{8,9},{9,8},{10,11... | collective-permute-start | bytes 786440 | tf_op jit(solution)/shard_map/ppermute | solution.py:43
  414.6 22.6 %collective-permute-start.96 = (bf16[512,1024]{1,0:T(8,128)(2,1)}, bf16[512,1024]{1,0:T(8,128)(2,1)S(1)}, u32[]{:S(2)}, u32[]{:S(2)}) collective-permute-start(bf16[512,1024]{1,0:T(8,128)(2,1)} %convolution_convert_fusion.2), channel_id=1, source_target_pairs={{0,4},{4,0},{8,12},{12,8},{16,20},{20,16},{24,28},{28,24},{1,5},{5... | collective-permute-start | bytes 3145736 | tf_op jit(solution)/shard_map/ppermute | solution.py:43
  439.0 22.0 %collective-permute-start.98 = (bf16[256,1024]{1,0:T(8,128)(2,1)}, bf16[256,1024]{1,0:T(8,128)(2,1)}, u32[]{:S(2)}, u32[]{:S(2)}) collective-permute-start(bf16[256,1024]{1,0:T(8,128)(2,1)} %slice.421), channel_id=1, source_target_pairs={{0,8},{4,12},{8,0},{12,4},{16,24},{20,28},{24,16},{28,20},{1,9},{5... | collective-permute-start | bytes 1572872 | tf_op jit(solution)/shard_map/ppermute | solution.py:43
  (211 other events, 1821.9 us)

commit v4 on v3

--- a/solution.py
+++ b/solution.py
@@ -139,12 +139,15 @@
         if not self.mask:
             half = self.pairs[0][0].shape[1] // 2
             upper = [outer_sum(left[:, half:], right).astype(LOW) for left, right in self.pairs]
-            lower = [
-                outer_sum(after(left[:, :half], *later), right) for left, right in self.pairs
-            ]
-            self.upper, self.kept = jnp.concatenate(upper, axis=1), jnp.concatenate(lower, axis=1)
-            self.upper, self.mask = after(self.upper, *tokens), 1
+            self.later = later
+            self.upper, self.mask = after(jnp.concatenate(upper, axis=1), *tokens), 1
         else:
+            if self.mask == 1 << 1:
+                lower = [
+                    outer_sum(after(left, *self.later)[:, : left.shape[1] // 2], right)
+                    for left, right in self.pairs
+                ]
+                self.kept = jnp.concatenate(lower, axis=1)
             total = self.kept + after(self.sent, *tokens).astype(FLOAT)
             half = total.shape[0] // 2
             self.upper, self.kept = total[half:].astype(LOW), total[:half]
@@ -204,7 +207,7 @@
     return pl.BlockSpec(memory_space=pl.ANY)
 
 
-def call(kernel, outs, scratch, flops, *operands, limit=6, saved=()):
+def call(kernel, outs, scratch, flops, *operands, limit=6, room=50, saved=()):
     places = dict(smem=in_smem, vmem=in_vmem, any=anywhere, hbm=in_hbm)
     count, inner = len(operands), len(scratch)
 
@@ -238,7 +241,7 @@
         out_specs=tuple(in_hbm() if i in saved else in_vmem() for i in range(len(outs))),
         scratch_shapes=list(scratch) + extra,
         compiler_params=pltpu.CompilerParams(
-            vmem_limit_bytes=(50 if scratch else limit) * 2**20
+            vmem_limit_bytes=(room if scratch else limit) * 2**20
         ),
         cost_estimate=pl.CostEstimate(flops=flops, bytes_accessed=0, transcendentals=0),
     )(*[array for _, array in operands])
@@ -321,7 +324,12 @@
 
 def ffn_backward_kernel(*refs, pieces, weights, up_columns, down_columns, gains, save):
     if gains:
-        hat_ref, gain_grad_ref, refs = refs[-10], refs[-4], refs[:-10] + refs[-9:-4] + refs[-3:]
+        (hat_ref, *others), gain_grad_ref, refs = (
+            refs[-9 - gains : -9], refs[-4], refs[: -9 - gains] + refs[-9:-4] + refs[-3:]
+        )
+        gain_grad_ref[...] = jnp.zeros_like(gain_grad_ref)
+        for n, other in enumerate(others):
+            gain_grad_ref[n + 1 : n + 2, :] = other[...]
     row_refs, refs = refs[:pieces], refs[pieces:]
     up_refs, refs = refs[:weights], refs[weights:]
     down_refs, refs = refs[:weights], refs[weights:]
@@ -348,7 +356,7 @@
         product = times_transposed(grad_ref[...], up[features, :])
         write_parts(hi_ref, next_ref, own_ref, features, product)
         if gains:
-            gain_grad_ref[:, features] = jnp.sum(
+            gain_grad_ref[0:1, features] = jnp.sum(
                 product * hat_ref[:, features].astype(FLOAT), axis=0, keepdims=True
             )
 
@@ -360,7 +368,7 @@
 
 
 def ffn_call(
-    kernel, rows, ups, downs, up_columns, down_columns, before=None, hat=None
+    kernel, rows, ups, downs, up_columns, down_columns, before=None, hats=(), room=50
 ):
     row_count = len(rows) * rows[0].shape[0]
     features = rows[0].shape[1]
@@ -375,11 +383,11 @@
     operands += [("any" if len(ups) > 1 else "hbm", array) for array in list(ups) + list(downs)]
     if before is not None:
         operands.append(("vmem", before))
-        kernel = functools.partial(kernel, gains=hat is not None)
+        kernel = functools.partial(kernel, gains=len(hats))
     outs += row_parts(row_count, features)
-    if hat is not None:
-        operands.append(("vmem", hat))
-        outs.append(((1, features), FLOAT))
+    if hats:
+        operands += [("vmem", array) for array in hats]
+        outs.append(((8, features), FLOAT))
     return call(
         functools.partial(
             kernel, pieces=len(rows), weights=len(ups), up_columns=up_columns,
@@ -390,7 +398,7 @@
         + [pltpu.SemaphoreType.DMA((count,))],
         4 * row_count * features * hidden,
         *operands,
-        saved=(0, 1, 2, 3, 4) if before is None else (0, 1),
+        saved=(0, 1, 2, 3, 4) if before is None else (0, 1), room=room,
     )
 
 
@@ -510,7 +518,7 @@
         ("vmem", content_bias), ("vmem", position_bias),
         *[("any", array) for array in list(rows) + list(weights)],
         ("hbm", table),
-        saved=tuple(range(9)),
+        saved=tuple(range(9)), room=54,
     )
 
 
@@ -690,7 +698,7 @@
         ("smem", place), ("smem", lengths), ("vmem", taps),
         *[("any", array) for array in rows],
         *[("any" if len(weights) > 1 else "hbm", array) for array in weights],
-        saved=(0, 1, 2),
+        saved=(0, 1, 2), room=54,
     )
 
 
@@ -747,7 +755,7 @@
         ("smem", place), ("smem", lengths),
         ("vmem", affine), ("vmem", sums), ("vmem", convolved),
         *[("any" if len(weights) > 1 else "hbm", array) for array in weights],
-        saved=(0,),
+        saved=(0,), room=50,
     )
 
 
@@ -1189,7 +1197,7 @@
     normed_a = (hat_a * first_gain).astype(LOW)
     hat_a = hat_a.astype(LOW)
     _, before_a, active_a, up_a, down_a, hi, next_part, own_part = ffn_call(
-        ffn_forward_kernel, [normed_a], ups, downs, whole, whole
+        ffn_forward_kernel, [normed_a], ups, downs, whole, whole, room=54
     )
     attention_spread.go((3, 5), hi, time=10)
     parts, sent = sum_rows(hi, next_part, own_part)
@@ -1232,7 +1240,7 @@
 
     normed_d, before_d, active_d, up_d, down_d, hi, next_part, own_part = ffn_call(
         ffn_forward_kernel, all_rows(own_d), second_all, second_all, first_half,
-        second_half,
+        second_half, room=50,
     )
     parts, sent = sum_rows(hi, next_part, own_part)
     own_result, residual_grad, branch, final_gain_grad = turn(
@@ -1266,10 +1274,10 @@
         (normed_c, after(lifted_grad, sent)), (branch_rows, after(swished, sent))
     )
     convolution_sum.advance(links=links)
-    second_down_sum.advance(sent, links=links)
     residual_grad, branch, convolution_gain_grad = step_back(
         parts, residual_two, convolution_gain, residual_grad, 1.0
     )
+    second_down_sum.advance(branch, links=links)
     first_row = dp_at * local_channels
     gain_piece = lax.dynamic_slice_in_dim(back_sums[1], first_row, local_channels)
     shift_piece = lax.dynamic_slice_in_dim(back_sums[0], first_row, local_channels)
@@ -1287,15 +1295,9 @@
         (normed_b, after(qkv_grad, sent)), (sin_table, after(position_grad, sent)),
         (branch_rows, after(mixed_rows, sent)),
     )
-    attention_sum.advance(links=links, later=(branch,))
+    attention_later = []
+    attention_sum.advance(links=links, later=attention_later)
     second_up_sum.advance(branch, links=links)
-
-    branch_rows, before_grad, hi, next_part, own_part, first_gain_grad = ffn_call(
-        ffn_backward_kernel, all_rows(branch), [up_a], [down_a], whole, whole, before_a,
-        hat_a,
-    )
-    first_down_sum = WeightSum((branch_rows, active_a))
-    first_up_sum = WeightSum((normed_a, before_grad))
 
     bias_grads, taps_grad = after((bias_grads, taps_grad), branch)
     plain_grads = jnp.concatenate(
@@ -1310,42 +1312,73 @@
         block_selection.astype(FLOAT), plain_grads, (((0,), (0,)), ((), ())),
         precision=lax.Precision.HIGHEST, preferred_element_type=FLOAT,
     )
+
+    branch_rows, before_grad, hi, next_part, own_part, gain_grads = ffn_call(
+        ffn_backward_kernel, all_rows(branch), [up_a], [down_a], whole, whole, before_a,
+        (
+            hat_a, attention_gain_grad, convolution_gain_grad, second_gain_grad, final_gain_grad
+        ),
+    )
+    attention_later.append(hi)
+    first_down_sum = WeightSum((branch_rows, active_a))
+    first_up_sum = WeightSum((normed_a, before_grad))
+
     parts, sent = sum_rows(hi, next_part, own_part)
-    first_gain_grad = after(first_gain_grad, sent)
-    gain_grads = jnp.concatenate(
-        [
-            first_gain_grad, attention_gain_grad, convolution_gain_grad, second_gain_grad,
-            final_gain_grad,
-        ],
-        axis=0,
-    )
-    gain_grads = gain_grads.reshape(5, dp_size, block).transpose(1, 0, 2)
-    small_grads = jnp.concatenate([gain_grads.reshape(dp_size, 5 * block), plain_grads], axis=1)
-
     first_down_sum.advance(later=(sent,))
+    first_up_sum.advance(first_down_sum.upper, later=(sent,))
     convolution_sum.advance(first_down_sum.upper)
+    second_up_sum.advance(first_down_sum.upper)
     attention_sum.advance()
-    first_up_sum.advance(attention_sum.sent, later=(sent,))
-    second_up_sum.advance(first_down_sum.upper)
-    residual_grad, _, _ = step_back(parts, residual_zero, first_gain, residual_grad, 1.0)
+    residual_grad, _, _ = step_back(
+        after(parts, attention_sum.upper), residual_zero, first_gain, residual_grad, 1.0
+    )
     inputs_rows = all_rows(
         times_transposed(residual_grad.astype(LOW), selection).astype(LOW)
     )
     result_rows = all_rows(
         times_transposed(after(own_result, parts[2]), selection).astype(LOW)
     )
-    mask, small_grads, down_hop = 1, after(small_grads, first_down_sum.upper), first_down_sum.sent
-    while mask < dp_size:
-        kept = small_grads.shape[0] // 2
-        small_token = after(swap(small_grads[kept:], "dp", mask), down_hop)
-        small_grads = small_grads[:kept] + small_token
+    first_down_sum.advance(attention_sum.upper)
+
+    attention_sum.advance(
+        first_down_sum.upper, convolution_sum.sent, second_up_sum.sent, second_down_sum.sent
+    )
+    gain_grads, plain_grads = after((gain_grads, plain_grads), attention_sum.upper)
+    mask, small_hops = 1, []
+    while 4 * mask < dp_size:
+        width, count = gain_grads.shape[1] // 2, plain_grads.shape[0] // 2
+        small_hops.append(
+            (swap(gain_grads[:, width:], "dp", mask), swap(plain_grads[count:], "dp", mask))
+        )
+        if 8 * mask < dp_size:
+            gain_grads = gain_grads[:, :width] + small_hops[-1][0]
+            plain_grads = plain_grads[:count] + small_hops[-1][1]
         mask *= 2
-    first_down_sum.advance()
-    attention_sum.advance(first_down_sum.upper)
-    down_hop = first_down_sum.sent
+
     first_down_sum.advance(attention_sum.upper)
-    first_up_sum.advance(down_hop, inputs_rows[3], result_rows[3], small_token)
+    first_up_sum.advance(first_down_sum.upper, inputs_rows[3], result_rows[3])
+
+    arrived = after(small_hops[-1], first_up_sum.upper)
+    gain_grads = gain_grads[:, :width] + arrived[0]
+    plain_grads = plain_grads[:count] + arrived[1]
+    arrived = []
+    masks = (dp_size // 2, dp_size // 4, 3 * dp_size // 4)
+    for p, mask in enumerate(masks):
+        columns = slice((p + 1) * block, (p + 2) * block)
+        arrived.append(
+            (
+                swap(gain_grads[:, columns], "dp", mask),
+                swap(plain_grads[p + 1 : p + 2], "dp", mask),
+            )
+        )
+    gain_grads, plain_grads = gain_grads[:, :block], plain_grads[:1]
+
+    last_hop = first_up_sum.sent
     first_up_sum.advance(attention_sum.sent, first_down_sum.sent)
+    arrived = after(arrived, first_up_sum.upper)
+    for gain_hop, plain_hop in arrived:
+        gain_grads = gain_grads + gain_hop
+        plain_grads = plain_grads + plain_hop
     for part in (
         second_down_sum, second_up_sum, convolution_sum, attention_sum, first_down_sum,
         first_up_sum,
@@ -1354,17 +1387,15 @@
 
     second_down_grad, second_up_grad, convolution_in_grad, convolution_out_grad = finish(
         [second_down_sum, second_up_sum, convolution_sum],
-        [hidden, hidden, 2 * channels, channels], parts[2],
-    )
-    attention_grads = finish([attention_sum], [heads] * 5)
+        [hidden, hidden, 2 * channels, channels], last_hop,
+    )
+    attention_grads = finish([attention_sum], [heads] * 5, last_hop)
     first_down_grad, first_up_grad = join([first_down_sum]), join([first_up_sum])
 
-    result = select_rows(place, result_rows, LOW)
-    inputs_grad = select_rows(place, inputs_rows, FLOAT)
-
-    small_grads = small_grads[0]
-    gain_grads = total_over(small_grads[: 5 * block].reshape(5, block), "mp")
-    plain_grads = small_grads[5 * block :]
+    result = select_rows(place, after(result_rows, first_up_sum.upper), LOW)
+    inputs_grad = select_rows(place, after(inputs_rows, first_up_sum.upper), FLOAT)
+
+    gain_grads, plain_grads = total_over(gain_grads, "mp"), plain_grads[0]
 
     return (
         result,

time: 482 us -> 468 us (0.971)
  local copies, waits for them, and re-layouts: 63.9 us -> 40.3 us
  waiting for transfers between devices: 168 us -> 188 us
  matrix products: 30.1 us -> 24.8 us
    ppermute x110 -> x115, waiting for transfers between devices: 168 us -> 188 us  [swap(): return lax.ppermute(values, axis, [(i, i ^ mask) for i in range(size)])]
    unnamed x258 -> x245, local copies, waits for them, and re-layouts: 42.4 us -> 27.4 us
    slice x9 -> x4, local copies, waits for them, and re-layouts: 6.77 us -> 0.02 us  [the longest x1 0.01 us: per_device(): plain_grads[p + 1:p + 2]]
    dot_general x18, matrix products: 21 us -> 15 us  [outer_sum(): lax.dot_general(left_side, right_side, (((0,), (0,)), ((), ())), preferre...]
    ppermute x110 -> x115, starting transfers between devices: 108 us -> 107 us  [swap(): return lax.ppermute(values, axis, [(i, i ^ mask) for i in range(size)])]
  transfers between devices with their start and end apart: 110 -> 115, of which waited for: 48 -> 55; matrix products, arithmetic and copies ran while one was open for 15% -> 12% of each run, Pallas kernels for 15% -> 15%
where the time goes in v4:
time: 468 us; the launch traced here: 461 us
  waiting for transfers between devices  188 us (40%)
  starting transfers between devices  107 us (23%)
  Pallas kernels  84.9 us (18%)
  local copies, waits for them, and re-layouts  40.3 us (9%)
  matrix products  24.8 us (5%)
  other arithmetic  13.7 us (3%)
    ppermute x115, waiting for transfers between devices, swap(): return lax.ppermute(values, axis, [(i, i ^ mask) for i in range(size)])  188 us
    ppermute x115, starting transfers between devices, swap(): return lax.ppermute(values, axis, [(i, i ^ mask) for i in range(size)])  107 us
    pallas_call x32, Pallas kernels, call(): pl.pallas_call(saving if saved else kernel, out_shape=tuple((jax.ShapeDty...  84.9 us
    unnamed x245, local copies, waits for them, and re-layouts  27.4 us
    dot_general x18, matrix products, outer_sum(): lax.dot_general(left_side, right_side, (((0,), (0,)), ((), ())), preferre...  15 us
  transfers between devices with their start and end apart: 115, of which 55 were waited for; matrix products, arithmetic and copies ran while one was open for 12% of the time, Pallas kernels for 15%

profile of v4, /device:TPU:0, one launch (start us, length us, event | category | flops | bytes accessed | tf_op | source)
XLA Modules:
  0.0 461.1 jit_solution(17022470557269962936)
XLA Ops:
  52.3 5.8 %collective-permute-start.22 = (bf16[128,1280]{1,0:T(8,128)(2,1)S(1)}, bf16[128,1280]{1,0:T(8,128)(2,1)S(1)}, u32[]{:S(2)}, u32[]{:S(2)}) collective-permute-start(bf16[128,1280]{1,0:T(8,128)(2,1)S(1)} %convert_dynamic-update-slice_fusion.refs_8_), channel_id=1, source_target_pairs={{0,16},{4,20},{8,24},{12,28},{16,0},{20,4},{24,8},{28,12},{1,17},{... | collective-permute-start | bytes 983048 | tf_op jit(solution)/shard_map/ppermute | solution.py:43
  67.7 8.5 %shard_map.407 = (bf16[512,1024]{1,0:T(8,128)(2,1)}, bf16[512,1024]{1,0:T(8,128)(2,1)}, bf16[512,1024]{1,0:T(8,128)(2,1)}, bf16[1024,1024]{1,0:T(8,128)(2,1)}, b...) custom-call(bf16[512,1024]{1,0:T(8,128)(2,1)} %get-tuple-element.344.ref, ...), custom_call_target="tpu_custom_call" | custom-call | flops 2147483648 | tf_op jit(solution)/shard_map/pallas_call | solution.py:237
  79.6 7.9 %collective-permute-done.24.source_ref = bf16[128,1280]{1,0:T(8,128)(2,1)} collective-permute-done((bf16[128,1280]{1,0:T(8,128)(2,1)}, bf16[128,1280]{1,0:T(8,128)(2,1)}, u32[]{:S(2)}, u32[]{:S(2)}) %collective-permute-start.24) | collective-permute-done | bytes 327712 | tf_op jit(solution)/shard_map/ppermute | solution.py:43
  103.6 4.8 %collective-permute-done.28.source_ref = bf16[128,1280]{1,0:T(8,128)(2,1)S(1)} collective-permute-done((bf16[128,1280]{1,0:T(8,128)(2,1)}, bf16[128,1280]{1,0:T(8,128)(2,1)S(1)}, u32[]{:S(2)}, u32[]{:S(2)}) %collective-permute-start.28) | collective-permute-done | bytes 327712 | tf_op jit(solution)/shard_map/ppermute | solution.py:43
  110.0 13.0 %shard_map.417 = (bf16[512,1024]{1,0:T(8,128)(2,1)}, bf16[512,256]{1,0:T(8,128)(2,1)}, bf16[2,512,512]{2,1,0:T(8,128)(2,1)}, bf16[512,256]{1,0:T(8,128)(2,1)}, b...) custom-call(s32[1]{0:T(128)} %bitcast.refs_0_.place_ref, ...), custom_call_target="tpu_custom_call" | custom-call | flops 2214592512 | tf_op jit(solution)/shard_map/pallas_call | solution.py:237
  144.7 9.6 %collective-permute-done.40.source_ref = bf16[128,768]{1,0:T(8,128)(2,1)} collective-permute-done((bf16[128,768]{1,0:T(8,128)(2,1)}, bf16[128,768]{1,0:T(8,128)(2,1)}, u32[]{:S(2)}, u32[]{:S(2)}) %collective-permute-start.40) | collective-permute-done | bytes 196640 | tf_op jit(solution)/shard_map/ppermute | solution.py:43
  156.9 5.5 %shard_map.427 = (bf16[512,1024]{1,0:T(8,128)(2,1)}, f32[512,512]{1,0:T(8,128)}, bf16[1024,768]{1,0:T(8,128)(2,1)}, f32[512,256]{1,0:T(8,128)}, f32[8,256]{1,0:T(8,128)}) custom-call(s32[1]{0:T(128)} %bitcast.refs_0_.place_ref, s32[1,4]{1,0:T(1,128)} %refs_1_.9, f32[5,256]{1,0:T(8,128)} %bitcast.61, bf16[128,1024]{1,0:T(8,128)(2,1)} %copy-done.26, ...), custom_call_target="tpu_custom_call" | custom-call | flops 536870912 | tf_op jit(solution)/shard_map/pallas_call | solution.py:237
  187.8 4.7 %collective-permute-done.45.far_ref = bf16[128,1024]{1,0:T(8,128)(2,1)S(1)} collective-permute-done((bf16[128,1024]{1,0:T(8,128)(2,1)S(1)}, bf16[128,1024]{1,0:T(8,128)(2,1)S(1)}, u32[]{:S(2)}, u32[]{:S(2)}) %collective-permute-start.45) | collective-permute-done | bytes 262176 | tf_op jit(solution)/shard_map/ppermute | solution.py:43
  206.8 6.8 %shard_map.438 = (bf16[512,1024]{1,0:T(8,128)(2,1)}, bf16[512,1024]{1,0:T(8,128)(2,1)}, bf16[512,1024]{1,0:T(8,128)(2,1)}, bf16[1024,1024]{1,0:T(8,128)(2,1)}, b...) custom-call(bf16[128,1024]{1,0:T(8,128)(2,1)S(1)} %get-tuple-element, ...), custom_call_target="tpu_custom_call" | custom-call | flops 2147483648 | tf_op jit(solution)/shard_map/pallas_call | solution.py:237
  217.3 6.9 %collective-permute-done.57.far_ref = bf16[128,1024]{1,0:T(8,128)(2,1)S(1)} collective-permute-done((bf16[128,1024]{1,0:T(8,128)(2,1)S(1)}, bf16[128,1024]{1,0:T(8,128)(2,1)S(1)}, u32[]{:S(2)}, u32[]{:S(2)}) %collective-permute-start.57) | collective-permute-done | bytes 262176 | tf_op jit(solution)/shard_map/ppermute | solution.py:43
  225.9 7.0 %collective-permute-done.58.refs_1_ = bf16[128,1024]{1,0:T(8,128)(2,1)S(1)} collective-permute-done((bf16[128,1024]{1,0:T(8,128)(2,1)S(1)}, bf16[128,1024]{1,0:T(8,128)(2,1)S(1)}, u32[]{:S(2)}, u32[]{:S(2)}) %collective-permute-start.58) | collective-permute-done | bytes 262176 | tf_op jit(solution)/shard_map/ppermute | solution.py:43
  234.4 6.9 %shard_map.441 = (bf16[512,1024]{1,0:T(8,128)(2,1)S(1)}, bf16[512,1024]{1,0:T(8,128)(2,1)}, bf16[256,1024]{1,0:T(8,128)(2,1)S(1)}, bf16[128,1024]{1,0:T(8,128)(2,1)S(1)}, f32[128,1024]{1,0:T(8,128)S(1)}) custom-call(bf16[128,1024]{1,0:T(8,128)(2,1)S(1)} %get-tuple-element.305.refs_0_, bf16[128,1024]{1,0:T(8,128)(2,1)S(1)} %collective-permute-done.58.refs_1_, ...), custom_call_target="tpu_custom_call" | custom-call | flops 2147483648 | tf_op jit(solution)/shard_map/pallas_call | solution.py:237
  243.9 7.8 %collective-permute-done.62.far_ref = bf16[128,1024]{1,0:T(8,128)(2,1)S(1)} collective-permute-done((bf16[128,1024]{1,0:T(8,128)(2,1)S(1)}, bf16[128,1024]{1,0:T(8,128)(2,1)S(1)}, u32[]{:S(2)}, u32[]{:S(2)}) %collective-permute-start.62) | collective-permute-done | bytes 262176 | tf_op jit(solution)/shard_map/ppermute | solution.py:43
  279.8 5.0 %shard_map.445 = (bf16[512,512]{1,0:T(8,128)(2,1)S(1)}, f32[8,256]{1,0:T(8,128)S(1)}, bf16[256,1024]{1,0:T(8,128)(2,1)S(1)}, bf16[128,1024]{1,0:T(8,128)(2,1)S(1)}, f32[128,1024]{1,0:T(8,128)S(1)}) custom-call(s32[1]{0:T(128)} %bitcast.refs_0_.place_ref, s32[1,4]{1,0:T(1,128)S(1)} %copy-done.39, f32[5,256]{1,0:T(8,128)S(1)} %bitcast.62, ...), custom_call_target="tpu_custom_call" | custom-call | flops 536870912 | tf_op jit(solution)/shard_map/pallas_call | solution.py:237
  291.8 6.8 %collective-permute-done.70.far_ref = bf16[128,1024]{1,0:T(8,128)(2,1)S(1)} collective-permute-done((bf16[128,1024]{1,0:T(8,128)(2,1)S(1)}, bf16[128,1024]{1,0:T(8,128)(2,1)S(1)}, u32[]{:S(2)}, u32[]{:S(2)}) %collective-permute-start.70) | collective-permute-done | bytes 262176 | tf_op jit(solution)/shard_map/ppermute | solution.py:43
  300.5 5.9 %collective-permute-done.71.refs_2_ = bf16[128,1024]{1,0:T(8,128)(2,1)S(1)} collective-permute-done((bf16[128,1024]{1,0:T(8,128)(2,1)S(1)}, bf16[128,1024]{1,0:T(8,128)(2,1)S(1)}, u32[]{:S(2)}, u32[]{:S(2)}) %collective-permute-start.71) | collective-permute-done | bytes 262176 | tf_op jit(solution)/shard_map/ppermute | solution.py:43
  308.2 12.0 %shard_map.448 = (bf16[512,1024]{1,0:T(8,128)(2,1)}, bf16[512,768]{1,0:T(8,128)(2,1)}, bf16[1024,256]{1,0:T(8,128)(2,1)S(1)}, f32[4,128]{1,0:T(4,128)S(1)}, bf16...) custom-call(s32[1]{0:T(128)} %bitcast.refs_0_.place_ref, ...), custom_call_target="tpu_custom_call" | custom-call | flops 2147483648 | tf_op jit(solution)/shard_map/pallas_call | solution.py:237
  342.6 7.6 %shard_map.451 = (bf16[512,1024]{1,0:T(8,128)(2,1)S(1)}, bf16[512,1024]{1,0:T(8,128)(2,1)}, bf16[256,1024]{1,0:T(8,128)(2,1)S(1)}, bf16[128,1024]{1,0:T(8,128)(2...) custom-call(bf16[128,1024]{1,0:T(8,128)(2,1)} %get-tuple-element.333.refs_0_, ...), custom_call_target="tpu_custom_call" | custom-call | flops 2147483648 | tf_op jit(solution)/shard_map/pallas_call | solution.py:237
  353.4 5.6 %collective-permute-done.91 = bf16[256,768]{1,0:T(8,128)(2,1)S(1)} collective-permute-done((bf16[256,768]{1,0:T(8,128)(2,1)}, bf16[256,768]{1,0:T(8,128)(2,1)S(1)}, u32[]{:S(2)}, u32[]{:S(2)}) %collective-permute-start.91) | collective-permute-done | bytes 393248 | tf_op jit(solution)/shard_map/ppermute | solution.py:43
  368.3 5.4 %collective-permute-done.80.far_ref = bf16[128,1024]{1,0:T(8,128)(2,1)S(1)} collective-permute-done((bf16[128,1024]{1,0:T(8,128)(2,1)S(1)}, bf16[128,1024]{1,0:T(8,128)(2,1)S(1)}, u32[]{:S(2)}, u32[]{:S(2)}) %collective-permute-start.80) | collective-permute-done | bytes 262176 | tf_op jit(solution)/shard_map/ppermute | solution.py:43
  385.8 5.9 %collective-permute-done.98.refs_1_ = bf16[128,1024]{1,0:T(8,128)(2,1)S(1)} collective-permute-done((bf16[128,1024]{1,0:T(8,128)(2,1)}, bf16[128,1024]{1,0:T(8,128)(2,1)S(1)}, u32[]{:S(2)}, u32[]{:S(2)}) %collective-permute-start.98) | collective-permute-done | bytes 262176 | tf_op jit(solution)/shard_map/ppermute | solution.py:43
  398.3 16.2 %collective-permute-done.88 = bf16[256,1024]{1,0:T(8,128)(2,1)S(1)} collective-permute-done((bf16[256,1024]{1,0:T(8,128)(2,1)S(1)}, bf16[256,1024]{1,0:T(8,128)(2,1)S(1)}, u32[]{:S(2)}, u32[]{:S(2)}) %collective-permute-start.88) | collective-permute-done | bytes 524320 | tf_op jit(solution)/shard_map/ppermute | solution.py:43
  422.9 8.1 %collective-permute-done.102.refs_1_ = bf16[128,1024]{1,0:T(8,128)(2,1)S(1)} collective-permute-done((bf16[128,1024]{1,0:T(8,128)(2,1)S(1)}, bf16[128,1024]{1,0:T(8,128)(2,1)S(1)}, u32[]{:S(2)}, u32[]{:S(2)}) %collective-permute-start.102) | collective-permute-done | bytes 262176 | tf_op jit(solution)/shard_map/ppermute | solution.py:43
  433.2 4.5 collective-permute-done.100
  (637 shorter events, 280.3 us)
Async XLA Ops:
  12.5 21.7 %collective-permute-start = (bf16[1,928]{1,0:T(2,128)(2,1)S(1)}, bf16[1,928]{1,0:T(2,128)(2,1)S(1)}, u32[]{:S(2)}, u32[]{:S(2)}) collective-permute-start(bf16[1,928]{1,0:T(2,128)(2,1)S(1)} %broadcast_in_dim.2), channel_id=1, source_target_pairs={{0,16},{4,20},{8,24},{12,28},{16,0},{20,4},{24,8},{28,12},{1,17},{... | collective-permute-start | bytes 5576 | tf_op jit(solution)/shard_map/ppermute | solution.py:43
  52.3 24.0 %collective-permute-start.22 = (bf16[128,1280]{1,0:T(8,128)(2,1)S(1)}, bf16[128,1280]{1,0:T(8,128)(2,1)S(1)}, u32[]{:S(2)}, u32[]{:S(2)}) collective-permute-start(bf16[128,1280]{1,0:T(8,128)(2,1)S(1)} %convert_dynamic-update-slice_fusion.refs_8_), channel_id=1, source_target_pairs={{0,16},{4,20},{8,24},{12,28},{16,0},{20,4},{24,8},{28,12},{1,17},{... | collective-permute-start | bytes 983048 | tf_op jit(solution)/shard_map/ppermute | solution.py:43
  89.7 33.3 %collective-permute-start.34 = (bf16[128,768]{1,0:T(8,128)(2,1)}, bf16[128,768]{1,0:T(8,128)(2,1)}, u32[]{:S(2)}, u32[]{:S(2)}) collective-permute-start(bf16[128,768]{1,0:T(8,128)(2,1)} %pad_maximum_fusion.3.refs_7_), channel_id=1, source_target_pairs={{0,16},{4,20},{8,24},{12,28},{16,0},{20,4},{24,8},{28,12},{1,17},{... | collective-permute-start | bytes 589832 | tf_op jit(solution)/shard_map/ppermute | solution.py:43
  101.5 24.9 %collective-permute-start.35 = (bf16[128,768]{1,0:T(8,128)(2,1)}, bf16[128,768]{1,0:T(8,128)(2,1)S(1)}, u32[]{:S(2)}, u32[]{:S(2)}) collective-permute-start(bf16[128,768]{1,0:T(8,128)(2,1)} %pad_maximum_fusion.3.refs_7_), channel_id=1, source_target_pairs={{0,8},{4,12},{8,0},{12,4},{16,24},{20,28},{24,16},{28,20},{1,9},{5... | collective-permute-start | bytes 589832 | tf_op jit(solution)/shard_map/ppermute | solution.py:43
  135.0 28.0 %collective-permute-start.49 = (bf16[128,2048]{1,0:T(8,128)(2,1)S(1)}, bf16[128,2048]{1,0:T(8,128)(2,1)}, u32[]{:S(2)}, u32[]{:S(2)}) collective-permute-start(bf16[128,2048]{1,0:T(8,128)(2,1)S(1)} %copy-done.2), channel_id=1, source_target_pairs={{0,16},{4,20},{8,24},{12,28},{16,0},{20,4},{24,8},{28,12},{1,17},{... | collective-permute-start | bytes 1572872 | tf_op jit(solution)/shard_map/ppermute | solution.py:43
  137.8 31.0 %collective-permute-start.52 = (bf16[128,2048]{1,0:T(8,128)(2,1)S(1)}, bf16[128,2048]{1,0:T(8,128)(2,1)}, u32[]{:S(2)}, u32[]{:S(2)}) collective-permute-start(bf16[128,2048]{1,0:T(8,128)(2,1)S(1)} %copy-done.2), channel_id=1, source_target_pairs={{0,4},{4,0},{8,12},{12,8},{16,20},{20,16},{24,28},{28,24},{1,5},{5... | collective-permute-start | bytes 1572872 | tf_op jit(solution)/shard_map/ppermute | solution.py:43
  143.2 29.3 %collective-permute-start.50 = (bf16[128,2048]{1,0:T(8,128)(2,1)S(1)}, bf16[128,2048]{1,0:T(8,128)(2,1)}, u32[]{:S(2)}, u32[]{:S(2)}) collective-permute-start(bf16[128,2048]{1,0:T(8,128)(2,1)S(1)} %copy-done.2), channel_id=1, source_target_pairs={{0,8},{4,12},{8,0},{12,4},{16,24},{20,28},{24,16},{28,20},{1,9},{5... | collective-permute-start | bytes 1572872 | tf_op jit(solution)/shard_map/ppermute | solution.py:43
  174.8 24.2 %collective-permute-start.54 = (bf16[128,2048]{1,0:T(8,128)(2,1)}, bf16[128,2048]{1,0:T(8,128)(2,1)}, u32[]{:S(2)}, u32[]{:S(2)}) collective-permute-start(bf16[128,2048]{1,0:T(8,128)(2,1)} %shard_map.432.refs_6_.refs_14_), channel_id=1, source_target_pairs={{0,4},{4,0},{8,12},{12,8},{16,20},{20,16},{24,28},{28,24},{1,5},{5... | collective-permute-start | bytes 1572872 | tf_op jit(solution)/shard_map/ppermute | solution.py:43
  181.9 24.9 %collective-permute-start.55 = (bf16[128,2048]{1,0:T(8,128)(2,1)}, bf16[128,2048]{1,0:T(8,128)(2,1)}, u32[]{:S(2)}, u32[]{:S(2)}) collective-permute-start(bf16[128,2048]{1,0:T(8,128)(2,1)} %shard_map.433.refs_7_.refs_15_), channel_id=1, source_target_pairs={{0,4},{4,0},{8,12},{12,8},{16,20},{20,16},{24,28},{28,24},{1,5},{5... | collective-permute-start | bytes 1572872 | tf_op jit(solution)/shard_map/ppermute | solution.py:43
  255.3 31.4 %collective-permute-start.86 = (bf16[512,1024]{1,0:T(8,128)(2,1)}, bf16[512,1024]{1,0:T(8,128)(2,1)}, u32[]{:S(2)}, u32[]{:S(2)}) collective-permute-start(bf16[512,1024]{1,0:T(8,128)(2,1)} %convolution_convert_fusion.1), channel_id=1, source_target_pairs={{0,4},{4,0},{8,12},{12,8},{16,20},{20,16},{24,28},{28,24},{1,5},{5... | collective-permute-start | bytes 3145736 | tf_op jit(solution)/shard_map/ppermute | solution.py:43
  284.9 49.4 %collective-permute-start.93 = (bf16[512,1024]{1,0:T(8,128)(2,1)}, bf16[512,1024]{1,0:T(8,128)(2,1)S(1)}, u32[]{:S(2)}, u32[]{:S(2)}) collective-permute-start(bf16[512,1024]{1,0:T(8,128)(2,1)} %convolution_convert_fusion), channel_id=1, source_target_pairs={{0,4},{4,0},{8,12},{12,8},{16,20},{20,16},{24,28},{28,24},{1,5},{5... | collective-permute-start | bytes 3145736 | tf_op jit(solution)/shard_map/ppermute | solution.py:43
  288.8 32.1 %collective-permute-start.94 = (bf16[256,1024]{1,0:T(8,128)(2,1)S(1)}, bf16[256,1024]{1,0:T(8,128)(2,1)}, u32[]{:S(2)}, u32[]{:S(2)}) collective-permute-start(bf16[256,1024]{1,0:T(8,128)(2,1)S(1)} %slice.453), channel_id=1, source_target_pairs={{0,8},{4,12},{8,0},{12,4},{16,24},{20,28},{24,16},{28,20},{1,9},{5... | collective-permute-start | bytes 1572872 | tf_op jit(solution)/shard_map/ppermute | solution.py:43
  306.9 22.2 %collective-permute-start.90 = (bf16[512,768]{1,0:T(8,128)(2,1)S(1)}, bf16[512,768]{1,0:T(8,128)(2,1)}, u32[]{:S(2)}, u32[]{:S(2)}) collective-permute-start(bf16[512,768]{1,0:T(8,128)(2,1)S(1)} %pad_maximum_fusion.1), channel_id=1, source_target_pairs={{0,4},{4,0},{8,12},{12,8},{16,20},{20,16},{24,28},{28,24},{1,5},{5... | collective-permute-start | bytes 2359304 | tf_op jit(solution)/shard_map/ppermute | solution.py:43
  323.1 59.2 %collective-permute-start.97 = (bf16[128,1024]{1,0:T(8,128)(2,1)}, bf16[128,1024]{1,0:T(8,128)(2,1)S(1)}, u32[]{:S(2)}, u32[]{:S(2)}) collective-permute-start(bf16[128,1024]{1,0:T(8,128)(2,1)} %slice.460), channel_id=1, source_target_pairs={{0,16},{4,20},{8,24},{12,28},{16,0},{20,4},{24,8},{28,12},{1,17},{... | collective-permute-start | bytes 786440 | tf_op jit(solution)/shard_map/ppermute | solution.py:43
  328.2 37.7 %collective-permute-start.87 = (bf16[512,1280]{1,0:T(8,128)(2,1)}, bf16[512,1280]{1,0:T(8,128)(2,1)}, u32[]{:S(2)}, u32[]{:S(2)}) collective-permute-start(bf16[512,1280]{1,0:T(8,128)(2,1)} %pad_maximum_fusion), channel_id=1, source_target_pairs={{0,4},{4,0},{8,12},{12,8},{16,20},{20,16},{24,28},{28,24},{1,5},{5... | collective-permute-start | bytes 3932168 | tf_op jit(solution)/shard_map/ppermute | solution.py:43
  351.2 30.1 %collective-permute-start.85 = (bf16[512,1024]{1,0:T(8,128)(2,1)S(1)}, bf16[512,1024]{1,0:T(8,128)(2,1)S(1)}, u32[]{:S(2)}, u32[]{:S(2)}) collective-permute-start(bf16[512,1024]{1,0:T(8,128)(2,1)S(1)} %convolution_convert_fusion.2), channel_id=1, source_target_pairs={{0,4},{4,0},{8,12},{12,8},{16,20},{20,16},{24,28},{28,24},{1,5},{5... | collective-permute-start | bytes 3145736 | tf_op jit(solution)/shard_map/ppermute | solution.py:43
  359.2 26.0 %collective-permute-start.96 = (bf16[128,1024]{1,0:T(8,128)(2,1)S(1)}, bf16[128,1024]{1,0:T(8,128)(2,1)S(1)}, u32[]{:S(2)}, u32[]{:S(2)}) collective-permute-start(bf16[128,1024]{1,0:T(8,128)(2,1)S(1)} %slice.461), channel_id=1, source_target_pairs={{0,16},{4,20},{8,24},{12,28},{16,0},{20,4},{24,8},{28,12},{1,17},{... | collective-permute-start | bytes 786440 | tf_op jit(solution)/shard_map/ppermute | solution.py:43
  373.7 22.7 %collective-permute-start.89 = (bf16[256,1280]{1,0:T(8,128)(2,1)S(1)}, bf16[256,1280]{1,0:T(8,128)(2,1)S(1)}, u32[]{:S(2)}, u32[]{:S(2)}) collective-permute-start(bf16[256,1280]{1,0:T(8,128)(2,1)S(1)} %slice.451), channel_id=1, source_target_pairs={{0,8},{4,12},{8,0},{12,4},{16,24},{20,28},{24,16},{28,20},{1,9},{5... | collective-permute-start | bytes 1966088 | tf_op jit(solution)/shard_map/ppermute | solution.py:43
  381.3 34.5 %collective-permute-start.84 = (bf16[512,1024]{1,0:T(8,128)(2,1)S(1)}, bf16[512,1024]{1,0:T(8,128)(2,1)S(1)}, u32[]{:S(2)}, u32[]{:S(2)}) collective-permute-start(bf16[512,1024]{1,0:T(8,128)(2,1)S(1)} %convolution_convert_fusion.3), channel_id=1, source_target_pairs={{0,4},{4,0},{8,12},{12,8},{16,20},{20,16},{24,28},{28,24},{1,5},{5... | collective-permute-start | bytes 3145736 | tf_op jit(solution)/shard_map/ppermute | solution.py:43
  385.1 29.4 %collective-permute-start.88 = (bf16[256,1024]{1,0:T(8,128)(2,1)S(1)}, bf16[256,1024]{1,0:T(8,128)(2,1)S(1)}, u32[]{:S(2)}, u32[]{:S(2)}) collective-permute-start(bf16[256,1024]{1,0:T(8,128)(2,1)S(1)} %slice.455), channel_id=1, source_target_pairs={{0,8},{4,12},{8,0},{12,4},{16,24},{20,28},{24,16},{28,20},{1,9},{5... | collective-permute-start | bytes 1572872 | tf_op jit(solution)/shard_map/ppermute | solution.py:43
  391.7 25.1 %collective-permute-start.99 = (bf16[128,1024]{1,0:T(8,128)(2,1)S(1)}, bf16[128,1024]{1,0:T(8,128)(2,1)S(1)}, u32[]{:S(2)}, u32[]{:S(2)}) collective-permute-start(bf16[128,1024]{1,0:T(8,128)(2,1)S(1)} %collective-permute-done.98.refs_1_), channel_id=1, source_target_pairs={{0,1},{1,0},{2,3},{3,2},{4,5},{5,4},{6,7},{7,6},{8,9},{9,8},{10,11... | collective-permute-start | bytes 786440 | tf_op jit(solution)/shard_map/ppermute | solution.py:43
  395.0 22.5 %collective-permute-start.83 = (bf16[128,1024]{1,0:T(8,128)(2,1)S(1)}, bf16[128,1024]{1,0:T(8,128)(2,1)S(1)}, u32[]{:S(2)}, u32[]{:S(2)}) collective-permute-start(bf16[128,1024]{1,0:T(8,128)(2,1)S(1)} %collective-permute-done.81.refs_1_), channel_id=1, source_target_pairs={{0,1},{1,0},{2,3},{3,2},{4,5},{5,4},{6,7},{7,6},{8,9},{9,8},{10,11... | collective-permute-start | bytes 786440 | tf_op jit(solution)/shard_map/ppermute | solution.py:43
  396.6 36.6 %collective-permute-start.101 = (bf16[128,1280]{1,0:T(8,128)(2,1)S(1)}, bf16[128,1280]{1,0:T(8,128)(2,1)S(1)}, u32[]{:S(2)}, u32[]{:S(2)}) collective-permute-start(bf16[128,1280]{1,0:T(8,128)(2,1)S(1)} %slice.457), channel_id=1, source_target_pairs={{0,16},{4,20},{8,24},{12,28},{16,0},{20,4},{24,8},{28,12},{1,17},{... | collective-permute-start | bytes 983048 | tf_op jit(solution)/shard_map/ppermute | solution.py:43
  418.3 19.4 %collective-permute-start.100 = (bf16[256,1024]{1,0:T(8,128)(2,1)S(1)}, bf16[256,1024]{1,0:T(8,128)(2,1)S(1)}, u32[]{:S(2)}, u32[]{:S(2)}) collective-permute-start(bf16[256,1024]{1,0:T(8,128)(2,1)S(1)} %slice.452), channel_id=1, source_target_pairs={{0,8},{4,12},{8,0},{12,4},{16,24},{20,28},{24,16},{28,20},{1,9},{5... | collective-permute-start | bytes 1572872 | tf_op jit(solution)/shard_map/ppermute | solution.py:43
  (210 other events, 1836.0 us)

commit v5 on v4

--- a/solution.py
+++ b/solution.py
@@ -223,9 +223,9 @@
         for i, ref in zip(saved, held_refs):
             targets[i] = ref
 
-        def save():
-            for copy in copies:
-                copy.start()
+        def save(*which):
+            for n in which:
+                copies[n].start()
 
         kernel(*sources, *targets, *kept, save=save)
         for copy in copies:
@@ -305,6 +305,7 @@
     up_copies = copies.weight(up_refs, up, up_columns)
     down_copies = copies.weight(down_refs, down, down_columns)
     wait(rows_copies + up_copies)
+    save(0, 3)
 
     @tiles(up.shape[1])
     def _(columns):
@@ -312,8 +313,9 @@
         before_ref[:, columns] = before.astype(LOW)
         active_ref[:, columns] = (before * jax.nn.sigmoid(before)).astype(LOW)
 
+    save(1, 2)
     wait(down_copies)
-    save()
+    save(4)
 
     @tiles(down.shape[0])
     def _(features):
@@ -339,6 +341,7 @@
     down_copies = copies.weight(down_refs, down, down_columns)
     up_copies = copies.weight(up_refs, up, up_columns)
     wait(rows_copies + down_copies)
+    save(0)
 
     @tiles(down.shape[1])
     def _(columns):
@@ -347,7 +350,7 @@
         grad = matmul(rows_ref[...], down[:, columns])
         grad_ref[:, columns] = (grad * squashed * (1.0 + before * (1.0 - squashed))).astype(LOW)
 
-    save()
+    save(1)
 
     wait(up_copies)
 
@@ -440,6 +443,7 @@
     table_copy = copies.start(table_ref, table)
     firsts = block_firsts(place_ref, pieces, row_block)
     wait(rows_copies + weight_copies_)
+    save(0, 8)
 
     @tiles(3 * heads)
     def _(columns):
@@ -457,6 +461,8 @@
         rows = pl.ds(q * row_block, row_block)
         key_ref[pl.ds(firsts[q], row_block), :] = qkv[rows, heads : 2 * heads].astype(LOW)
         value_ref[pl.ds(firsts[q], row_block), :] = qkv[rows, 2 * heads :].astype(LOW)
+
+    save(5, 6, 7)
 
     along = lax.broadcasted_iota(jnp.int32, (1, row_count), 1)
     column_segment = segment_of(lengths_ref, along)
@@ -484,7 +490,7 @@
             prob_ref[h, rows, :] = prob
             mixed_ref[rows, columns] = matmul(prob, value_ref[:, columns]).astype(LOW)
 
-    save()
+    save(1, 2, 3, 4)
 
     @tiles(weight.shape[0])
     def _(features):
@@ -549,6 +555,7 @@
         == row_block - 1
     ).astype(LOW)
     wait(rows_copies + weight_copies_)
+    save(0)
     mixed_grad_ref[...] = matmul(rows_ref[...], weight[:, 4 * heads : 5 * heads]).astype(LOW)
     for h in range(head_count):
         columns = slice(h * head_size, (h + 1) * head_size)
@@ -585,7 +592,7 @@
         qkv_grad_ref[rows, 2 * heads :] = value_sum[plain, :].astype(LOW)
     position_grad_ref[...] = (position_sum[...] * scale).astype(LOW)
 
-    save()
+    save(1, 2)
 
     @tiles(weight.shape[0])
     def _(features):
@@ -659,6 +666,7 @@
     padded[:MARGIN, :] = jnp.zeros((MARGIN, channels), FLOAT)
     padded[MARGIN + row_count :, :] = jnp.zeros((MARGIN, channels), FLOAT)
     wait(rows_copies + weight_copies_)
+    save(0, 2)
     lifted = matmul(rows_ref[...], weight[:, : 2 * channels])
     for q in range(pieces):
         lifted_ref[pl.ds(firsts[q], row_block), :] = lifted[q * row_block : (q + 1) * row_block]
@@ -669,7 +677,7 @@
         first = MARGIN + t - taps // 2
         convolved += taps_ref[t : t + 1, :] * matches[t] * padded[first : first + row_count, :]
     convolved_ref[...] = convolved
-    save()
+    save(1)
 
     masked = convolved * valid
     sums_ref[...] = jnp.zeros_like(sums_ref)
@@ -730,7 +738,7 @@
         swished_ref[q * row_block : (q + 1) * row_block, :] = plain[
             pl.ds(firsts[q], row_block), :
         ]
-    save()
+    save(0)
 
     wait(weight_copies_)
 
@@ -783,7 +791,7 @@
     product = matmul(rows_ref[...], weight[...])
     for q in range(pieces):
         plain[pl.ds(firsts[q], row_block), :] = product[q * row_block : (q + 1) * row_block]
-    save()
+    save(0)
 
     normal = plain[...] * valid * squashed * (1.0 + normalized * (1.0 - squashed))
     normal_ref[...] = normal
@@ -860,7 +868,7 @@
         lifted_grad_ref[q * row_block : (q + 1) * row_block, :] = plain[
             pl.ds(firsts[q], row_block), :
         ]
-    save()
+    save(0)
 
     wait(weight_copies_)
 
@@ -1199,7 +1207,7 @@
     _, before_a, active_a, up_a, down_a, hi, next_part, own_part = ffn_call(
         ffn_forward_kernel, [normed_a], ups, downs, whole, whole, room=54
     )
-    attention_spread.go((3, 5), hi, time=10)
+    attention_spread.go((3, 5), hi, time=3)
     parts, sent = sum_rows(hi, next_part, own_part)
     attention_spread.go((6,), sent, time=10)
     attention_spread.go((7,), parts[2], time=10)
@@ -1218,7 +1226,7 @@
     )
     parts, sent = sum_rows(hi, next_part, own_part)
     convolution_spread.go((3, 5, 6), sent, time=10)
-    convolution_spread.go((7,), parts[2], time=10)
+    convolution_spread.go((7,), sent, time=10)
     convolution_all = convolution_spread.blocks
     second_spread.go(ORDER[:3], time=10)
     residual_two, own_c = step(parts, residual_one, convolution_gain, 1.0)
@@ -1282,12 +1290,14 @@
     gain_piece = lax.dynamic_slice_in_dim(back_sums[1], first_row, local_channels)
     shift_piece = lax.dynamic_slice_in_dim(back_sums[0], first_row, local_channels)
 
+    rows = all_rows(branch)
+    rows[0] = after(rows[0], second_down_sum.upper)
     branch_rows, qkv_grad, position_grad, bias_grads, hi, next_part, own_part = attention_backward(
-        place, all_rows(branch), [attention_weight],
+        place, rows, [attention_weight],
         (position, prob, content_rows, position_rows, keys, values), head_count,
     )
     parts, sent = sum_rows(hi, next_part, own_part)
-    convolution_sum.advance(sent, links=links)
+    second_up_sum.advance(sent, links=links)
     residual_grad, branch, attention_gain_grad = step_back(
         parts, residual_one, attention_gain, residual_grad, 0.5
     )
@@ -1297,7 +1307,7 @@
     )
     attention_later = []
     attention_sum.advance(links=links, later=attention_later)
-    second_up_sum.advance(branch, links=links)
+    convolution_sum.advance(branch, links=links)
 
     bias_grads, taps_grad = after((bias_grads, taps_grad), branch)
     plain_grads = jnp.concatenate(
@@ -1390,10 +1400,12 @@
         [hidden, hidden, 2 * channels, channels], last_hop,
     )
     attention_grads = finish([attention_sum], [heads] * 5, last_hop)
-    first_down_grad, first_up_grad = join([first_down_sum]), join([first_up_sum])
+    first_down_grad = join([first_down_sum])
 
     result = select_rows(place, after(result_rows, first_up_sum.upper), LOW)
     inputs_grad = select_rows(place, after(inputs_rows, first_up_sum.upper), FLOAT)
+    first_up_sum.kept = after(first_up_sum.kept, result, inputs_grad, first_down_grad)
+    first_up_grad = join([first_up_sum])
 
     gain_grads, plain_grads = total_over(gain_grads, "mp"), plain_grads[0]
 

time: 468 us -> 453 us (0.968)
  waiting for transfers between devices: 188 us -> 166 us
  starting transfers between devices: 107 us -> 112 us
    ppermute x115, waiting for transfers between devices: 188 us -> 166 us  [swap(): return lax.ppermute(values, axis, [(i, i ^ mask) for i in range(size)])]
    ppermute x115, starting transfers between devices: 107 us -> 112 us  [swap(): return lax.ppermute(values, axis, [(i, i ^ mask) for i in range(size)])]
    unnamed x245 -> x239, local copies, waits for them, and re-layouts: 27.4 us -> 29.1 us
  transfers between devices with their start and end apart: 115 -> 115, of which waited for: 55 -> 56; matrix products, arithmetic and copies ran while one was open for 12% -> 13% of each run, Pallas kernels for 15% -> 15%
where the time goes in v5:
time: 453 us; the launch traced here: 446 us
  waiting for transfers between devices  166 us (37%)
  starting transfers between devices  112 us (25%)
  Pallas kernels  80.4 us (18%)
  local copies, waits for them, and re-layouts  44 us (10%)
  matrix products  24.9 us (5%)
  other arithmetic  16 us (4%)
    ppermute x115, waiting for transfers between devices, swap(): return lax.ppermute(values, axis, [(i, i ^ mask) for i in range(size)])  166 us
    ppermute x115, starting transfers between devices, swap(): return lax.ppermute(values, axis, [(i, i ^ mask) for i in range(size)])  112 us
    pallas_call x32, Pallas kernels, call(): pl.pallas_call(saving if saved else kernel, out_shape=tuple((jax.ShapeDty...  80.4 us
    unnamed x239, local copies, waits for them, and re-layouts  29.1 us
    dot_general x18, matrix products, outer_sum(): lax.dot_general(left_side, right_side, (((0,), (0,)), ((), ())), preferre...  15.1 us
  transfers between devices with their start and end apart: 115, of which 56 were waited for; matrix products, arithmetic and copies ran while one was open for 13% of the time, Pallas kernels for 15%

profile of v5, /device:TPU:0, one launch (start us, length us, event | category | flops | bytes accessed | tf_op | source)
XLA Modules:
  0.0 446.4 jit_solution(16504353186978086569)
XLA Ops:
  22.4 5.0 %collective-permute-done.5.refs_6_ = bf16[128,1024]{1,0:T(8,128)(2,1)S(1)} collective-permute-done((bf16[128,1024]{1,0:T(8,128)(2,1)S(1)}, bf16[128,1024]{1,0:T(8,128)(2,1)S(1)}, u32[]{:S(2)}, u32[]{:S(2)}) %collective-permute-start.5) | collective-permute-done | bytes 262176 | tf_op jit(solution)/shard_map/ppermute | solution.py:43
  52.7 5.3 %collective-permute-start.22 = (bf16[128,1280]{1,0:T(8,128)(2,1)}, bf16[128,1280]{1,0:T(8,128)(2,1)}, u32[]{:S(2)}, u32[]{:S(2)}) collective-permute-start(bf16[128,1280]{1,0:T(8,128)(2,1)} %convert_dynamic-update-slice_fusion.refs_8_), channel_id=1, source_target_pairs={{0,16},{4,20},{8,24},{12,28},{16,0},{20,4},{24,8},{28,12},{1,17},{... | collective-permute-start | bytes 983048 | tf_op jit(solution)/shard_map/ppermute | solution.py:43
  68.0 7.4 %shard_map.407 = (bf16[512,1024]{1,0:T(8,128)(2,1)}, bf16[512,1024]{1,0:T(8,128)(2,1)}, bf16[512,1024]{1,0:T(8,128)(2,1)}, bf16[1024,1024]{1,0:T(8,128)(2,1)}, b...) custom-call(bf16[512,1024]{1,0:T(8,128)(2,1)} %get-tuple-element.352.ref, ...), custom_call_target="tpu_custom_call" | custom-call | flops 2147483648 | tf_op jit(solution)/shard_map/pallas_call | solution.py:237
  77.8 8.2 %collective-permute-done.24.source_ref = bf16[128,1280]{1,0:T(8,128)(2,1)} collective-permute-done((bf16[128,1280]{1,0:T(8,128)(2,1)}, bf16[128,1280]{1,0:T(8,128)(2,1)}, u32[]{:S(2)}, u32[]{:S(2)}) %collective-permute-start.24) | collective-permute-done | bytes 327712 | tf_op jit(solution)/shard_map/ppermute | solution.py:43
  102.2 5.2 %collective-permute-done.28.source_ref = bf16[128,1280]{1,0:T(8,128)(2,1)S(1)} collective-permute-done((bf16[128,1280]{1,0:T(8,128)(2,1)}, bf16[128,1280]{1,0:T(8,128)(2,1)S(1)}, u32[]{:S(2)}, u32[]{:S(2)}) %collective-permute-start.28) | collective-permute-done | bytes 327712 | tf_op jit(solution)/shard_map/ppermute | solution.py:43
  108.8 11.7 %shard_map.417 = (bf16[512,1024]{1,0:T(8,128)(2,1)}, bf16[512,256]{1,0:T(8,128)(2,1)}, bf16[2,512,512]{2,1,0:T(8,128)(2,1)}, bf16[512,256]{1,0:T(8,128)(2,1)}, b...) custom-call(s32[1]{0:T(128)} %bitcast.refs_0_.place_ref, ...), custom_call_target="tpu_custom_call" | custom-call | flops 2214592512 | tf_op jit(solution)/shard_map/pallas_call | solution.py:237
  126.7 4.1 collective-permute-done.38.source_ref
  147.8 5.1 %shard_map.427 = (bf16[512,1024]{1,0:T(8,128)(2,1)}, f32[512,512]{1,0:T(8,128)}, bf16[1024,768]{1,0:T(8,128)(2,1)}, f32[512,256]{1,0:T(8,128)}, f32[8,256]{1,0:T(8,128)}) custom-call(s32[1]{0:T(128)} %bitcast.refs_0_.place_ref, s32[1,4]{1,0:T(1,128)} %refs_1_.9, f32[5,256]{1,0:T(8,128)} %bitcast.61, bf16[128,1024]{1,0:T(8,128)(2,1)} %copy-done.25, ...), custom_call_target="tpu_custom_call" | custom-call | flops 536870912 | tf_op jit(solution)/shard_map/pallas_call | solution.py:237
  153.0 4.2 collective-permute-done.49.source_ref
  179.6 4.7 %collective-permute-done.45.far_ref = bf16[128,1024]{1,0:T(8,128)(2,1)S(1)} collective-permute-done((bf16[128,1024]{1,0:T(8,128)(2,1)S(1)}, bf16[128,1024]{1,0:T(8,128)(2,1)S(1)}, u32[]{:S(2)}, u32[]{:S(2)}) %collective-permute-start.45) | collective-permute-done | bytes 262176 | tf_op jit(solution)/shard_map/ppermute | solution.py:43
  190.8 4.2 collective-permute-done.46.refs_1_
  197.8 5.7 %shard_map.438 = (bf16[512,1024]{1,0:T(8,128)(2,1)}, bf16[512,1024]{1,0:T(8,128)(2,1)}, bf16[512,1024]{1,0:T(8,128)(2,1)}, bf16[1024,1024]{1,0:T(8,128)(2,1)}, b...) custom-call(bf16[128,1024]{1,0:T(8,128)(2,1)S(1)} %get-tuple-element, ...), custom_call_target="tpu_custom_call" | custom-call | flops 2147483648 | tf_op jit(solution)/shard_map/pallas_call | solution.py:237
  207.8 6.2 %collective-permute-done.57.far_ref = bf16[128,1024]{1,0:T(8,128)(2,1)S(1)} collective-permute-done((bf16[128,1024]{1,0:T(8,128)(2,1)S(1)}, bf16[128,1024]{1,0:T(8,128)(2,1)S(1)}, u32[]{:S(2)}, u32[]{:S(2)}) %collective-permute-start.57) | collective-permute-done | bytes 262176 | tf_op jit(solution)/shard_map/ppermute | solution.py:43
  216.4 6.3 %collective-permute-done.58.refs_1_ = bf16[128,1024]{1,0:T(8,128)(2,1)S(1)} collective-permute-done((bf16[128,1024]{1,0:T(8,128)(2,1)S(1)}, bf16[128,1024]{1,0:T(8,128)(2,1)S(1)}, u32[]{:S(2)}, u32[]{:S(2)}) %collective-permute-start.58) | collective-permute-done | bytes 262176 | tf_op jit(solution)/shard_map/ppermute | solution.py:43
  224.2 6.9 %shard_map.441 = (bf16[512,1024]{1,0:T(8,128)(2,1)S(1)}, bf16[512,1024]{1,0:T(8,128)(2,1)}, bf16[256,1024]{1,0:T(8,128)(2,1)S(1)}, bf16[128,1024]{1,0:T(8,128)(2,1)S(1)}, f32[128,1024]{1,0:T(8,128)S(1)}) custom-call(bf16[128,1024]{1,0:T(8,128)(2,1)S(1)} %get-tuple-element.307.refs_0_, bf16[128,1024]{1,0:T(8,128)(2,1)S(1)} %collective-permute-done.58.refs_1_, ...), custom_call_target="tpu_custom_call" | custom-call | flops 2147483648 | tf_op jit(solution)/shard_map/pallas_call | solution.py:237
  234.4 7.2 %collective-permute-done.62.far_ref = bf16[128,1024]{1,0:T(8,128)(2,1)S(1)} collective-permute-done((bf16[128,1024]{1,0:T(8,128)(2,1)S(1)}, bf16[128,1024]{1,0:T(8,128)(2,1)S(1)}, u32[]{:S(2)}, u32[]{:S(2)}) %collective-permute-start.62) | collective-permute-done | bytes 262176 | tf_op jit(solution)/shard_map/ppermute | solution.py:43
  270.3 5.0 %shard_map.445 = (bf16[512,512]{1,0:T(8,128)(2,1)S(1)}, f32[8,256]{1,0:T(8,128)S(1)}, bf16[256,1024]{1,0:T(8,128)(2,1)S(1)}, bf16[128,1024]{1,0:T(8,128)(2,1)S(1)}, f32[128,1024]{1,0:T(8,128)S(1)}) custom-call(s32[1]{0:T(128)} %bitcast.refs_0_.place_ref, s32[1,4]{1,0:T(1,128)S(1)} %copy-done.38, f32[5,256]{1,0:T(8,128)S(1)} %bitcast.62, ...), custom_call_target="tpu_custom_call" | custom-call | flops 536870912 | tf_op jit(solution)/shard_map/pallas_call | solution.py:237
  281.4 6.5 %collective-permute-done.70.far_ref = bf16[128,1024]{1,0:T(8,128)(2,1)S(1)} collective-permute-done((bf16[128,1024]{1,0:T(8,128)(2,1)S(1)}, bf16[128,1024]{1,0:T(8,128)(2,1)S(1)}, u32[]{:S(2)}, u32[]{:S(2)}) %collective-permute-start.70) | collective-permute-done | bytes 262176 | tf_op jit(solution)/shard_map/ppermute | solution.py:43
  297.3 12.1 %shard_map.448 = (bf16[512,1024]{1,0:T(8,128)(2,1)}, bf16[512,768]{1,0:T(8,128)(2,1)}, bf16[1024,256]{1,0:T(8,128)(2,1)S(1)}, f32[4,128]{1,0:T(4,128)S(1)}, bf16...) custom-call(s32[1]{0:T(128)} %bitcast.refs_0_.place_ref, ...), custom_call_target="tpu_custom_call" | custom-call | flops 2147483648 | tf_op jit(solution)/shard_map/pallas_call | solution.py:237
  338.2 7.6 %shard_map.451 = (bf16[512,1024]{1,0:T(8,128)(2,1)S(1)}, bf16[512,1024]{1,0:T(8,128)(2,1)}, bf16[256,1024]{1,0:T(8,128)(2,1)S(1)}, bf16[128,1024]{1,0:T(8,128)(2...) custom-call(bf16[128,1024]{1,0:T(8,128)(2,1)S(1)} %get-tuple-element.341.refs_0_, ...), custom_call_target="tpu_custom_call" | custom-call | flops 2147483648 | tf_op jit(solution)/shard_map/pallas_call | solution.py:237
  358.2 5.1 %collective-permute-done.82.far_ref = bf16[128,1024]{1,0:T(8,128)(2,1)S(1)} collective-permute-done((bf16[128,1024]{1,0:T(8,128)(2,1)S(1)}, bf16[128,1024]{1,0:T(8,128)(2,1)S(1)}, u32[]{:S(2)}, u32[]{:S(2)}) %collective-permute-start.82) | collective-permute-done | bytes 262176 | tf_op jit(solution)/shard_map/ppermute | solution.py:43
  377.7 5.1 %collective-permute-done.98.refs_1_ = bf16[128,1024]{1,0:T(8,128)(2,1)S(1)} collective-permute-done((bf16[128,1024]{1,0:T(8,128)(2,1)}, bf16[128,1024]{1,0:T(8,128)(2,1)S(1)}, u32[]{:S(2)}, u32[]{:S(2)}) %collective-permute-start.98) | collective-permute-done | bytes 262176 | tf_op jit(solution)/shard_map/ppermute | solution.py:43
  388.3 10.6 %collective-permute-done.89 = bf16[256,1024]{1,0:T(8,128)(2,1)S(1)} collective-permute-done((bf16[256,1024]{1,0:T(8,128)(2,1)S(1)}, bf16[256,1024]{1,0:T(8,128)(2,1)S(1)}, u32[]{:S(2)}, u32[]{:S(2)}) %collective-permute-start.89) | collective-permute-done | bytes 524320 | tf_op jit(solution)/shard_map/ppermute | solution.py:43
  407.3 9.0 %collective-permute-done.102.refs_1_ = bf16[128,1024]{1,0:T(8,128)(2,1)S(1)} collective-permute-done((bf16[128,1024]{1,0:T(8,128)(2,1)S(1)}, bf16[128,1024]{1,0:T(8,128)(2,1)S(1)}, u32[]{:S(2)}, u32[]{:S(2)}) %collective-permute-start.102) | collective-permute-done | bytes 262176 | tf_op jit(solution)/shard_map/ppermute | solution.py:43
  (631 shorter events, 285.4 us)
Async XLA Ops:
  12.5 22.3 %collective-permute-start = (bf16[1,928]{1,0:T(2,128)(2,1)S(1)}, bf16[1,928]{1,0:T(2,128)(2,1)S(1)}, u32[]{:S(2)}, u32[]{:S(2)}) collective-permute-start(bf16[1,928]{1,0:T(2,128)(2,1)S(1)} %broadcast_in_dim.2), channel_id=1, source_target_pairs={{0,16},{4,20},{8,24},{12,28},{16,0},{20,4},{24,8},{28,12},{1,17},{... | collective-permute-start | bytes 5576 | tf_op jit(solution)/shard_map/ppermute | solution.py:43
  52.7 22.8 %collective-permute-start.22 = (bf16[128,1280]{1,0:T(8,128)(2,1)}, bf16[128,1280]{1,0:T(8,128)(2,1)}, u32[]{:S(2)}, u32[]{:S(2)}) collective-permute-start(bf16[128,1280]{1,0:T(8,128)(2,1)} %convert_dynamic-update-slice_fusion.refs_8_), channel_id=1, source_target_pairs={{0,16},{4,20},{8,24},{12,28},{16,0},{20,4},{24,8},{28,12},{1,17},{... | collective-permute-start | bytes 983048 | tf_op jit(solution)/shard_map/ppermute | solution.py:43
  88.1 32.6 %collective-permute-start.34 = (bf16[128,768]{1,0:T(8,128)(2,1)}, bf16[128,768]{1,0:T(8,128)(2,1)}, u32[]{:S(2)}, u32[]{:S(2)}) collective-permute-start(bf16[128,768]{1,0:T(8,128)(2,1)} %pad_maximum_fusion.3.refs_7_), channel_id=1, source_target_pairs={{0,16},{4,20},{8,24},{12,28},{16,0},{20,4},{24,8},{28,12},{1,17},{... | collective-permute-start | bytes 589832 | tf_op jit(solution)/shard_map/ppermute | solution.py:43
  100.2 24.3 %collective-permute-start.35 = (bf16[128,768]{1,0:T(8,128)(2,1)}, bf16[128,768]{1,0:T(8,128)(2,1)}, u32[]{:S(2)}, u32[]{:S(2)}) collective-permute-start(bf16[128,768]{1,0:T(8,128)(2,1)} %pad_maximum_fusion.3.refs_7_), channel_id=1, source_target_pairs={{0,8},{4,12},{8,0},{12,4},{16,24},{20,28},{24,16},{28,20},{1,9},{5... | collective-permute-start | bytes 589832 | tf_op jit(solution)/shard_map/ppermute | solution.py:43
  131.7 25.5 %collective-permute-start.49 = (bf16[128,2048]{1,0:T(8,128)(2,1)S(1)}, bf16[128,2048]{1,0:T(8,128)(2,1)}, u32[]{:S(2)}, u32[]{:S(2)}) collective-permute-start(bf16[128,2048]{1,0:T(8,128)(2,1)S(1)} %pad_maximum_fusion.2.refs_4_.refs_12_), channel_id=1, source_target_pairs={{0,16},{4,20},{8,24},{12,28},{16,0},{20,4},{24,8},{28,12},{1,17},{... | collective-permute-start | bytes 1572872 | tf_op jit(solution)/shard_map/ppermute | solution.py:43
  135.9 23.5 %collective-permute-start.52 = (bf16[128,2048]{1,0:T(8,128)(2,1)S(1)}, bf16[128,2048]{1,0:T(8,128)(2,1)}, u32[]{:S(2)}, u32[]{:S(2)}) collective-permute-start(bf16[128,2048]{1,0:T(8,128)(2,1)S(1)} %pad_maximum_fusion.2.refs_4_.refs_12_), channel_id=1, source_target_pairs={{0,4},{4,0},{8,12},{12,8},{16,20},{20,16},{24,28},{28,24},{1,5},{5... | collective-permute-start | bytes 1572872 | tf_op jit(solution)/shard_map/ppermute | solution.py:43
  140.2 24.2 %collective-permute-start.50 = (bf16[128,2048]{1,0:T(8,128)(2,1)S(1)}, bf16[128,2048]{1,0:T(8,128)(2,1)}, u32[]{:S(2)}, u32[]{:S(2)}) collective-permute-start(bf16[128,2048]{1,0:T(8,128)(2,1)S(1)} %pad_maximum_fusion.2.refs_4_.refs_12_), channel_id=1, source_target_pairs={{0,8},{4,12},{8,0},{12,4},{16,24},{20,28},{24,16},{28,20},{1,9},{5... | collective-permute-start | bytes 1572872 | tf_op jit(solution)/shard_map/ppermute | solution.py:43
  166.7 24.1 %collective-permute-start.54 = (bf16[128,2048]{1,0:T(8,128)(2,1)}, bf16[128,2048]{1,0:T(8,128)(2,1)}, u32[]{:S(2)}, u32[]{:S(2)}) collective-permute-start(bf16[128,2048]{1,0:T(8,128)(2,1)} %shard_map.432.refs_6_.refs_14_), channel_id=1, source_target_pairs={{0,4},{4,0},{8,12},{12,8},{16,20},{20,16},{24,28},{28,24},{1,5},{5... | collective-permute-start | bytes 1572872 | tf_op jit(solution)/shard_map/ppermute | solution.py:43
  173.7 24.1 %collective-permute-start.55 = (bf16[128,2048]{1,0:T(8,128)(2,1)}, bf16[128,2048]{1,0:T(8,128)(2,1)}, u32[]{:S(2)}, u32[]{:S(2)}) collective-permute-start(bf16[128,2048]{1,0:T(8,128)(2,1)} %shard_map.433.refs_7_.refs_15_), channel_id=1, source_target_pairs={{0,4},{4,0},{8,12},{12,8},{16,20},{20,16},{24,28},{28,24},{1,5},{5... | collective-permute-start | bytes 1572872 | tf_op jit(solution)/shard_map/ppermute | solution.py:43
  245.8 31.2 %collective-permute-start.71 = (bf16[512,1024]{1,0:T(8,128)(2,1)}, bf16[512,1024]{1,0:T(8,128)(2,1)}, u32[]{:S(2)}, u32[]{:S(2)}) collective-permute-start(bf16[512,1024]{1,0:T(8,128)(2,1)} %convolution_convert_fusion.3), channel_id=1, source_target_pairs={{0,4},{4,0},{8,12},{12,8},{16,20},{20,16},{24,28},{28,24},{1,5},{5... | collective-permute-start | bytes 3145736 | tf_op jit(solution)/shard_map/ppermute | solution.py:43
  275.4 43.8 %collective-permute-start.94 = (bf16[512,1024]{1,0:T(8,128)(2,1)}, bf16[512,1024]{1,0:T(8,128)(2,1)S(1)}, u32[]{:S(2)}, u32[]{:S(2)}) collective-permute-start(bf16[512,1024]{1,0:T(8,128)(2,1)} %convolution_convert_fusion), channel_id=1, source_target_pairs={{0,4},{4,0},{8,12},{12,8},{16,20},{20,16},{24,28},{28,24},{1,5},{5... | collective-permute-start | bytes 3145736 | tf_op jit(solution)/shard_map/ppermute | solution.py:43
  290.0 34.1 %collective-permute-start.91 = (bf16[512,768]{1,0:T(8,128)(2,1)S(1)}, bf16[512,768]{1,0:T(8,128)(2,1)}, u32[]{:S(2)}, u32[]{:S(2)}) collective-permute-start(bf16[512,768]{1,0:T(8,128)(2,1)S(1)} %pad_maximum_fusion.1), channel_id=1, source_target_pairs={{0,4},{4,0},{8,12},{12,8},{16,20},{20,16},{24,28},{28,24},{1,5},{5... | collective-permute-start | bytes 2359304 | tf_op jit(solution)/shard_map/ppermute | solution.py:43
  310.4 62.9 %collective-permute-start.97 = (bf16[128,1024]{1,0:T(8,128)(2,1)}, bf16[128,1024]{1,0:T(8,128)(2,1)S(1)}, u32[]{:S(2)}, u32[]{:S(2)}) collective-permute-start(bf16[128,1024]{1,0:T(8,128)(2,1)} %slice.461), channel_id=1, source_target_pairs={{0,16},{4,20},{8,24},{12,28},{16,0},{20,4},{24,8},{28,12},{1,17},{... | collective-permute-start | bytes 786440 | tf_op jit(solution)/shard_map/ppermute | solution.py:43
  318.2 37.4 %collective-permute-start.88 = (bf16[512,1280]{1,0:T(8,128)(2,1)}, bf16[512,1280]{1,0:T(8,128)(2,1)}, u32[]{:S(2)}, u32[]{:S(2)}) collective-permute-start(bf16[512,1280]{1,0:T(8,128)(2,1)} %pad_maximum_fusion), channel_id=1, source_target_pairs={{0,4},{4,0},{8,12},{12,8},{16,20},{20,16},{24,28},{28,24},{1,5},{5... | collective-permute-start | bytes 3932168 | tf_op jit(solution)/shard_map/ppermute | solution.py:43
  320.9 26.0 %collective-permute-start.95 = (bf16[256,1024]{1,0:T(8,128)(2,1)}, bf16[256,1024]{1,0:T(8,128)(2,1)}, u32[]{:S(2)}, u32[]{:S(2)}) collective-permute-start(bf16[256,1024]{1,0:T(8,128)(2,1)} %slice.453), channel_id=1, source_target_pairs={{0,8},{4,12},{8,0},{12,4},{16,24},{20,28},{24,16},{28,20},{1,9},{5... | collective-permute-start | bytes 1572872 | tf_op jit(solution)/shard_map/ppermute | solution.py:43
  346.9 25.3 %collective-permute-start.87 = (bf16[512,1024]{1,0:T(8,128)(2,1)S(1)}, bf16[512,1024]{1,0:T(8,128)(2,1)S(1)}, u32[]{:S(2)}, u32[]{:S(2)}) collective-permute-start(bf16[512,1024]{1,0:T(8,128)(2,1)S(1)} %convolution_convert_fusion.1), channel_id=1, source_target_pairs={{0,4},{4,0},{8,12},{12,8},{16,20},{20,16},{24,28},{28,24},{1,5},{5... | collective-permute-start | bytes 3145736 | tf_op jit(solution)/shard_map/ppermute | solution.py:43
  349.5 26.7 %collective-permute-start.96 = (bf16[128,1024]{1,0:T(8,128)(2,1)S(1)}, bf16[128,1024]{1,0:T(8,128)(2,1)S(1)}, u32[]{:S(2)}, u32[]{:S(2)}) collective-permute-start(bf16[128,1024]{1,0:T(8,128)(2,1)S(1)} %slice.460), channel_id=1, source_target_pairs={{0,16},{4,20},{8,24},{12,28},{16,0},{20,4},{24,8},{28,12},{1,17},{... | collective-permute-start | bytes 786440 | tf_op jit(solution)/shard_map/ppermute | solution.py:43
  353.9 20.2 %collective-permute-start.93 = (bf16[128,768]{1,0:T(8,128)(2,1)S(1)}, bf16[128,768]{1,0:T(8,128)(2,1)S(1)}, u32[]{:S(2)}, u32[]{:S(2)}) collective-permute-start(bf16[128,768]{1,0:T(8,128)(2,1)S(1)} %slice.463), channel_id=1, source_target_pairs={{0,16},{4,20},{8,24},{12,28},{16,0},{20,4},{24,8},{28,12},{1,17},{... | collective-permute-start | bytes 589832 | tf_op jit(solution)/shard_map/ppermute | solution.py:43
  363.4 23.4 %collective-permute-start.90 = (bf16[256,1280]{1,0:T(8,128)(2,1)S(1)}, bf16[256,1280]{1,0:T(8,128)(2,1)S(1)}, u32[]{:S(2)}, u32[]{:S(2)}) collective-permute-start(bf16[256,1280]{1,0:T(8,128)(2,1)S(1)} %slice.451), channel_id=1, source_target_pairs={{0,8},{4,12},{8,0},{12,4},{16,24},{20,28},{24,16},{28,20},{1,9},{5... | collective-permute-start | bytes 1966088 | tf_op jit(solution)/shard_map/ppermute | solution.py:43
  372.2 27.8 %collective-permute-start.86 = (bf16[512,1024]{1,0:T(8,128)(2,1)S(1)}, bf16[512,1024]{1,0:T(8,128)(2,1)S(1)}, u32[]{:S(2)}, u32[]{:S(2)}) collective-permute-start(bf16[512,1024]{1,0:T(8,128)(2,1)S(1)} %convolution_convert_fusion.2), channel_id=1, source_target_pairs={{0,4},{4,0},{8,12},{12,8},{16,20},{20,16},{24,28},{28,24},{1,5},{5... | collective-permute-start | bytes 3145736 | tf_op jit(solution)/shard_map/ppermute | solution.py:43
  376.2 22.7 %collective-permute-start.89 = (bf16[256,1024]{1,0:T(8,128)(2,1)S(1)}, bf16[256,1024]{1,0:T(8,128)(2,1)S(1)}, u32[]{:S(2)}, u32[]{:S(2)}) collective-permute-start(bf16[256,1024]{1,0:T(8,128)(2,1)S(1)} %slice.454), channel_id=1, source_target_pairs={{0,8},{4,12},{8,0},{12,4},{16,24},{20,28},{24,16},{28,20},{1,9},{5... | collective-permute-start | bytes 1572872 | tf_op jit(solution)/shard_map/ppermute | solution.py:43
  387.3 31.7 %collective-permute-start.101 = (bf16[128,1280]{1,0:T(8,128)(2,1)S(1)}, bf16[128,1280]{1,0:T(8,128)(2,1)S(1)}, u32[]{:S(2)}, u32[]{:S(2)}) collective-permute-start(bf16[128,1280]{1,0:T(8,128)(2,1)S(1)} %slice.457), channel_id=1, source_target_pairs={{0,16},{4,20},{8,24},{12,28},{16,0},{20,4},{24,8},{28,12},{1,17},{... | collective-permute-start | bytes 983048 | tf_op jit(solution)/shard_map/ppermute | solution.py:43
  402.1 20.7 %collective-permute-start.100 = (bf16[256,1024]{1,0:T(8,128)(2,1)S(1)}, bf16[256,1024]{1,0:T(8,128)(2,1)S(1)}, u32[]{:S(2)}, u32[]{:S(2)}) collective-permute-start(bf16[256,1024]{1,0:T(8,128)(2,1)S(1)} %slice.452), channel_id=1, source_target_pairs={{0,8},{4,12},{8,0},{12,4},{16,24},{20,28},{24,16},{28,20},{1,9},{5... | collective-permute-start | bytes 1572872 | tf_op jit(solution)/shard_map/ppermute | solution.py:43
  405.3 20.5 %collective-permute-start.109 = (f32[1,224]{1,0:T(1,128)S(1)}, f32[1,224]{1,0:T(1,128)S(1)}, u32[]{:S(2)}, u32[]{:S(2)}) collective-permute-start(f32[1,224]{1,0:T(1,128)S(1)} %get-tuple-element.510), channel_id=1, source_target_pairs={{0,8},{4,12},{8,0},{12,4},{16,24},{20,28},{24,16},{28,20},{1,9},{5... | collective-permute-start | bytes 2696 | tf_op jit(solution)/shard_map/ppermute | solution.py:43
  (207 other events, 1744.4 us)

commit v6 on v5

--- a/solution.py
+++ b/solution.py
@@ -1397,7 +1397,7 @@
 
     second_down_grad, second_up_grad, convolution_in_grad, convolution_out_grad = finish(
         [second_down_sum, second_up_sum, convolution_sum],
-        [hidden, hidden, 2 * channels, channels], last_hop,
+        [hidden, hidden, 2 * channels, channels], attention_sum.sent,
     )
     attention_grads = finish([attention_sum], [heads] * 5, last_hop)
     first_down_grad = join([first_down_sum])

time: 453 us -> 453 us (level)
    unnamed x239 -> x231, local copies, waits for them, and re-layouts: 29.1 us -> 24.2 us
  transfers between devices with their start and end apart: 115 -> 115, of which waited for: 56 -> 59; matrix products, arithmetic and copies ran while one was open for 13% -> 14% of each run, Pallas kernels for 15% -> 15%
where the time goes in v6:
time: 453 us; the launch traced here: 446 us
  waiting for transfers between devices  169 us (37%)
  starting transfers between devices  109 us (24%)
  Pallas kernels  79.6 us (18%)
  local copies, waits for them, and re-layouts  41.4 us (9%)
  matrix products  27.6 us (6%)
  other arithmetic  16.6 us (4%)
    ppermute x115, waiting for transfers between devices, swap(): return lax.ppermute(values, axis, [(i, i ^ mask) for i in range(size)])  169 us
    ppermute x115, starting transfers between devices, swap(): return lax.ppermute(values, axis, [(i, i ^ mask) for i in range(size)])  109 us
    pallas_call x32, Pallas kernels, call(): pl.pallas_call(saving if saved else kernel, out_shape=tuple((jax.ShapeDty...  79.6 us
    unnamed x231, local copies, waits for them, and re-layouts  24.2 us
    dot_general x18, matrix products, outer_sum(): lax.dot_general(left_side, right_side, (((0,), (0,)), ((), ())), preferre...  18.4 us
  transfers between devices with their start and end apart: 115, of which 59 were waited for; matrix products, arithmetic and copies ran while one was open for 14% of the time, Pallas kernels for 15%

profile of v6, /device:TPU:0, one launch (start us, length us, event | category | flops | bytes accessed | tf_op | source)
XLA Modules:
  0.0 446.1 jit_solution(8589582062741809143)
XLA Ops:
  22.4 5.0 %collective-permute-done.5.refs_6_ = bf16[128,1024]{1,0:T(8,128)(2,1)S(1)} collective-permute-done((bf16[128,1024]{1,0:T(8,128)(2,1)S(1)}, bf16[128,1024]{1,0:T(8,128)(2,1)S(1)}, u32[]{:S(2)}, u32[]{:S(2)}) %collective-permute-start.5) | collective-permute-done | bytes 262176 | tf_op jit(solution)/shard_map/ppermute | solution.py:43
  52.7 5.3 %collective-permute-start.22 = (bf16[128,1280]{1,0:T(8,128)(2,1)}, bf16[128,1280]{1,0:T(8,128)(2,1)}, u32[]{:S(2)}, u32[]{:S(2)}) collective-permute-start(bf16[128,1280]{1,0:T(8,128)(2,1)} %convert_dynamic-update-slice_fusion.refs_8_), channel_id=1, source_target_pairs={{0,16},{4,20},{8,24},{12,28},{16,0},{20,4},{24,8},{28,12},{1,17},{... | collective-permute-start | bytes 983048 | tf_op jit(solution)/shard_map/ppermute | solution.py:43
  68.0 7.4 %shard_map.407 = (bf16[512,1024]{1,0:T(8,128)(2,1)}, bf16[512,1024]{1,0:T(8,128)(2,1)}, bf16[512,1024]{1,0:T(8,128)(2,1)}, bf16[1024,1024]{1,0:T(8,128)(2,1)}, b...) custom-call(bf16[512,1024]{1,0:T(8,128)(2,1)} %get-tuple-element.352.ref, ...), custom_call_target="tpu_custom_call" | custom-call | flops 2147483648 | tf_op jit(solution)/shard_map/pallas_call | solution.py:237
  77.8 8.2 %collective-permute-done.24.source_ref = bf16[128,1280]{1,0:T(8,128)(2,1)} collective-permute-done((bf16[128,1280]{1,0:T(8,128)(2,1)}, bf16[128,1280]{1,0:T(8,128)(2,1)}, u32[]{:S(2)}, u32[]{:S(2)}) %collective-permute-start.24) | collective-permute-done | bytes 327712 | tf_op jit(solution)/shard_map/ppermute | solution.py:43
  102.2 5.2 %collective-permute-done.28.source_ref = bf16[128,1280]{1,0:T(8,128)(2,1)S(1)} collective-permute-done((bf16[128,1280]{1,0:T(8,128)(2,1)}, bf16[128,1280]{1,0:T(8,128)(2,1)S(1)}, u32[]{:S(2)}, u32[]{:S(2)}) %collective-permute-start.28) | collective-permute-done | bytes 327712 | tf_op jit(solution)/shard_map/ppermute | solution.py:43
  108.8 11.7 %shard_map.417 = (bf16[512,1024]{1,0:T(8,128)(2,1)}, bf16[512,256]{1,0:T(8,128)(2,1)}, bf16[2,512,512]{2,1,0:T(8,128)(2,1)}, bf16[512,256]{1,0:T(8,128)(2,1)}, b...) custom-call(s32[1]{0:T(128)} %bitcast.refs_0_.place_ref, ...), custom_call_target="tpu_custom_call" | custom-call | flops 2214592512 | tf_op jit(solution)/shard_map/pallas_call | solution.py:237
  126.7 4.1 collective-permute-done.38.source_ref
  147.8 5.1 %shard_map.427 = (bf16[512,1024]{1,0:T(8,128)(2,1)}, f32[512,512]{1,0:T(8,128)}, bf16[1024,768]{1,0:T(8,128)(2,1)}, f32[512,256]{1,0:T(8,128)}, f32[8,256]{1,0:T(8,128)}) custom-call(s32[1]{0:T(128)} %bitcast.refs_0_.place_ref, s32[1,4]{1,0:T(1,128)} %refs_1_.9, f32[5,256]{1,0:T(8,128)} %bitcast.61, bf16[128,1024]{1,0:T(8,128)(2,1)} %copy-done.23, ...), custom_call_target="tpu_custom_call" | custom-call | flops 536870912 | tf_op jit(solution)/shard_map/pallas_call | solution.py:237
  153.0 4.2 collective-permute-done.49.source_ref
  179.5 4.7 %collective-permute-done.45.far_ref = bf16[128,1024]{1,0:T(8,128)(2,1)S(1)} collective-permute-done((bf16[128,1024]{1,0:T(8,128)(2,1)S(1)}, bf16[128,1024]{1,0:T(8,128)(2,1)S(1)}, u32[]{:S(2)}, u32[]{:S(2)}) %collective-permute-start.45) | collective-permute-done | bytes 262176 | tf_op jit(solution)/shard_map/ppermute | solution.py:43
  190.8 4.1 collective-permute-done.46.refs_1_
  197.8 5.7 %shard_map.438 = (bf16[512,1024]{1,0:T(8,128)(2,1)}, bf16[512,1024]{1,0:T(8,128)(2,1)}, bf16[512,1024]{1,0:T(8,128)(2,1)}, bf16[1024,1024]{1,0:T(8,128)(2,1)}, b...) custom-call(bf16[128,1024]{1,0:T(8,128)(2,1)S(1)} %get-tuple-element, ...), custom_call_target="tpu_custom_call" | custom-call | flops 2147483648 | tf_op jit(solution)/shard_map/pallas_call | solution.py:237
  207.7 6.2 %collective-permute-done.57.far_ref = bf16[128,1024]{1,0:T(8,128)(2,1)S(1)} collective-permute-done((bf16[128,1024]{1,0:T(8,128)(2,1)S(1)}, bf16[128,1024]{1,0:T(8,128)(2,1)S(1)}, u32[]{:S(2)}, u32[]{:S(2)}) %collective-permute-start.57) | collective-permute-done | bytes 262176 | tf_op jit(solution)/shard_map/ppermute | solution.py:43
  216.4 6.3 %collective-permute-done.58.refs_1_ = bf16[128,1024]{1,0:T(8,128)(2,1)S(1)} collective-permute-done((bf16[128,1024]{1,0:T(8,128)(2,1)S(1)}, bf16[128,1024]{1,0:T(8,128)(2,1)S(1)}, u32[]{:S(2)}, u32[]{:S(2)}) %collective-permute-start.58) | collective-permute-done | bytes 262176 | tf_op jit(solution)/shard_map/ppermute | solution.py:43
  224.2 6.9 %shard_map.441 = (bf16[512,1024]{1,0:T(8,128)(2,1)S(1)}, bf16[512,1024]{1,0:T(8,128)(2,1)}, bf16[256,1024]{1,0:T(8,128)(2,1)S(1)}, bf16[128,1024]{1,0:T(8,128)(2,1)S(1)}, f32[128,1024]{1,0:T(8,128)S(1)}) custom-call(bf16[128,1024]{1,0:T(8,128)(2,1)S(1)} %get-tuple-element.307.refs_0_, bf16[128,1024]{1,0:T(8,128)(2,1)S(1)} %collective-permute-done.58.refs_1_, ...), custom_call_target="tpu_custom_call" | custom-call | flops 2147483648 | tf_op jit(solution)/shard_map/pallas_call | solution.py:237
  234.4 7.1 %collective-permute-done.62.far_ref = bf16[128,1024]{1,0:T(8,128)(2,1)S(1)} collective-permute-done((bf16[128,1024]{1,0:T(8,128)(2,1)S(1)}, bf16[128,1024]{1,0:T(8,128)(2,1)S(1)}, u32[]{:S(2)}, u32[]{:S(2)}) %collective-permute-start.62) | collective-permute-done | bytes 262176 | tf_op jit(solution)/shard_map/ppermute | solution.py:43
  270.3 5.0 %shard_map.445 = (bf16[512,512]{1,0:T(8,128)(2,1)S(1)}, f32[8,256]{1,0:T(8,128)S(1)}, bf16[256,1024]{1,0:T(8,128)(2,1)S(1)}, bf16[128,1024]{1,0:T(8,128)(2,1)S(1)}, f32[128,1024]{1,0:T(8,128)S(1)}) custom-call(s32[1]{0:T(128)} %bitcast.refs_0_.place_ref, s32[1,4]{1,0:T(1,128)S(1)} %copy-done.34, f32[5,256]{1,0:T(8,128)S(1)} %bitcast.62, ...), custom_call_target="tpu_custom_call" | custom-call | flops 536870912 | tf_op jit(solution)/shard_map/pallas_call | solution.py:237
  281.4 6.6 %collective-permute-done.70.far_ref = bf16[128,1024]{1,0:T(8,128)(2,1)S(1)} collective-permute-done((bf16[128,1024]{1,0:T(8,128)(2,1)S(1)}, bf16[128,1024]{1,0:T(8,128)(2,1)S(1)}, u32[]{:S(2)}, u32[]{:S(2)}) %collective-permute-start.70) | collective-permute-done | bytes 262176 | tf_op jit(solution)/shard_map/ppermute | solution.py:43
  297.4 12.1 %shard_map.448 = (bf16[512,1024]{1,0:T(8,128)(2,1)}, bf16[512,768]{1,0:T(8,128)(2,1)}, bf16[1024,256]{1,0:T(8,128)(2,1)S(1)}, f32[4,128]{1,0:T(4,128)S(1)}, bf16...) custom-call(s32[1]{0:T(128)} %bitcast.refs_0_.place_ref, ...), custom_call_target="tpu_custom_call" | custom-call | flops 2147483648 | tf_op jit(solution)/shard_map/pallas_call | solution.py:237
  325.3 5.4 %collective-permute-done.78.refs_1_ = bf16[128,1024]{1,0:T(8,128)(2,1)S(1)} collective-permute-done((bf16[128,1024]{1,0:T(8,128)(2,1)S(1)}, bf16[128,1024]{1,0:T(8,128)(2,1)S(1)}, u32[]{:S(2)}, u32[]{:S(2)}) %collective-permute-start.78) | collective-permute-done | bytes 262176 | tf_op jit(solution)/shard_map/ppermute | solution.py:43
  332.9 7.6 %shard_map.451 = (bf16[512,1024]{1,0:T(8,128)(2,1)S(1)}, bf16[512,1024]{1,0:T(8,128)(2,1)}, bf16[256,1024]{1,0:T(8,128)(2,1)S(1)}, bf16[128,1024]{1,0:T(8,128)(2...) custom-call(bf16[128,1024]{1,0:T(8,128)(2,1)S(1)} %get-tuple-element.341.refs_0_, ...), custom_call_target="tpu_custom_call" | custom-call | flops 2147483648 | tf_op jit(solution)/shard_map/pallas_call | solution.py:237
  367.1 9.4 %collective-permute-done.87 = bf16[512,1024]{1,0:T(8,128)(2,1)S(1)} collective-permute-done((bf16[512,1024]{1,0:T(8,128)(2,1)S(1)}, bf16[512,1024]{1,0:T(8,128)(2,1)S(1)}, u32[]{:S(2)}, u32[]{:S(2)}) %collective-permute-start.87) | collective-permute-done | bytes 1048608 | tf_op jit(solution)/shard_map/ppermute | solution.py:43
  392.3 8.8 %collective-permute-done.101.refs_1_ = bf16[128,1280]{1,0:T(8,128)(2,1)S(1)} collective-permute-done((bf16[128,1280]{1,0:T(8,128)(2,1)}, bf16[128,1280]{1,0:T(8,128)(2,1)S(1)}, u32[]{:S(2)}, u32[]{:S(2)}) %collective-permute-start.101) | collective-permute-done | bytes 327712 | tf_op jit(solution)/shard_map/ppermute | solution.py:43
  420.0 7.6 %collective-permute-done.100 = bf16[256,1024]{1,0:T(8,128)(2,1)S(1)} collective-permute-done((bf16[256,1024]{1,0:T(8,128)(2,1)S(1)}, bf16[256,1024]{1,0:T(8,128)(2,1)S(1)}, u32[]{:S(2)}, u32[]{:S(2)}) %collective-permute-start.100) | collective-permute-done | bytes 524320 | tf_op jit(solution)/shard_map/ppermute | solution.py:43
  (623 shorter events, 283.6 us)
Async XLA Ops:
  12.5 22.3 %collective-permute-start = (bf16[1,928]{1,0:T(2,128)(2,1)S(1)}, bf16[1,928]{1,0:T(2,128)(2,1)S(1)}, u32[]{:S(2)}, u32[]{:S(2)}) collective-permute-start(bf16[1,928]{1,0:T(2,128)(2,1)S(1)} %broadcast_in_dim.2), channel_id=1, source_target_pairs={{0,16},{4,20},{8,24},{12,28},{16,0},{20,4},{24,8},{28,12},{1,17},{... | collective-permute-start | bytes 5576 | tf_op jit(solution)/shard_map/ppermute | solution.py:43
  27.3 18.1 %collective-permute-start.8 = (bf16[128,1024]{1,0:T(8,128)(2,1)S(1)}, bf16[128,1024]{1,0:T(8,128)(2,1)S(1)}, u32[]{:S(2)}, u32[]{:S(2)}) collective-permute-start(bf16[128,1024]{1,0:T(8,128)(2,1)S(1)} %convert_element_type.132.refs_9_), channel_id=1, source_target_pairs={{0,16},{4,20},{8,24},{12,28},{16,0},{20,4},{24,8},{28,12},{1,17},{... | collective-permute-start | bytes 786440 | tf_op jit(solution)/shard_map/ppermute | solution.py:43
  52.7 22.8 %collective-permute-start.22 = (bf16[128,1280]{1,0:T(8,128)(2,1)}, bf16[128,1280]{1,0:T(8,128)(2,1)}, u32[]{:S(2)}, u32[]{:S(2)}) collective-permute-start(bf16[128,1280]{1,0:T(8,128)(2,1)} %convert_dynamic-update-slice_fusion.refs_8_), channel_id=1, source_target_pairs={{0,16},{4,20},{8,24},{12,28},{16,0},{20,4},{24,8},{28,12},{1,17},{... | collective-permute-start | bytes 983048 | tf_op jit(solution)/shard_map/ppermute | solution.py:43
  88.1 32.6 %collective-permute-start.34 = (bf16[128,768]{1,0:T(8,128)(2,1)}, bf16[128,768]{1,0:T(8,128)(2,1)}, u32[]{:S(2)}, u32[]{:S(2)}) collective-permute-start(bf16[128,768]{1,0:T(8,128)(2,1)} %pad_maximum_fusion.3.refs_7_), channel_id=1, source_target_pairs={{0,16},{4,20},{8,24},{12,28},{16,0},{20,4},{24,8},{28,12},{1,17},{... | collective-permute-start | bytes 589832 | tf_op jit(solution)/shard_map/ppermute | solution.py:43
  100.2 24.3 %collective-permute-start.35 = (bf16[128,768]{1,0:T(8,128)(2,1)}, bf16[128,768]{1,0:T(8,128)(2,1)}, u32[]{:S(2)}, u32[]{:S(2)}) collective-permute-start(bf16[128,768]{1,0:T(8,128)(2,1)} %pad_maximum_fusion.3.refs_7_), channel_id=1, source_target_pairs={{0,8},{4,12},{8,0},{12,4},{16,24},{20,28},{24,16},{28,20},{1,9},{5... | collective-permute-start | bytes 589832 | tf_op jit(solution)/shard_map/ppermute | solution.py:43
  131.7 25.5 %collective-permute-start.49 = (bf16[128,2048]{1,0:T(8,128)(2,1)S(1)}, bf16[128,2048]{1,0:T(8,128)(2,1)}, u32[]{:S(2)}, u32[]{:S(2)}) collective-permute-start(bf16[128,2048]{1,0:T(8,128)(2,1)S(1)} %pad_maximum_fusion.2.refs_4_.refs_12_), channel_id=1, source_target_pairs={{0,16},{4,20},{8,24},{12,28},{16,0},{20,4},{24,8},{28,12},{1,17},{... | collective-permute-start | bytes 1572872 | tf_op jit(solution)/shard_map/ppermute | solution.py:43
  135.9 23.4 %collective-permute-start.52 = (bf16[128,2048]{1,0:T(8,128)(2,1)S(1)}, bf16[128,2048]{1,0:T(8,128)(2,1)}, u32[]{:S(2)}, u32[]{:S(2)}) collective-permute-start(bf16[128,2048]{1,0:T(8,128)(2,1)S(1)} %pad_maximum_fusion.2.refs_4_.refs_12_), channel_id=1, source_target_pairs={{0,4},{4,0},{8,12},{12,8},{16,20},{20,16},{24,28},{28,24},{1,5},{5... | collective-permute-start | bytes 1572872 | tf_op jit(solution)/shard_map/ppermute | solution.py:43
  140.2 24.2 %collective-permute-start.50 = (bf16[128,2048]{1,0:T(8,128)(2,1)S(1)}, bf16[128,2048]{1,0:T(8,128)(2,1)}, u32[]{:S(2)}, u32[]{:S(2)}) collective-permute-start(bf16[128,2048]{1,0:T(8,128)(2,1)S(1)} %pad_maximum_fusion.2.refs_4_.refs_12_), channel_id=1, source_target_pairs={{0,8},{4,12},{8,0},{12,4},{16,24},{20,28},{24,16},{28,20},{1,9},{5... | collective-permute-start | bytes 1572872 | tf_op jit(solution)/shard_map/ppermute | solution.py:43
  166.8 24.0 %collective-permute-start.54 = (bf16[128,2048]{1,0:T(8,128)(2,1)}, bf16[128,2048]{1,0:T(8,128)(2,1)}, u32[]{:S(2)}, u32[]{:S(2)}) collective-permute-start(bf16[128,2048]{1,0:T(8,128)(2,1)} %shard_map.432.refs_6_.refs_14_), channel_id=1, source_target_pairs={{0,4},{4,0},{8,12},{12,8},{16,20},{20,16},{24,28},{28,24},{1,5},{5... | collective-permute-start | bytes 1572872 | tf_op jit(solution)/shard_map/ppermute | solution.py:43
  173.7 24.1 %collective-permute-start.55 = (bf16[128,2048]{1,0:T(8,128)(2,1)}, bf16[128,2048]{1,0:T(8,128)(2,1)}, u32[]{:S(2)}, u32[]{:S(2)}) collective-permute-start(bf16[128,2048]{1,0:T(8,128)(2,1)} %shard_map.433.refs_7_.refs_15_), channel_id=1, source_target_pairs={{0,4},{4,0},{8,12},{12,8},{16,20},{20,16},{24,28},{28,24},{1,5},{5... | collective-permute-start | bytes 1572872 | tf_op jit(solution)/shard_map/ppermute | solution.py:43
  245.8 31.2 %collective-permute-start.71 = (bf16[512,1024]{1,0:T(8,128)(2,1)}, bf16[512,1024]{1,0:T(8,128)(2,1)}, u32[]{:S(2)}, u32[]{:S(2)}) collective-permute-start(bf16[512,1024]{1,0:T(8,128)(2,1)} %convolution_convert_fusion.3), channel_id=1, source_target_pairs={{0,4},{4,0},{8,12},{12,8},{16,20},{20,16},{24,28},{28,24},{1,5},{5... | collective-permute-start | bytes 3145736 | tf_op jit(solution)/shard_map/ppermute | solution.py:43
  275.3 40.0 %collective-permute-start.94 = (bf16[512,1024]{1,0:T(8,128)(2,1)}, bf16[512,1024]{1,0:T(8,128)(2,1)}, u32[]{:S(2)}, u32[]{:S(2)}) collective-permute-start(bf16[512,1024]{1,0:T(8,128)(2,1)} %convolution_convert_fusion), channel_id=1, source_target_pairs={{0,4},{4,0},{8,12},{12,8},{16,20},{20,16},{24,28},{28,24},{1,5},{5... | collective-permute-start | bytes 3145736 | tf_op jit(solution)/shard_map/ppermute | solution.py:43
  290.9 34.4 %collective-permute-start.91 = (bf16[512,768]{1,0:T(8,128)(2,1)}, bf16[512,768]{1,0:T(8,128)(2,1)}, u32[]{:S(2)}, u32[]{:S(2)}) collective-permute-start(bf16[512,768]{1,0:T(8,128)(2,1)} %pad_maximum_fusion.1), channel_id=1, source_target_pairs={{0,4},{4,0},{8,12},{12,8},{16,20},{20,16},{24,28},{28,24},{1,5},{5... | collective-permute-start | bytes 2359304 | tf_op jit(solution)/shard_map/ppermute | solution.py:43
  310.5 68.7 %collective-permute-start.97 = (bf16[128,1024]{1,0:T(8,128)(2,1)}, bf16[128,1024]{1,0:T(8,128)(2,1)S(1)}, u32[]{:S(2)}, u32[]{:S(2)}) collective-permute-start(bf16[128,1024]{1,0:T(8,128)(2,1)} %slice.461), channel_id=1, source_target_pairs={{0,16},{4,20},{8,24},{12,28},{16,0},{20,4},{24,8},{28,12},{1,17},{... | collective-permute-start | bytes 786440 | tf_op jit(solution)/shard_map/ppermute | solution.py:43
  318.2 23.3 %collective-permute-start.95 = (bf16[256,1024]{1,0:T(8,128)(2,1)}, bf16[256,1024]{1,0:T(8,128)(2,1)S(1)}, u32[]{:S(2)}, u32[]{:S(2)}) collective-permute-start(bf16[256,1024]{1,0:T(8,128)(2,1)} %slice.453), channel_id=1, source_target_pairs={{0,8},{4,12},{8,0},{12,4},{16,24},{20,28},{24,16},{28,20},{1,9},{5... | collective-permute-start | bytes 1572872 | tf_op jit(solution)/shard_map/ppermute | solution.py:43
  324.3 31.9 %collective-permute-start.88 = (bf16[512,1280]{1,0:T(8,128)(2,1)S(1)}, bf16[512,1280]{1,0:T(8,128)(2,1)}, u32[]{:S(2)}, u32[]{:S(2)}) collective-permute-start(bf16[512,1280]{1,0:T(8,128)(2,1)S(1)} %pad_maximum_fusion), channel_id=1, source_target_pairs={{0,4},{4,0},{8,12},{12,8},{16,20},{20,16},{24,28},{28,24},{1,5},{5... | collective-permute-start | bytes 3932168 | tf_op jit(solution)/shard_map/ppermute | solution.py:43
  341.5 35.0 %collective-permute-start.87 = (bf16[512,1024]{1,0:T(8,128)(2,1)S(1)}, bf16[512,1024]{1,0:T(8,128)(2,1)S(1)}, u32[]{:S(2)}, u32[]{:S(2)}) collective-permute-start(bf16[512,1024]{1,0:T(8,128)(2,1)S(1)} %convolution_convert_fusion.1), channel_id=1, source_target_pairs={{0,4},{4,0},{8,12},{12,8},{16,20},{20,16},{24,28},{28,24},{1,5},{5... | collective-permute-start | bytes 3145736 | tf_op jit(solution)/shard_map/ppermute | solution.py:43
  346.7 34.5 %collective-permute-start.96 = (bf16[128,1024]{1,0:T(8,128)(2,1)S(1)}, bf16[128,1024]{1,0:T(8,128)(2,1)S(1)}, u32[]{:S(2)}, u32[]{:S(2)}) collective-permute-start(bf16[128,1024]{1,0:T(8,128)(2,1)S(1)} %slice.460), channel_id=1, source_target_pairs={{0,16},{4,20},{8,24},{12,28},{16,0},{20,4},{24,8},{28,12},{1,17},{... | collective-permute-start | bytes 786440 | tf_op jit(solution)/shard_map/ppermute | solution.py:43
  352.1 28.3 %collective-permute-start.93 = (bf16[128,768]{1,0:T(8,128)(2,1)S(1)}, bf16[128,768]{1,0:T(8,128)(2,1)S(1)}, u32[]{:S(2)}, u32[]{:S(2)}) collective-permute-start(bf16[128,768]{1,0:T(8,128)(2,1)S(1)} %slice.463), channel_id=1, source_target_pairs={{0,16},{4,20},{8,24},{12,28},{16,0},{20,4},{24,8},{28,12},{1,17},{... | collective-permute-start | bytes 589832 | tf_op jit(solution)/shard_map/ppermute | solution.py:43
  362.5 19.8 %collective-permute-start.90 = (bf16[256,1280]{1,0:T(8,128)(2,1)S(1)}, bf16[256,1280]{1,0:T(8,128)(2,1)S(1)}, u32[]{:S(2)}, u32[]{:S(2)}) collective-permute-start(bf16[256,1280]{1,0:T(8,128)(2,1)S(1)} %slice.451), channel_id=1, source_target_pairs={{0,8},{4,12},{8,0},{12,4},{16,24},{20,28},{24,16},{28,20},{1,9},{5... | collective-permute-start | bytes 1966088 | tf_op jit(solution)/shard_map/ppermute | solution.py:43
  376.5 31.9 %collective-permute-start.86 = (bf16[512,1024]{1,0:T(8,128)(2,1)}, bf16[512,1024]{1,0:T(8,128)(2,1)}, u32[]{:S(2)}, u32[]{:S(2)}) collective-permute-start(bf16[512,1024]{1,0:T(8,128)(2,1)} %convolution_convert_fusion.2), channel_id=1, source_target_pairs={{0,4},{4,0},{8,12},{12,8},{16,20},{20,16},{24,28},{28,24},{1,5},{5... | collective-permute-start | bytes 3145736 | tf_op jit(solution)/shard_map/ppermute | solution.py:43
  381.2 24.4 %collective-permute-start.89 = (bf16[256,1024]{1,0:T(8,128)(2,1)}, bf16[256,1024]{1,0:T(8,128)(2,1)}, u32[]{:S(2)}, u32[]{:S(2)}) collective-permute-start(bf16[256,1024]{1,0:T(8,128)(2,1)} %slice.454), channel_id=1, source_target_pairs={{0,8},{4,12},{8,0},{12,4},{16,24},{20,28},{24,16},{28,20},{1,9},{5... | collective-permute-start | bytes 1572872 | tf_op jit(solution)/shard_map/ppermute | solution.py:43
  383.3 17.8 %collective-permute-start.101 = (bf16[128,1280]{1,0:T(8,128)(2,1)}, bf16[128,1280]{1,0:T(8,128)(2,1)S(1)}, u32[]{:S(2)}, u32[]{:S(2)}) collective-permute-start(bf16[128,1280]{1,0:T(8,128)(2,1)} %slice.457), channel_id=1, source_target_pairs={{0,16},{4,20},{8,24},{12,28},{16,0},{20,4},{24,8},{28,12},{1,17},{... | collective-permute-start | bytes 983048 | tf_op jit(solution)/shard_map/ppermute | solution.py:43
  388.2 20.2 %collective-permute-start.99 = (bf16[128,1024]{1,0:T(8,128)(2,1)}, bf16[128,1024]{1,0:T(8,128)(2,1)}, u32[]{:S(2)}, u32[]{:S(2)}) collective-permute-start(bf16[128,1024]{1,0:T(8,128)(2,1)} %collective-permute-done.98.refs_1_), channel_id=1, source_target_pairs={{0,1},{1,0},{2,3},{3,2},{4,5},{5,4},{6,7},{7,6},{8,9},{9,8},{10,11... | collective-permute-start | bytes 786440 | tf_op jit(solution)/shard_map/ppermute | solution.py:43
  (203 other events, 1772.5 us)
